TPU v7x, 32 devices: a whole 2x2x4 slice. The times are simulated.
32 devices in a mesh: energy: 16 (over z, y, x), cell: 2 (over core).
Axes of the slice: x: 2, y: 2, z: 4, core: 2. Of those that a mesh axis runs over, the one named last changes fastest.
Arguments:
- green_pair: float32 [4, 16, 4, 256, 256], P(None, 'energy', 'cell'), may hold values from -4 to 4
- retarded_diag: float32 [2, 16, 4, 256, 256], P(None, 'energy', 'cell'), may hold values from -0.25 to 0.25
- retarded_upper: float32 [2, 16, 4, 256, 256], P(None, 'energy', 'cell'), may hold values from -0.25 to 0.25
- coulomb_diag: float32 [4, 256, 256], P('cell'), may hold values from -0.375 to 0.375
- coulomb_upper: float32 [4, 256, 256], P('cell'), may hold values from -0.375 to 0.375
Outputs:
- lesser_new: float32 [2, 16, 4, 256, 256], P(None, 'energy', 'cell')
All inputs are finite; a program needn't handle non-finite values.
Results may differ from a plain program's by a relative error of at most 0.00014.
Values sent between devices are 32-bit elements; how exact they have to be, the bound alone decides.
No kernel may reach another device: no remote copies, remote signals or barrier semaphores. Data moves between devices by JAX's collectives and lax.ppermute only.
A program may use at most 64 MiB of HBM per device.

v0:
```python
import functools
import math

import jax
import jax.numpy as jnp
from jax import lax
from jax.experimental import pallas as pl
from jax.experimental.pallas import tpu as pltpu
from jax.sharding import PartitionSpec as P

VMEM = pl.BlockSpec(memory_space=pltpu.VMEM)
f32 = jnp.float32
bf16 = jnp.bfloat16


def times_root(value, turn, points, sign):
    re, im = value
    turn = turn % points
    if turn == 0:
        return value
    if 4 * turn == points:
        return (-im, re) if sign > 0 else (im, -re)
    if 2 * turn == points:
        return (-re, -im)
    if 4 * turn == 3 * points:
        return (im, -re) if sign > 0 else (-im, re)
    angle = 2.0 * math.pi * turn / points
    c, s = math.cos(angle), sign * math.sin(angle)
    if 8 * turn % points == 0:
        unit = abs(c)
        a = re if c > 0 else -re
        b = im if c > 0 else -im
        if (s > 0) == (c > 0):
            return ((a - b) * unit, (a + b) * unit)
        return ((a + b) * unit, (b - a) * unit)
    return (re * c - im * s, re * s + im * c)


def fourier(values, sign):
    points = len(values)
    if points == 1:
        return values
    if points % 2:
        out = []
        for k in range(points):
            total = values[0]
            for n in range(1, points):
                term = times_root(values[n], k * n, points, sign)
                total = (total[0] + term[0], total[1] + term[1])
            out.append(total)
        return out
    even = fourier(values[0::2], sign)
    odd = fourier(values[1::2], sign)
    low, high = [], []
    for k in range(points // 2):
        a = even[k]
        b = times_root(odd[k], k, points, sign)
        low.append((a[0] + b[0], a[1] + b[1]))
        high.append((a[0] - b[0], a[1] - b[1]))
    return low + high


def tiles_of(cells, rows, lanes):
    step_rows = 8 if rows % 8 == 0 else rows
    step_lanes = 128 if lanes % 128 == 0 else lanes
    return [
        (c, pl.ds(r, step_rows), pl.ds(b, step_lanes))
        for c in range(cells)
        for r in range(0, rows, step_rows)
        for b in range(0, lanes, step_lanes)
    ]


def polarize_kernel(scaling, entries, lesser_hat, polar_hat):
    points, _, cells, rows, lanes = entries.shape
    for c, r, b in tiles_of(cells, rows, lanes):
        hats = []
        for pair in (0, 2):
            hats.append(
                fourier([(entries[n, pair, c, r, b], entries[n, pair + 1, c, r, b]) for n in range(points)], -1)
            )
            if pair == 0:
                for k in range(points):
                    lesser_hat[k, 0, c, r, b] = hats[0][k][0]
                    lesser_hat[k, 1, c, r, b] = hats[0][k][1]
        for k in range(points):
            greater_re, greater_im = hats[1][k]
            lesser_re = lesser_hat[k, 0, c, r, b]
            lesser_im = lesser_hat[k, 1, c, r, b]
            polar_hat[k, 0, c, r, b] = (lesser_re * greater_im - lesser_im * greater_re) * scaling
            polar_hat[k, 1, c, r, b] = (lesser_re * greater_re + lesser_im * greater_im) * scaling


def convolve_kernel(factor, lesser_hat, screened_hat, sigma):
    points, _, cells, rows, lanes = screened_hat.shape
    for c, r, b in tiles_of(cells, rows, lanes):
        spectral = []
        for k in range(points):
            lesser_re, lesser_im = lesser_hat[k, 0, c, r, b], lesser_hat[k, 1, c, r, b]
            w_re, w_im = screened_hat[k, 0, c, r, b], screened_hat[k, 1, c, r, b]
            spectral.append(
                ((lesser_re * w_re - lesser_im * w_im) * factor, (lesser_re * w_im + lesser_im * w_re) * factor)
            )
        for n, (re, im) in enumerate(fourier(spectral, 1)):
            sigma[n, 0, c, r, b] = -im
            sigma[n, 1, c, r, b] = re


def parts(matrix):
    high = matrix.astype(bf16)
    return (high, (matrix - high.astype(f32)).astype(bf16))


def join(pieces, axis):
    return tuple(jnp.concatenate(p, axis) for p in zip(*pieces, strict=True))


def negative(pair):
    return tuple(-p for p in pair)


def product(left, right, turned=False):
    dims = (((1,), (1 if turned else 0,)), ((), ()))
    dot = functools.partial(lax.dot_general, dimension_numbers=dims, preferred_element_type=f32)
    return dot(left[0], right[0]) + (dot(left[0], right[1]) + dot(left[1], right[0]))


def block_of(ref, plane, cell):
    slabs, _, _, rows, lanes = ref.shape
    return ref[:, plane, cell].reshape(slabs * rows, lanes)


def neighbours(cells, here, before, after):
    previous = [(before, 0)] + [(here, c) for c in range(cells - 1)]
    following = [(here, c) for c in range(1, cells)] + [(after, 0)]
    return previous, following


def screen_kernel(here, before, after, diag, upper, lower, out):
    slabs, planes, cells, rows, lanes = here.shape
    previous, following = neighbours(cells, here, before, after)
    for c in range(cells):
        symmetric = (diag[c] + diag[c].T) * 0.5
        lefts, inners = [], []
        for matrix, (ref, cell) in (
            (symmetric, (here, c)),
            (upper[c], following[c]),
            (lower[c].T, previous[c]),
        ):
            left = parts(matrix)
            lefts.append(left)
            stacked = jnp.concatenate([block_of(ref, p, cell) for p in range(planes)], 0)
            inners.append(parts(product(parts(stacked), left, True)))
        left = join(lefts, 1)
        for p in range(planes):
            inner = join([tuple(q[p * lanes : (p + 1) * lanes] for q in i) for i in inners], 0)
            out[:, p, c] = product(left, inner).reshape(slabs, rows, lanes)


def output_kernel(here, before, after, diag, upper, lower, out):
    _, planes, cells, _, lanes = here.shape
    previous, following = neighbours(cells, here, before, after)
    for c in range(cells):
        total = None
        for matrix, turned, (ref, cell) in (
            (diag, False, (here, c)),
            (upper, False, following[c]),
            (lower, True, previous[c]),
        ):
            re, im = matrix[0, 0, c], matrix[1, 0, c]
            if turned:
                re, im = re.T, im.T
            re, im = parts(re), parts(im)
            middle = parts(jnp.concatenate([block_of(ref, p, cell) for p in range(planes)], 0))
            left = join([join([re, negative(im)], 1), join([im, re], 1)], 0)
            inner = parts(product(left, middle))
            inner_re = tuple(q[:lanes] for q in inner)
            inner_im = tuple(q[lanes:] for q in inner)
            rows = join([join([inner_re, inner_im], 1), join([inner_im, negative(inner_re)], 1)], 0)
            term = product(rows, join([re, im], 1), True)
            total = term if total is None else total + term
        out[0, 0, c] = total[:lanes]
        out[1, 0, c] = total[lanes:]


def call(kernel, outs, *args):
    return pl.pallas_call(
        kernel,
        out_shape=outs,
        in_specs=[VMEM] * len(args),
        out_specs=jax.tree.map(lambda _: VMEM, outs),
        compiler_params=pltpu.CompilerParams(vmem_limit_bytes=48 * 1024 * 1024),
    )(*args)


def shape(dims):
    return jax.ShapeDtypeStruct(tuple(dims), f32)


def exchange(values):
    return lax.all_to_all(values, "energy", split_axis=0, concat_axis=0, tiled=True)


def shifted(block, axis, step):
    count = lax.axis_size(axis)
    route = [(i, i + step) for i in range(count) if 0 <= i + step < count]
    return lax.ppermute(block, axis, route)


def halo(values):
    return (shifted(values[:, :, -1:], "cell", 1), shifted(values[:, :, :1], "cell", -1))


def per_device(green_pair, retarded_diag, retarded_upper, coulomb_diag, coulomb_upper):
    devices = lax.axis_size("energy")
    _, held, cells, orbitals, _ = green_pair.shape
    points = devices * held
    scaling = 1.0 / math.sqrt(points)
    rows = orbitals // devices
    coulomb_edge = shifted(coulomb_upper[-1:], "cell", 1)
    retarded_edge = shifted(retarded_upper[:, :, -1:], "cell", 1)
    coulomb_before = jnp.concatenate([coulomb_edge, coulomb_upper[:-1]], 0)
    retarded_before = jnp.concatenate([retarded_edge, retarded_upper[:, :, :-1]], 2)
    slabs = green_pair.reshape(4, cells, devices, rows, orbitals).transpose(2, 0, 1, 3, 4)
    entries = exchange(slabs)
    half = shape((points, 2, cells, rows, orbitals))
    lesser_hat, polar_hat = call(functools.partial(polarize_kernel, scaling), (half, half), entries)
    polar = exchange(polar_hat)
    screened = call(screen_kernel, half, polar, *halo(polar), coulomb_diag, coulomb_upper, coulomb_before)
    screened_hat = exchange(screened)
    sigma_entries = call(functools.partial(convolve_kernel, scaling / points), half, lesser_hat, screened_hat)
    sigma = exchange(sigma_entries)
    return call(
        output_kernel,
        shape(retarded_diag.shape),
        sigma,
        *halo(sigma),
        retarded_diag,
        retarded_upper,
        retarded_before,
    )


def solution(mesh):
    over_both = P(None, "energy", "cell", None, None)
    over_cell = P("cell", None, None)
    return jax.shard_map(
        per_device,
        mesh=mesh,
        in_specs=(over_both, over_both, over_both, over_cell, over_cell),
        out_specs=over_both,
        check_vma=False,
    )
```

profile of v0, /device:TPU:1, one launch (start us, length us, event | category | flops | bytes accessed | tf_op | source)
XLA Modules:
  0.0 170.7 jit_solution(7668507699202138017)
XLA Ops:
  0.0 1.8 %copy.8 = f32[4,2,16,16,256]{4,3,1,0,2:T(8,128)S(1)} copy(f32[4,2,16,16,256]{4,3,2,1,0:T(8,128)} %bitcast.5) | data formatting | bytes 4194304 | tf_op jit(solution)/shard_map/reshape | solution.py:224
  1.8 54.2 %all_to_all.20.entries = f32[16,4,2,16,256]{4,3,2,1,0:T(8,128)S(1)} all-to-all(f32[16,4,2,16,256]{4,3,2,1,0:T(8,128)S(1)} %bitcast.4), channel_id=1, replica_groups=mesh['energy'=16,'cell'=2] {'energy'}, dimensions={0} | all-to-all | bytes 4194304 | tf_op jit(solution)/shard_map/all_to_all | solution.py:201
  56.0 0.7 shard_map.55
  56.6 0.0 copy-start.1
  56.7 29.3 %all_to_all.21.here = f32[16,2,2,16,256]{4,3,2,1,0:T(8,128)S(1)} all-to-all(f32[16,2,2,16,256]{4,3,2,1,0:T(8,128)S(1)} %get-tuple-element.8), channel_id=1, replica_groups=mesh['energy'=16,'cell'=2] {'energy'}, dimensions={0} | all-to-all | bytes 2097152 | tf_op jit(solution)/shard_map/all_to_all | solution.py:201
  86.0 0.0 copy-start.3
  86.0 0.1 fusion.2
  86.1 1.4 collective-permute-start
  87.5 4.9 %collective-permute-start.1 = (f32[16,2,1,16,256]{4,3,2,1,0:T(8,128)S(1)}, f32[16,2,1,16,256]{4,3,2,1,0:T(8,128)S(1)}, u32[]{:S(2)}, u32[]{:S(2)}) collective-permute-start(f32[16,2,1,16,256]{4,3,2,1,0:T(8,128)S(1)} %get-tuple-element.13), channel_id=1, source_target_pairs={{1,0},{3,2},{5,4},{7,6},{9,8},{11,10},{13,12},{15,14},{17,16},{19,... | collective-permute-start | bytes 1572872 | tf_op jit(solution)/shard_map/ppermute | solution.py:207
  92.4 0.0 copy-done.1
  92.5 1.3 collective-permute-start.2
  93.8 2.1 %collective-permute-done.2 = f32[1,256,256]{2,1,0:T(8,128)S(1)} collective-permute-done((f32[1,256,256]{2,1,0:T(8,128)S(1)}, f32[1,256,256]{2,1,0:T(8,128)S(1)}, u32[]{:S(2)}, u32[]{:S(2)}) %collective-permute-start.2) | collective-permute-done | bytes 262176 | tf_op jit(solution)/shard_map/ppermute | solution.py:207
  96.0 0.0 collective-permute-done.before
  96.0 0.0 collective-permute-done.1.after
  96.0 0.0 copy-done.3
  96.0 3.0 %shard_map.56 = f32[16,2,2,16,256]{4,3,2,1,0:T(8,128)S(1)} custom-call(f32[16,2,2,16,256]{4,3,2,1,0:T(8,128)S(1)} %all_to_all.21.here, f32[16,2,1,16,256]{4,3,2,1,0:T(8,128)S(1)} %collective-permute-done.before, f32[16,2,1,16,256]{4,3,2,1,0:T(8,128)S(1)} %collective-permute-done.1.after, f32[2,256,256]{2,1,0:T(8,128)S(1)} %copy-done.3, ...), custom_call_target="tpu_custom_call" | custom-call | tf_op jit(solution)/shard_map/pallas_call | solution.py:187
  99.0 28.1 %all_to_all.22.screened_hat = f32[16,2,2,16,256]{4,3,2,1,0:T(8,128)S(1)} all-to-all(f32[16,2,2,16,256]{4,3,2,1,0:T(8,128)S(1)} %shard_map.56), channel_id=1, replica_groups=mesh['energy'=16,'cell'=2] {'energy'}, dimensions={0} | all-to-all | bytes 2097152 | tf_op jit(solution)/shard_map/all_to_all | solution.py:201
  127.1 0.0 copy-start
  127.1 1.5 shard_map.57
  128.7 4.8 %all-to-all-start.3 = ((f32[16,2,2,16,256]{4,3,2,1,0:T(8,128)}), f32[16,2,2,16,256]{4,3,2,1,0:T(8,128)S(1)}, u32[]{:S(2)}, u32[]{:S(2)}) async-start(f32[16,2,2,16,256]{4,3,2,1,0:T(8,128)} %shard_map.57), calls=%async_computation.3 | async-start | bytes 2097152 | tf_op jit(solution)/shard_map/all_to_all | solution.py:201
  133.5 0.0 copy-done
  133.5 1.1 fusion
  134.6 0.0 copy-start.2
  134.6 1.4 collective-permute-start.5
  136.0 19.7 %all-to-all-done.3.here = f32[16,2,2,16,256]{4,3,2,1,0:T(8,128)S(1)} async-done(((f32[16,2,2,16,256]{4,3,2,1,0:T(8,128)}), f32[16,2,2,16,256]{4,3,2,1,0:T(8,128)S(1)}, u32[]{:S(2)}, u32[]{:S(2)}) %all-to-all-start.3) | async-done | bytes 1048608 | tf_op jit(solution)/shard_map/all_to_all | solution.py:201
  155.7 0.0 copy-start.4
  155.7 0.1 fusion.1
  155.8 1.4 collective-permute-start.3
  157.2 5.2 %collective-permute-start.4 = (f32[16,2,1,16,256]{4,3,2,1,0:T(8,128)S(1)}, f32[16,2,1,16,256]{4,3,2,1,0:T(8,128)S(1)}, u32[]{:S(2)}, u32[]{:S(2)}) collective-permute-start(f32[16,2,1,16,256]{4,3,2,1,0:T(8,128)S(1)} %get-tuple-element.11), channel_id=1, source_target_pairs={{1,0},{3,2},{5,4},{7,6},{9,8},{11,10},{13,12},{15,14},{17,16},{19,... | collective-permute-start | bytes 1572872 | tf_op jit(solution)/shard_map/ppermute | solution.py:207
  162.4 0.0 collective-permute-done.5
  162.4 0.0 copy-done.4
  162.4 1.1 pad_maximum_fusion.lower
  163.6 0.0 collective-permute-done.3.before
  163.6 0.3 collective-permute-done.4.after
  163.9 0.0 copy-done.2
  163.9 6.8 %shard_map.58 = f32[2,1,2,256,256]{4,3,2,1,0:T(8,128)} custom-call(f32[16,2,2,16,256]{4,3,2,1,0:T(8,128)S(1)} %all-to-all-done.3.here, f32[16,2,1,16,256]{4,3,2,1,0:T(8,128)S(1)} %collective-permute-done.3.before, f32[16,2,1,16,256]{4,3,2,1,0:T(8,128)S(1)} %collective-permute-done.4.after, f32[2,1,2,256,256]{4,3,2,1,0:T(8,128)S(1)} %copy-done.2, ...), custom_call_target="tpu_custom_call" | custom-call | tf_op jit(solution)/shard_map/pallas_call | solution.py:187
  (2 shorter events, 0.1 us)
Async XLA Ops:
  56.6 35.8 %copy-start.1 = (f32[2,256,256]{2,1,0:T(8,128)S(1)}, f32[2,256,256]{2,1,0:T(8,128)}, u32[]{:S(2)}) copy-start(f32[2,256,256]{2,1,0:T(8,128)} %upper.2) | copy-start | bytes 1572868
  86.0 10.0 %copy-start.3 = (f32[2,256,256]{2,1,0:T(8,128)S(1)}, f32[2,256,256]{2,1,0:T(8,128)}, u32[]{:S(2)}) copy-start(f32[2,256,256]{2,1,0:T(8,128)} %diag.2) | copy-start | bytes 1572868
  86.1 9.9 %collective-permute-start = (f32[16,2,1,16,256]{4,3,2,1,0:T(8,128)S(1)}, f32[16,2,1,16,256]{4,3,2,1,0:T(8,128)S(1)}, u32[]{:S(2)}, u32[]{:S(2)}) collective-permute-start(f32[16,2,1,16,256]{4,3,2,1,0:T(8,128)S(1)} %get-tuple-element.14), channel_id=1, source_target_pairs={{0,1},{2,3},{4,5},{6,7},{8,9},{10,11},{12,13},{14,15},{16,17},{18,... | collective-permute-start | bytes 1572872 | tf_op jit(solution)/shard_map/ppermute | solution.py:207
  87.5 8.4 %collective-permute-start.1 = (f32[16,2,1,16,256]{4,3,2,1,0:T(8,128)S(1)}, f32[16,2,1,16,256]{4,3,2,1,0:T(8,128)S(1)}, u32[]{:S(2)}, u32[]{:S(2)}) collective-permute-start(f32[16,2,1,16,256]{4,3,2,1,0:T(8,128)S(1)} %get-tuple-element.13), channel_id=1, source_target_pairs={{1,0},{3,2},{5,4},{7,6},{9,8},{11,10},{13,12},{15,14},{17,16},{19,... | collective-permute-start | bytes 1572872 | tf_op jit(solution)/shard_map/ppermute | solution.py:207
  92.5 3.4 %collective-permute-start.2 = (f32[1,256,256]{2,1,0:T(8,128)S(1)}, f32[1,256,256]{2,1,0:T(8,128)S(1)}, u32[]{:S(2)}, u32[]{:S(2)}) collective-permute-start(f32[1,256,256]{2,1,0:T(8,128)S(1)} %get-tuple-element.15), channel_id=1, source_target_pairs={{0,1},{2,3},{4,5},{6,7},{8,9},{10,11},{12,13},{14,15},{16,17},{18,... | collective-permute-start | bytes 786440 | tf_op jit(solution)/shard_map/ppermute | solution.py:207
  127.1 6.4 %copy-start = (f32[2,1,2,256,256]{4,3,2,1,0:T(8,128)S(1)}, f32[2,1,2,256,256]{4,3,2,1,0:T(8,128)}, u32[]{:S(2)}) copy-start(f32[2,1,2,256,256]{4,3,2,1,0:T(8,128)} %upper.3) | copy-start | bytes 3145732
  128.7 27.0 %all-to-all-start.3 = ((f32[16,2,2,16,256]{4,3,2,1,0:T(8,128)}), f32[16,2,2,16,256]{4,3,2,1,0:T(8,128)S(1)}, u32[]{:S(2)}, u32[]{:S(2)}) async-start(f32[16,2,2,16,256]{4,3,2,1,0:T(8,128)} %shard_map.57), calls=%async_computation.3 | async-start | bytes 2097152 | tf_op jit(solution)/shard_map/all_to_all | solution.py:201
  134.6 29.3 %copy-start.2 = (f32[2,1,2,256,256]{4,3,2,1,0:T(8,128)S(1)}, f32[2,1,2,256,256]{4,3,2,1,0:T(8,128)}, u32[]{:S(2)}) copy-start(f32[2,1,2,256,256]{4,3,2,1,0:T(8,128)} %diag.3) | copy-start | bytes 3145732
  134.6 27.9 %collective-permute-start.5 = (f32[2,1,1,256,256]{4,3,2,1,0:T(8,128)}, f32[2,1,1,256,256]{4,3,2,1,0:T(8,128)}, u32[]{:S(2)}, u32[]{:S(2)}) collective-permute-start(f32[2,1,1,256,256]{4,3,2,1,0:T(8,128)} %get-tuple-element.9), channel_id=1, source_target_pairs={{0,1},{2,3},{4,5},{6,7},{8,9},{10,11},{12,13},{14,15},{16,17},{18,... | collective-permute-start | bytes 1572872 | tf_op jit(solution)/shard_map/ppermute | solution.py:207
  155.7 6.7 %copy-start.4 = (f32[2,1,1,256,256]{4,3,2,1,0:T(8,128)S(1)}, f32[2,1,1,256,256]{4,3,2,1,0:T(8,128)}, u32[]{:S(2)}) copy-start(f32[2,1,1,256,256]{4,3,2,1,0:T(8,128)} %get-tuple-element.10) | copy-start | bytes 1572868
  155.8 7.8 %collective-permute-start.3 = (f32[16,2,1,16,256]{4,3,2,1,0:T(8,128)S(1)}, f32[16,2,1,16,256]{4,3,2,1,0:T(8,128)S(1)}, u32[]{:S(2)}, u32[]{:S(2)}) collective-permute-start(f32[16,2,1,16,256]{4,3,2,1,0:T(8,128)S(1)} %get-tuple-element.12), channel_id=1, source_target_pairs={{0,1},{2,3},{4,5},{6,7},{8,9},{10,11},{12,13},{14,15},{16,17},{18,... | collective-permute-start | bytes 1572872 | tf_op jit(solution)/shard_map/ppermute | solution.py:207
  157.2 6.7 %collective-permute-start.4 = (f32[16,2,1,16,256]{4,3,2,1,0:T(8,128)S(1)}, f32[16,2,1,16,256]{4,3,2,1,0:T(8,128)S(1)}, u32[]{:S(2)}, u32[]{:S(2)}) collective-permute-start(f32[16,2,1,16,256]{4,3,2,1,0:T(8,128)S(1)} %get-tuple-element.11), channel_id=1, source_target_pairs={{1,0},{3,2},{5,4},{7,6},{9,8},{11,10},{13,12},{15,14},{17,16},{19,... | collective-permute-start | bytes 1572872 | tf_op jit(solution)/shard_map/ppermute | solution.py:207
where the time goes:
time: 172 us; the launch traced here: 171 us
  blocking collectives  112 us (65%)
  waiting for transfers between devices  22.2 us (13%)
  starting transfers between devices  20.5 us (12%)
  Pallas kernels  12 us (7%)
  local copies, waits for them, and re-layouts  3.06 us (2%)
    all_to_all x3, blocking collectives, exchange(): lax.all_to_all(values, 'energy', split_axis=0, concat_axis=0, tiled=True)  112 us
    all_to_all x1, waiting for transfers between devices, exchange(): lax.all_to_all(values, 'energy', split_axis=0, concat_axis=0, tiled=True)  19.7 us
    ppermute x6, starting transfers between devices, shifted(): return lax.ppermute(block, axis, route)  15.7 us
    pallas_call x4, Pallas kernels, call(): pl.pallas_call(kernel, out_shape=outs, in_specs=[VMEM] * len(args), out_s...  12 us
    all_to_all x1, starting transfers between devices, exchange(): lax.all_to_all(values, 'energy', split_axis=0, concat_axis=0, tiled=True)  4.82 us
  transfers between devices with their start and end apart: 7, of which 3 were waited for; matrix products, arithmetic and copies ran while one was open for 1% of the time, Pallas kernels for 0%

commit v1 on v0

--- a/solution.py
+++ b/solution.py
@@ -130,66 +130,94 @@
     return ref[:, plane, cell].reshape(slabs * rows, lanes)
 
 
-def neighbours(cells, here, before, after):
-    previous = [(before, 0)] + [(here, c) for c in range(cells - 1)]
-    following = [(here, c) for c in range(1, cells)] + [(after, 0)]
-    return previous, following
-
-
-def screen_kernel(here, before, after, diag, upper, lower, out):
+def terms_of(cells, here, received, diag, upper, edges):
+    terms = []
+    for c in range(cells):
+        terms.append((c, functools.partial(diag, c), functools.partial(block_of, here, cell=c)))
+        if c + 1 < cells:
+            terms.append((c, functools.partial(upper, c), functools.partial(block_of, here, cell=c + 1)))
+            terms.append((c + 1, functools.partial(upper, c, turned=True), functools.partial(block_of, here, cell=c)))
+    for target, matrix, ref in zip(*edges, received, strict=True):
+        terms.append((target, matrix, functools.partial(block_of, ref, cell=0)))
+    return terms
+
+
+def screen_kernel(halos, targets, *refs):
+    here, diag, upper = refs[:3]
+    received, matrices, out = refs[3 : 3 + halos], refs[3 + halos : -1], refs[-1]
     slabs, planes, cells, rows, lanes = here.shape
-    previous, following = neighbours(cells, here, before, after)
-    for c in range(cells):
-        symmetric = (diag[c] + diag[c].T) * 0.5
-        lefts, inners = [], []
-        for matrix, (ref, cell) in (
-            (symmetric, (here, c)),
-            (upper[c], following[c]),
-            (lower[c].T, previous[c]),
-        ):
-            left = parts(matrix)
-            lefts.append(left)
-            stacked = jnp.concatenate([block_of(ref, p, cell) for p in range(planes)], 0)
-            inners.append(parts(product(parts(stacked), left, True)))
-        left = join(lefts, 1)
+
+    def symmetric(c):
+        return (diag[c] + diag[c].T) * 0.5
+
+    def above(c, turned=False):
+        return upper[c].T if turned else upper[c]
+
+    edges = ([targets[i] for i in range(halos)], [lambda m=m: m[...] for m in matrices])
+    by_cell, others = {}, []
+    for target, matrix, read in terms_of(cells, here, received, symmetric, above, edges):
+        left = parts(matrix())
+        stacked = parts(jnp.concatenate([read(plane=p) for p in range(planes)], 0))
+        term = (left, parts(product(stacked, left, True)))
+        if isinstance(target, int):
+            by_cell.setdefault(target, []).append(term)
+        else:
+            others.append((target, [term]))
+    for target, terms in list(by_cell.items()) + others:
+        left = join([t[0] for t in terms], 1)
         for p in range(planes):
-            inner = join([tuple(q[p * lanes : (p + 1) * lanes] for q in i) for i in inners], 0)
-            out[:, p, c] = product(left, inner).reshape(slabs, rows, lanes)
-
-
-def output_kernel(here, before, after, diag, upper, lower, out):
+            inner = join([tuple(q[p * lanes : (p + 1) * lanes] for q in t[1]) for t in terms], 0)
+            total = product(left, inner).reshape(slabs, rows, lanes)
+            if isinstance(target, int):
+                out[:, p, target] = total
+            else:
+                out[:, p, target] = out[:, p, target] + total
+
+
+def output_kernel(halos, targets, *refs):
+    here, diag, upper = refs[:3]
+    received, matrices, out = refs[3 : 3 + halos], refs[3 + halos : -1], refs[-1]
     _, planes, cells, _, lanes = here.shape
-    previous, following = neighbours(cells, here, before, after)
-    for c in range(cells):
-        total = None
-        for matrix, turned, (ref, cell) in (
-            (diag, False, (here, c)),
-            (upper, False, following[c]),
-            (lower, True, previous[c]),
-        ):
-            re, im = matrix[0, 0, c], matrix[1, 0, c]
-            if turned:
-                re, im = re.T, im.T
-            re, im = parts(re), parts(im)
-            middle = parts(jnp.concatenate([block_of(ref, p, cell) for p in range(planes)], 0))
-            left = join([join([re, negative(im)], 1), join([im, re], 1)], 0)
-            inner = parts(product(left, middle))
-            inner_re = tuple(q[:lanes] for q in inner)
-            inner_im = tuple(q[lanes:] for q in inner)
-            rows = join([join([inner_re, inner_im], 1), join([inner_im, negative(inner_re)], 1)], 0)
-            term = product(rows, join([re, im], 1), True)
-            total = term if total is None else total + term
+
+    def pair(ref, c, turned=False):
+        re, im = ref[0, 0, c], ref[1, 0, c]
+        return (re.T, im.T) if turned else (re, im)
+
+    edges = ([targets[i] for i in range(halos)], [lambda m=m: (m[0], m[1]) for m in matrices])
+    totals = {}
+    for target, matrix, read in terms_of(
+        cells, here, received, functools.partial(pair, diag), functools.partial(pair, upper), edges
+    ):
+        re, im = (parts(m) for m in matrix())
+        middle = parts(jnp.concatenate([read(plane=p) for p in range(planes)], 0))
+        left = join([join([re, negative(im)], 1), join([im, re], 1)], 0)
+        inner = parts(product(left, middle))
+        inner_re = tuple(q[:lanes] for q in inner)
+        inner_im = tuple(q[lanes:] for q in inner)
+        rows = join([join([inner_re, inner_im], 1), join([inner_im, negative(inner_re)], 1)], 0)
+        term = product(rows, join([re, im], 1), True)
+        if isinstance(target, int):
+            totals[target] = totals[target] + term if target in totals else term
+        else:
+            for c, total in totals.items():
+                out[0, 0, c] = total[:lanes]
+                out[1, 0, c] = total[lanes:]
+            totals = {}
+            out[0, 0, target] = out[0, 0, target] + term[:lanes]
+            out[1, 0, target] = out[1, 0, target] + term[lanes:]
+    for c, total in totals.items():
         out[0, 0, c] = total[:lanes]
         out[1, 0, c] = total[lanes:]
 
 
-def call(kernel, outs, *args):
+def call(kernel, outs, *args, scalars=False):
+    first = [pl.BlockSpec(memory_space=pltpu.SMEM)] if scalars else []
     return pl.pallas_call(
         kernel,
         out_shape=outs,
-        in_specs=[VMEM] * len(args),
+        in_specs=first + [VMEM] * (len(args) - len(first)),
         out_specs=jax.tree.map(lambda _: VMEM, outs),
-        compiler_params=pltpu.CompilerParams(vmem_limit_bytes=48 * 1024 * 1024),
+        compiler_params=pltpu.CompilerParams(vmem_limit_bytes=24 * 1024 * 1024),
     )(*args)
 
 
@@ -207,8 +235,37 @@
     return lax.ppermute(block, axis, route)
 
 
+def swapped(block):
+    return lax.ppermute(block, "cell", [(0, 1), (1, 0)])
+
+
 def halo(values):
-    return (shifted(values[:, :, -1:], "cell", 1), shifted(values[:, :, :1], "cell", -1))
+    count = lax.axis_size("cell")
+    if count == 1:
+        return []
+    head, tail = values[:, :, :1], values[:, :, -1:]
+    if count == 2:
+        return [swapped(jnp.where(lax.axis_index("cell") == 0, tail, head))]
+    return [shifted(tail, "cell", 1), shifted(head, "cell", -1)]
+
+
+def halo_targets(cells):
+    count = lax.axis_size("cell")
+    if count == 2:
+        targets = [jnp.where(lax.axis_index("cell") == 0, cells - 1, 0)]
+    else:
+        targets = [0, cells - 1]
+    return jnp.stack([jnp.asarray(t, jnp.int32) for t in targets])
+
+
+def halo_matrices(last_upper):
+    count = lax.axis_size("cell")
+    if count == 1:
+        return []
+    before = jnp.swapaxes(shifted(last_upper, "cell", 1), -1, -2)
+    if count == 2:
+        return [jnp.where(lax.axis_index("cell") == 0, last_upper, before)]
+    return [before, last_upper]
 
 
 def per_device(green_pair, retarded_diag, retarded_upper, coulomb_diag, coulomb_upper):
@@ -217,27 +274,39 @@
     points = devices * held
     scaling = 1.0 / math.sqrt(points)
     rows = orbitals // devices
-    coulomb_edge = shifted(coulomb_upper[-1:], "cell", 1)
-    retarded_edge = shifted(retarded_upper[:, :, -1:], "cell", 1)
-    coulomb_before = jnp.concatenate([coulomb_edge, coulomb_upper[:-1]], 0)
-    retarded_before = jnp.concatenate([retarded_edge, retarded_upper[:, :, :-1]], 2)
+    targets = halo_targets(cells)
+    coulomb_edges = halo_matrices(coulomb_upper[-1])
+    retarded_edges = halo_matrices(retarded_upper[:, 0, -1])
+    halos = len(coulomb_edges)
     slabs = green_pair.reshape(4, cells, devices, rows, orbitals).transpose(2, 0, 1, 3, 4)
     entries = exchange(slabs)
     half = shape((points, 2, cells, rows, orbitals))
     lesser_hat, polar_hat = call(functools.partial(polarize_kernel, scaling), (half, half), entries)
     polar = exchange(polar_hat)
-    screened = call(screen_kernel, half, polar, *halo(polar), coulomb_diag, coulomb_upper, coulomb_before)
+    screened = call(
+        functools.partial(screen_kernel, halos),
+        half,
+        targets,
+        polar,
+        coulomb_diag,
+        coulomb_upper,
+        *halo(polar),
+        *coulomb_edges,
+        scalars=True,
+    )
     screened_hat = exchange(screened)
     sigma_entries = call(functools.partial(convolve_kernel, scaling / points), half, lesser_hat, screened_hat)
     sigma = exchange(sigma_entries)
     return call(
-        output_kernel,
+        functools.partial(output_kernel, halos),
         shape(retarded_diag.shape),
+        targets,
         sigma,
-        *halo(sigma),
         retarded_diag,
         retarded_upper,
-        retarded_before,
+        *halo(sigma),
+        *retarded_edges,
+        scalars=True,
     )
 
 

time: 172 us -> 168 us (0.977)
  blocking collectives: 112 us -> 84.2 us
  waiting for transfers between devices: 22.2 us -> 45.8 us
    all_to_all x3 -> x2, blocking collectives: 112 us -> 84.2 us  [exchange(): lax.all_to_all(values, 'energy', split_axis=0, concat_axis=0, tiled=True)]
    all_to_all x1 -> x2, waiting for transfers between devices: 19.7 us -> 42 us  [exchange(): lax.all_to_all(values, 'energy', split_axis=0, concat_axis=0, tiled=True)]
    ppermute x6 -> x2, starting transfers between devices: 15.7 us -> 2.56 us  [shifted(): return lax.ppermute(block, axis, route)]
    ppermute x0 -> x2, starting transfers between devices: none -> 6.53 us  [swapped(): return lax.ppermute(block, 'cell', [(0, 1), (1, 0)])]
    all_to_all x1 -> x2, starting transfers between devices: 4.82 us -> 10.1 us  [exchange(): lax.all_to_all(values, 'energy', split_axis=0, concat_axis=0, tiled=True)]
    unnamed x10 -> x12, local copies, waits for them, and re-layouts: 0.02 us -> 2.81 us
  transfers between devices with their start and end apart: 7 -> 6, of which waited for: 3 -> 4; matrix products, arithmetic and copies ran while one was open for 1% -> 1% of each run, Pallas kernels for 0% -> 0%
where the time goes in v1:
time: 168 us; the launch traced here: 167 us
  blocking collectives  84.2 us (50%)
  waiting for transfers between devices  45.8 us (27%)
  starting transfers between devices  19.1 us (11%)
  Pallas kernels  11.6 us (7%)
  local copies, waits for them, and re-layouts  4.59 us (3%)
    all_to_all x2, blocking collectives, exchange(): lax.all_to_all(values, 'energy', split_axis=0, concat_axis=0, tiled=True)  84.2 us
    all_to_all x2, waiting for transfers between devices, exchange(): lax.all_to_all(values, 'energy', split_axis=0, concat_axis=0, tiled=True)  42 us
    pallas_call x4, Pallas kernels, call(): pl.pallas_call(kernel, out_shape=outs, in_specs=first + [VMEM] * (len(arg...  11.6 us
    all_to_all x2, starting transfers between devices, exchange(): lax.all_to_all(values, 'energy', split_axis=0, concat_axis=0, tiled=True)  10.1 us
    ppermute x2, starting transfers between devices, swapped(): return lax.ppermute(block, 'cell', [(0, 1), (1, 0)])  6.53 us
  transfers between devices with their start and end apart: 6, of which 4 were waited for; matrix products, arithmetic and copies ran while one was open for 1% of the time, Pallas kernels for 0%

profile of v1, /device:TPU:1, one launch (start us, length us, event | category | flops | bytes accessed | tf_op | source)
XLA Modules:
  0.0 166.6 jit_solution(13113895453278791655)
XLA Ops:
  0.0 1.8 %copy.20 = f32[4,2,16,16,256]{4,3,1,0,2:T(8,128)S(1)} copy(f32[4,2,16,16,256]{4,3,2,1,0:T(8,128)} %bitcast.16) | data formatting | bytes 4194304 | tf_op jit(solution)/shard_map/reshape | solution.py:281
  1.8 54.2 %all_to_all.20.entries = f32[16,4,2,16,256]{4,3,2,1,0:T(8,128)S(1)} all-to-all(f32[16,4,2,16,256]{4,3,2,1,0:T(8,128)S(1)} %bitcast.15), channel_id=1, replica_groups=mesh['energy'=16,'cell'=2] {'energy'}, dimensions={0} | all-to-all | bytes 4194304 | tf_op jit(solution)/shard_map/all_to_all | solution.py:229
  56.0 0.6 shard_map.55
  56.6 0.0 copy-start.2
  56.6 1.0 copy-done.2
  57.6 0.0 slice-start.1
  57.6 0.0 copy-start.1
  57.6 5.1 %all-to-all-start.1 = ((f32[16,2,2,16,256]{4,3,2,1,0:T(8,128)}), f32[16,2,2,16,256]{4,3,2,1,0:T(8,128)S(1)}, u32[]{:S(2)}, u32[]{:S(2)}) async-start(f32[16,2,2,16,256]{4,3,2,1,0:T(8,128)} %copy-done.2), calls=%async_computation.1 | async-start | bytes 2097152 | tf_op jit(solution)/shard_map/all_to_all | solution.py:229
  62.7 0.0 copy-start.4
  62.7 22.2 %all-to-all-done.1.refs_0_ = f32[16,2,2,16,256]{4,3,2,1,0:T(8,128)S(1)} async-done(((f32[16,2,2,16,256]{4,3,2,1,0:T(8,128)}), f32[16,2,2,16,256]{4,3,2,1,0:T(8,128)S(1)}, u32[]{:S(2)}, u32[]{:S(2)}) %all-to-all-start.1) | async-done | bytes 1048608 | tf_op jit(solution)/shard_map/all_to_all | solution.py:229
  84.9 0.9 slice_select_fusion.1
  85.7 3.2 %collective-permute-start = (f32[16,2,1,16,256]{4,3,2,1,0:T(8,128)}, f32[16,2,1,16,256]{4,3,2,1,0:T(8,128)}, u32[]{:S(2)}, u32[]{:S(2)}) collective-permute-start(f32[16,2,1,16,256]{4,3,2,1,0:T(8,128)} %slice_select_fusion.1), channel_id=1, source_target_pairs={{0,1},{1,0},{2,3},{3,2},{4,5},{5,4},{6,7},{7,6},{8,9},{9,8},{10,11... | collective-permute-start | bytes 1572872 | tf_op jit(solution)/shard_map/ppermute | solution.py:239
  89.0 0.0 slice-done.1
  89.0 0.8 copy.15
  89.8 1.3 collective-permute-start.1
  91.1 2.3 %collective-permute-done.1 = f32[256,256]{0,1:T(8,128)S(1)} collective-permute-done((f32[256,256]{0,1:T(8,128)}, f32[256,256]{0,1:T(8,128)S(1)}, u32[]{:S(2)}, u32[]{:S(2)}) %collective-permute-start.1) | collective-permute-done | bytes 262176 | tf_op jit(solution)/shard_map/ppermute | solution.py:235
  93.4 0.0 copy-done.1
  93.5 0.0 collective-permute-done.refs_3_
  93.5 0.0 copy-done.4
  93.5 3.4 %shard_map.56 = f32[16,2,2,16,256]{4,3,2,1,0:T(8,128)S(1)} custom-call(s32[1]{0:T(128)} %bitcast.targets, f32[16,2,2,16,256]{4,3,2,1,0:T(8,128)S(1)} %all-to-all-done.1.refs_0_, f32[2,256,256]{2,1,0:T(8,128)S(1)} %copy-done.4, f32[2,256,256]{2,1,0:T(8,128)S(1)} %copy-done.1, f32[16,2,1,16,256]{4,3,2,1,0:T(8,128)} %collective-permute-done.refs_3_, ...), custom_call_target="tpu_custom_call" | custom-call | tf_op jit(solution)/shard_map/pallas_call | solution.py:215
  96.9 30.0 %all_to_all.21.screened_hat = f32[16,2,2,16,256]{4,3,2,1,0:T(8,128)S(1)} all-to-all(f32[16,2,2,16,256]{4,3,2,1,0:T(8,128)S(1)} %shard_map.56), channel_id=1, replica_groups=mesh['energy'=16,'cell'=2] {'energy'}, dimensions={0} | all-to-all | bytes 2097152 | tf_op jit(solution)/shard_map/all_to_all | solution.py:229
  127.0 1.5 shard_map.57
  128.5 0.0 slice-start
  128.5 5.0 %all-to-all-start.3 = ((f32[16,2,2,16,256]{4,3,2,1,0:T(8,128)}), f32[16,2,2,16,256]{4,3,2,1,0:T(8,128)S(1)}, u32[]{:S(2)}, u32[]{:S(2)}) async-start(f32[16,2,2,16,256]{4,3,2,1,0:T(8,128)} %shard_map.57), calls=%async_computation.3 | async-start | bytes 2097152 | tf_op jit(solution)/shard_map/all_to_all | solution.py:229
  133.4 0.0 copy-start
  133.5 0.0 slice-done
  133.5 1.0 copy.16
  134.5 1.3 collective-permute-start.3
  135.8 19.9 %all-to-all-done.3.refs_0_ = f32[16,2,2,16,256]{4,3,2,1,0:T(8,128)S(1)} async-done(((f32[16,2,2,16,256]{4,3,2,1,0:T(8,128)}), f32[16,2,2,16,256]{4,3,2,1,0:T(8,128)S(1)}, u32[]{:S(2)}, u32[]{:S(2)}) %all-to-all-start.3) | async-done | bytes 1048608 | tf_op jit(solution)/shard_map/all_to_all | solution.py:229
  155.6 0.0 copy-start.3
  155.6 0.1 slice_select_fusion
  155.7 3.3 %collective-permute-start.2 = (f32[16,2,1,16,256]{4,3,2,1,0:T(8,128)S(1)}, f32[16,2,1,16,256]{4,3,2,1,0:T(8,128)S(1)}, u32[]{:S(2)}, u32[]{:S(2)}) collective-permute-start(f32[16,2,1,16,256]{4,3,2,1,0:T(8,128)S(1)} %slice_select_fusion), channel_id=1, source_target_pairs={{0,1},{1,0},{2,3},{3,2},{4,5},{5,4},{6,7},{7,6},{8,9},{9,8},{10,11... | collective-permute-start | bytes 1572872 | tf_op jit(solution)/shard_map/ppermute | solution.py:239
  159.0 0.0 collective-permute-done.3
  159.0 0.0 copy-done
  159.0 0.1 bitcast_select_fusion.refs_4_
  159.1 1.5 collective-permute-done.2.refs_3_
  160.6 0.0 copy-done.3
  160.6 6.0 %shard_map.58 = f32[2,1,2,256,256]{4,3,2,1,0:T(8,128)} custom-call(s32[1]{0:T(128)} %bitcast.targets, f32[16,2,2,16,256]{4,3,2,1,0:T(8,128)S(1)} %all-to-all-done.3.refs_0_, f32[2,1,2,256,256]{4,3,2,1,0:T(8,128)S(1)} %copy-done.3, f32[2,1,2,256,256]{4,3,2,1,0:T(8,128)S(1)} %copy-done, f32[16,2,1,16,256]{4,3,2,1,0:T(8,128)S(1)} %collective-permute-done.2.refs_3_, ...), custom_call_target="tpu_custom_call" | custom-call | tf_op jit(solution)/shard_map/pallas_call | solution.py:215
  (1 shorter events, 0.0 us)
Async XLA Ops:
  56.6 1.0 copy-start.2
  57.6 31.4 %slice-start.1 = ((f32[2,256,256]{2,1,0:T(8,128)}), f32[1,256,256]{2,1,0:T(8,128)S(1)}, s32[]{:S(2)}) async-start(f32[2,256,256]{2,1,0:T(8,128)} %refs_2_.2), calls=%async_computation.5 | async-start | bytes 524288 | tf_op jit(solution)/shard_map/slice | solution.py:278
  57.6 35.9 %copy-start.1 = (f32[2,256,256]{2,1,0:T(8,128)S(1)}, f32[2,256,256]{2,1,0:T(8,128)}, u32[]{:S(2)}) copy-start(f32[2,256,256]{2,1,0:T(8,128)} %refs_2_.2) | copy-start | bytes 1572868
  57.6 27.3 %all-to-all-start.1 = ((f32[16,2,2,16,256]{4,3,2,1,0:T(8,128)}), f32[16,2,2,16,256]{4,3,2,1,0:T(8,128)S(1)}, u32[]{:S(2)}, u32[]{:S(2)}) async-start(f32[16,2,2,16,256]{4,3,2,1,0:T(8,128)} %copy-done.2), calls=%async_computation.1 | async-start | bytes 2097152 | tf_op jit(solution)/shard_map/all_to_all | solution.py:229
  62.7 30.8 %copy-start.4 = (f32[2,256,256]{2,1,0:T(8,128)S(1)}, f32[2,256,256]{2,1,0:T(8,128)}, u32[]{:S(2)}) copy-start(f32[2,256,256]{2,1,0:T(8,128)} %refs_1_.2) | copy-start | bytes 1572868
  85.7 7.7 %collective-permute-start = (f32[16,2,1,16,256]{4,3,2,1,0:T(8,128)}, f32[16,2,1,16,256]{4,3,2,1,0:T(8,128)}, u32[]{:S(2)}, u32[]{:S(2)}) collective-permute-start(f32[16,2,1,16,256]{4,3,2,1,0:T(8,128)} %slice_select_fusion.1), channel_id=1, source_target_pairs={{0,1},{1,0},{2,3},{3,2},{4,5},{5,4},{6,7},{7,6},{8,9},{9,8},{10,11... | collective-permute-start | bytes 1572872 | tf_op jit(solution)/shard_map/ppermute | solution.py:239
  89.8 3.6 %collective-permute-start.1 = (f32[256,256]{0,1:T(8,128)}, f32[256,256]{0,1:T(8,128)S(1)}, u32[]{:S(2)}, u32[]{:S(2)}) collective-permute-start(f32[256,256]{0,1:T(8,128)} %bitcast.18), channel_id=1, source_target_pairs={{0,1},{2,3},{4,5},{6,7},{8,9},{10,11},{12,13},{14,15},{16,17},{18,... | collective-permute-start | bytes 786440 | tf_op jit(solution)/shard_map/ppermute | solution.py:235
  128.5 5.0 %slice-start = ((f32[2,1,2,256,256]{4,3,2,1,0:T(8,128)}), f32[2,1,1,256,256]{4,3,2,1,0:T(8,128)S(1)}, s32[]{:S(2)}) async-start(f32[2,1,2,256,256]{4,3,2,1,0:T(8,128)} %refs_2_.3), calls=%async_computation.4 | async-start | bytes 1048576 | tf_op jit(solution)/shard_map/slice | solution.py:279
  128.5 27.1 %all-to-all-start.3 = ((f32[16,2,2,16,256]{4,3,2,1,0:T(8,128)}), f32[16,2,2,16,256]{4,3,2,1,0:T(8,128)S(1)}, u32[]{:S(2)}, u32[]{:S(2)}) async-start(f32[16,2,2,16,256]{4,3,2,1,0:T(8,128)} %shard_map.57), calls=%async_computation.3 | async-start | bytes 2097152 | tf_op jit(solution)/shard_map/all_to_all | solution.py:229
  133.4 25.6 %copy-start = (f32[2,1,2,256,256]{4,3,2,1,0:T(8,128)S(1)}, f32[2,1,2,256,256]{4,3,2,1,0:T(8,128)}, u32[]{:S(2)}) copy-start(f32[2,1,2,256,256]{4,3,2,1,0:T(8,128)} %refs_2_.3) | copy-start | bytes 3145732
  134.5 24.6 %collective-permute-start.3 = (f32[2,256,256]{1,2,0:T(8,128)}, f32[2,256,256]{1,2,0:T(8,128)S(1)}, u32[]{:S(2)}, u32[]{:S(2)}) collective-permute-start(f32[2,256,256]{1,2,0:T(8,128)} %bitcast.17), channel_id=1, source_target_pairs={{0,1},{2,3},{4,5},{6,7},{8,9},{10,11},{12,13},{14,15},{16,17},{18,... | collective-permute-start | bytes 1572872 | tf_op jit(solution)/shard_map/ppermute | solution.py:235
  155.6 4.9 %copy-start.3 = (f32[2,1,2,256,256]{4,3,2,1,0:T(8,128)S(1)}, f32[2,1,2,256,256]{4,3,2,1,0:T(8,128)}, u32[]{:S(2)}) copy-start(f32[2,1,2,256,256]{4,3,2,1,0:T(8,128)} %refs_1_.3) | copy-start | bytes 3145732
  155.7 4.8 %collective-permute-start.2 = (f32[16,2,1,16,256]{4,3,2,1,0:T(8,128)S(1)}, f32[16,2,1,16,256]{4,3,2,1,0:T(8,128)S(1)}, u32[]{:S(2)}, u32[]{:S(2)}) collective-permute-start(f32[16,2,1,16,256]{4,3,2,1,0:T(8,128)S(1)} %slice_select_fusion), channel_id=1, source_target_pairs={{0,1},{1,0},{2,3},{3,2},{4,5},{5,4},{6,7},{7,6},{8,9},{9,8},{10,11... | collective-permute-start | bytes 1572872 | tf_op jit(solution)/shard_map/ppermute | solution.py:239

commit v2 on v0

v2 whole, which is shorter than its diff:
```python
import functools
import math

import jax
import jax.numpy as jnp
from jax import lax
from jax.experimental import pallas as pl
from jax.experimental.pallas import tpu as pltpu
from jax.sharding import PartitionSpec as P

VMEM = pl.BlockSpec(memory_space=pltpu.VMEM)
f32 = jnp.float32
bf16 = jnp.bfloat16


def times_root(value, turn, points, sign):
    re, im = value
    turn = turn % points
    if turn == 0:
        return value
    if 4 * turn == points:
        return (-im, re) if sign > 0 else (im, -re)
    if 2 * turn == points:
        return (-re, -im)
    if 4 * turn == 3 * points:
        return (im, -re) if sign > 0 else (-im, re)
    angle = 2.0 * math.pi * turn / points
    c, s = math.cos(angle), sign * math.sin(angle)
    if 8 * turn % points == 0:
        unit = abs(c)
        a = re if c > 0 else -re
        b = im if c > 0 else -im
        if (s > 0) == (c > 0):
            return ((a - b) * unit, (a + b) * unit)
        return ((a + b) * unit, (b - a) * unit)
    return (re * c - im * s, re * s + im * c)


def fourier(values, sign):
    points = len(values)
    if points == 1:
        return values
    if points % 2:
        out = []
        for k in range(points):
            total = values[0]
            for n in range(1, points):
                term = times_root(values[n], k * n, points, sign)
                total = (total[0] + term[0], total[1] + term[1])
            out.append(total)
        return out
    even = fourier(values[0::2], sign)
    odd = fourier(values[1::2], sign)
    low, high = [], []
    for k in range(points // 2):
        a = even[k]
        b = times_root(odd[k], k, points, sign)
        low.append((a[0] + b[0], a[1] + b[1]))
        high.append((a[0] - b[0], a[1] - b[1]))
    return low + high


def tiles_of(rows, lanes):
    step_rows = 8 if rows % 8 == 0 else rows
    step_lanes = 128 if lanes % 128 == 0 else lanes
    return [
        (pl.ds(r, step_rows), pl.ds(b, step_lanes))
        for r in range(0, rows, step_rows)
        for b in range(0, lanes, step_lanes)
    ]


def spectrum(read, points, sign):
    return fourier([read(n) for n in range(points)], sign)


def split_of(devices):
    inner = next(i for i in range(math.isqrt(devices), 0, -1) if devices % i == 0)
    return inner, devices // inner


def along_outer(blocks, inner):
    devices = lax.axis_size("energy")
    return [
        lax.ppermute(b, "energy", [(e, (e + s * inner) % devices) for e in range(devices)]) if s else b
        for s, b in enumerate(blocks)
    ]


def along_inner(blocks, inner):
    devices = lax.axis_size("energy")
    return [
        lax.ppermute(b, "energy", [(e, e - e % inner + (e + t) % inner) for e in range(devices)]) if t else b
        for t, b in enumerate(blocks)
    ]


def pack_kernel(outer, inner, place, *refs):
    blocks, outs = refs[:outer], refs[outer:]
    for t in range(inner):
        to = lax.rem(place[1] + t, inner)
        for s in range(outer):
            outs[t][lax.rem(place[0] + outer - s, outer)] = blocks[s][:, to]


def exchange(place, blocks, inner):
    outer = len(blocks)
    arrived = along_outer(blocks, inner)
    q, _, rows, lanes = blocks[0].shape
    packed = call(
        functools.partial(pack_kernel, outer, inner), [shape((outer, q, rows, lanes))] * inner, place, *arrived
    )
    return along_inner(packed, inner)


def gather(place, arrived, write):
    inner = len(arrived)
    for t, ref in enumerate(arrived):
        origin = lax.rem(place[1] + inner - t, inner)
        for z in range(ref.shape[0]):
            write(z * inner + origin, ref[z])


def emit(place, outs, inner, read):
    outer = len(outs)
    for s, out in enumerate(outs):
        out[...] = read(pl.multiple_of(lax.rem(place[0] + s, outer) * inner, inner), inner)


def polarize_kernel(scaling, inner, groups, place, *refs):
    arrived, lesser_hat, entries, polar = refs[:inner], refs[inner], refs[-2], refs[-1]
    outs = refs[inner + 1 : -2]
    outer = len(outs) // len(groups)
    points, _, rows, lanes = entries.shape

    def write(n, block):
        entries[n] = block

    gather(place, arrived, write)
    for r, b in tiles_of(rows, lanes):
        lesser = spectrum(lambda n: (entries[n, 0, r, b], entries[n, 1, r, b]), points, -1)
        for k, (re, im) in enumerate(lesser):
            lesser_hat[k, 0, r, b] = re
            lesser_hat[k, 1, r, b] = im
        greater = spectrum(lambda n: (entries[n, 2, r, b], entries[n, 3, r, b]), points, -1)
        for k, (re, im) in enumerate(greater):
            lesser_re, lesser_im = lesser_hat[k, 0, r, b], lesser_hat[k, 1, r, b]
            polar[0, k, r, b] = (lesser_re * im - lesser_im * re) * scaling
            polar[1, k, r, b] = (lesser_re * re + lesser_im * im) * scaling
    for g, planes in enumerate(groups):
        emit(
            place,
            outs[g * outer : (g + 1) * outer],
            inner,
            lambda start, count, planes=planes: polar[pl.ds(planes[0], len(planes)), pl.ds(start, count)],
        )


def convolve_kernel(factor, inner, cell, place, *refs):
    screened = (refs[:inner], refs[inner : 2 * inner])
    lesser_hat, outs, entries, sigma = refs[2 * inner], refs[2 * inner + 1 : -2], refs[-2], refs[-1]
    points, _, rows, lanes = entries.shape

    def write_re(k, block):
        entries[k, 0] = block[cell]

    def write_im(k, block):
        entries[k, 1] = block[0]

    gather(place, screened[0], write_re)
    gather(place, screened[1], write_im)
    for r, b in tiles_of(rows, lanes):

        def spectral(k):
            lesser_re, lesser_im = lesser_hat[k, 0, r, b], lesser_hat[k, 1, r, b]
            w_re, w_im = entries[k, 0, r, b], entries[k, 1, r, b]
            return ((lesser_re * w_re - lesser_im * w_im) * factor, (lesser_re * w_im + lesser_im * w_re) * factor)

        for n, (re, im) in enumerate(spectrum(spectral, points, 1)):
            sigma[0, n, r, b] = -im
            sigma[1, n, r, b] = re
    emit(place, outs, inner, lambda start, count: sigma[:, pl.ds(start, count)])


def parts(matrix):
    high = matrix.astype(bf16)
    return (high, (matrix - high.astype(f32)).astype(bf16))


def join(pieces, axis):
    return tuple(jnp.concatenate(p, axis) for p in zip(*pieces, strict=True))


def negative(pair):
    return tuple(-p for p in pair)


def product(left, right, turned=False):
    dims = (((1,), (1 if turned else 0,)), ((), ()))
    dot = functools.partial(lax.dot_general, dimension_numbers=dims, preferred_element_type=f32)
    return dot(left[0], right[0]) + (dot(left[0], right[1]) + dot(left[1], right[0]))


def gather_kernel(inner, cells, plane, halos, place, *refs):
    here, edges = refs[inner * cells], refs[inner * cells + 1 :]
    for c in range(cells):

        def write(e, block, c=c):
            here[c, e] = block[plane[c]]

        gather(place, refs[c * inner : (c + 1) * inner], write)
    for i in range(halos):
        edges[i][...] = here[place[2 + halos + i]]


def screen_kernel(inner, groups, halos, place, *refs):
    here, diag, upper = refs[:3]
    received, matrices = refs[3 : 3 + halos], refs[3 + halos : 3 + 2 * halos]
    outs, total = refs[3 + 2 * halos : -1], refs[-1]
    outer = len(outs) // len(groups)
    cells, devices, rows, lanes = here.shape

    def block(ref, *at):
        return ref[at].reshape(devices * rows, lanes) if at else ref[...].reshape(devices * rows, lanes)

    def inner_of(left, middle):
        return parts(product(parts(middle), left, True))

    for c in range(cells):
        terms = [((diag[c] + diag[c].T) * 0.5, block(here, c))]
        if c + 1 < cells:
            terms.append((upper[c], block(here, c + 1)))
        if c:
            terms.append((upper[c - 1].T, block(here, c - 1)))
        lefts = [parts(m) for m, _ in terms]
        inners = [inner_of(left, x) for left, (_, x) in zip(lefts, terms, strict=True)]
        total[c] = product(join(lefts, 1), join(inners, 0)).reshape(devices, rows, lanes)
    for i in range(halos):
        left = parts(matrices[i][...])
        term = product(left, inner_of(left, block(received[i]))).reshape(devices, rows, lanes)
        total[place[2 + i]] = total[place[2 + i]] + term
    for g, members in enumerate(groups):
        emit(
            place,
            outs[g * outer : (g + 1) * outer],
            inner,
            lambda start, count, members=members: total[pl.ds(members[0], len(members)), pl.ds(start, count)],
        )


def complex_outer(matrix, middle):
    re, im = (parts(m) for m in matrix)
    lanes = middle.shape[1]
    left = join([join([re, negative(im)], 1), join([im, re], 1)], 0)
    inner = parts(product(left, parts(middle)))
    inner_re = tuple(q[:lanes] for q in inner)
    inner_im = tuple(q[lanes:] for q in inner)
    rows = join([join([inner_re, inner_im], 1), join([inner_im, negative(inner_re)], 1)], 0)
    return product(rows, join([re, im], 1), True)


def edges_kernel(inner, cells, halos, place, *refs):
    for i, edge in enumerate(refs[inner * cells :]):
        for c in range(cells):

            @pl.when(place[2 + halos + i] == c)
            def _(edge=edge, c=c):
                def write(e, block):
                    edge[:, e] = block

                gather(place, refs[c * inner : (c + 1) * inner], write)


def output_kernel(inner, cell, place, *refs):
    arrived, diag, upper = refs[:inner], refs[inner], refs[inner + 1]
    before, out, sigma = refs[inner + 2 : -2], refs[-2], refs[-1]
    cells = out.shape[2]
    _, devices, rows, lanes = sigma.shape

    def write(e, block):
        sigma[:, e] = block

    gather(place, arrived, write)
    middle = sigma[...].reshape(2 * devices * rows, lanes)
    terms = [(cell, (diag[0, 0, cell], diag[1, 0, cell]))]
    if cell:
        terms.append((cell - 1, (upper[0, 0, cell - 1], upper[1, 0, cell - 1])))
    if cell + 1 < cells:
        terms.append((cell + 1, (upper[0, 0, cell].T, upper[1, 0, cell].T)))
    added = {target: complex_outer(matrix, middle) for target, matrix in terms}
    for c in range(cells):
        for p in range(2):
            value = added[c][p * lanes : (p + 1) * lanes] if c in added else None
            if before:
                value = before[0][p, 0, c] if value is None else before[0][p, 0, c] + value
            out[p, 0, c] = jnp.zeros((lanes, lanes), f32) if value is None else value


def finish_kernel(halos, place, *refs):
    before, received, matrices, out = refs[0], refs[1 : 1 + halos], refs[1 + halos : -1], refs[-1]
    out[...] = before[...]
    for i in range(halos):
        planes, devices, rows, lanes = received[i].shape
        middle = received[i][...].reshape(planes * devices * rows, lanes)
        term = complex_outer((matrices[i][0], matrices[i][1]), middle)
        c = place[2 + i]
        for p in range(2):
            out[p, 0, c] = out[p, 0, c] + term[p * lanes : (p + 1) * lanes]


def call(kernel, outs, place, *args, scratch=(), **more):
    return pl.pallas_call(
        kernel,
        out_shape=outs,
        in_specs=[pl.BlockSpec(memory_space=pltpu.SMEM)] + [VMEM] * len(args),
        out_specs=jax.tree.map(lambda _: VMEM, outs),
        scratch_shapes=[pltpu.VMEM(dims, f32) for dims in scratch],
        compiler_params=pltpu.CompilerParams(vmem_limit_bytes=24 * 1024 * 1024),
        **more,
    )(place, *args)


def shape(dims):
    return jax.ShapeDtypeStruct(tuple(dims), f32)


def shifted(block, step):
    count = lax.axis_size("cell")
    return lax.ppermute(block, "cell", [(i, i + step) for i in range(count) if 0 <= i + step < count])


def halo_cells(cells):
    count = lax.axis_size("cell")
    if count == 1:
        return []
    if count == 2:
        edge = jnp.where(lax.axis_index("cell") == 0, cells - 1, 0)
        return [edge, edge]
    return [0, cells - 1, cells - 1, 0]


def from_neighbours(edges):
    if lax.axis_size("cell") == 2:
        return [lax.ppermute(edges[0], "cell", [(0, 1), (1, 0)])]
    return [shifted(edge, step) for edge, step in zip(edges, (1, -1), strict=False)]


def halo_matrices(last_upper):
    count = lax.axis_size("cell")
    if count == 1:
        return []
    before = jnp.swapaxes(shifted(last_upper, 1), -1, -2)
    if count == 2:
        return [jnp.where(lax.axis_index("cell") == 0, last_upper, before)]
    return [before, last_upper]


def per_device(green_pair, retarded_diag, retarded_upper, coulomb_diag, coulomb_upper):
    devices = lax.axis_size("energy")
    outer, inner = split_of(devices)
    _, held, cells, orbitals, _ = green_pair.shape
    points = devices * held
    scaling = 1.0 / math.sqrt(points)
    rows = orbitals // devices
    me = lax.axis_index("energy")
    z, r = me // inner, me % inner
    borders = halo_cells(cells)
    halos = len(borders) // 2
    place = jnp.stack([jnp.asarray(v, jnp.int32) for v in [z, r, *borders]])
    coulomb_edges = halo_matrices(coulomb_upper[-1])
    retarded_edges = halo_matrices(retarded_upper[:, 0, -1])

    def block(q):
        return shape((q, inner, rows, orbitals))

    lesser_hat, polar = [], []
    arrived = []
    for c in range(cells):
        green = green_pair[:, 0, c].reshape(4, devices, rows, orbitals)
        blocks = [
            lax.dynamic_slice_in_dim(green, (z + s) % outer * inner, inner, axis=1) for s in range(outer)
        ]
        arrived.append(exchange(place, blocks, inner))
    for c in range(cells):
        groups = ((0, 1),) if c + 1 < cells else ((0,), (1,))
        hat, *blocks = call(
            functools.partial(polarize_kernel, scaling, inner, groups),
            [shape((points, 2, rows, orbitals))] + [block(len(g)) for g in groups for _ in range(outer)],
            place,
            *arrived[c],
            scratch=((points, 4, rows, orbitals), (2, points, rows, orbitals)),
        )
        lesser_hat.append(hat)
        got = [exchange(place, blocks[i : i + outer], inner) for i in range(0, len(blocks), outer)]
        polar.append([(got[0], 0), (got[0], 1)] if len(groups) == 1 else [(got[0], 0), (got[1], 0)])
    screened = []
    for plane in range(2):
        sources = [polar[c][plane] for c in range(cells)]
        here, *edges = call(
            functools.partial(gather_kernel, inner, cells, [q for _, q in sources], halos),
            [shape((cells, devices, rows, orbitals))] + [shape((devices, rows, orbitals))] * halos,
            place,
            *[b for blocks, _ in sources for b in blocks],
        )
        groups = (tuple(range(cells)),) if plane == 0 else tuple((c,) for c in range(cells))
        blocks = call(
            functools.partial(screen_kernel, inner, groups, halos),
            [block(len(g)) for g in groups for _ in range(outer)],
            place,
            here,
            coulomb_diag,
            coulomb_upper,
            *from_neighbours(edges),
            *coulomb_edges,
            scratch=((cells, devices, rows, orbitals),),
        )
        screened.append([exchange(place, blocks[i : i + outer], inner) for i in range(0, len(blocks), outer)])
    sigma = []
    for c in range(cells):
        blocks = call(
            functools.partial(convolve_kernel, scaling / points, inner, c),
            [block(2)] * outer,
            place,
            *screened[0][0],
            *screened[1][c],
            lesser_hat[c],
            scratch=((points, 2, rows, orbitals), (2, points, rows, orbitals)),
        )
        sigma.append(exchange(place, blocks, inner))
    edges = call(
        functools.partial(edges_kernel, inner, cells, halos),
        [shape((2, devices, rows, orbitals))] * halos,
        place,
        *[b for blocks in sigma for b in blocks],
    )
    received = from_neighbours(edges)
    total = []
    for c in range(cells):
        total = [
            call(
                functools.partial(output_kernel, inner, c),
                shape(retarded_diag.shape),
                place,
                *sigma[c],
                retarded_diag,
                retarded_upper,
                *total,
                scratch=((2, devices, rows, orbitals),),
            )
        ]
    return call(functools.partial(finish_kernel, halos), shape(retarded_diag.shape), place, *total, *received, *retarded_edges)


def solution(mesh):
    over_both = P(None, "energy", "cell", None, None)
    over_cell = P("cell", None, None)
    return jax.shard_map(
        per_device,
        mesh=mesh,
        in_specs=(over_both, over_both, over_both, over_cell, over_cell),
        out_specs=over_both,
        check_vma=False,
    )
```

time: 172 us -> 206 us (1.20)
  blocking collectives: 112 us -> 0 us
  starting transfers between devices: 20.5 us -> 88.3 us
  waiting for transfers between devices: 22.2 us -> 85.2 us
  Pallas kernels: 12 us -> 26.5 us
  local copies, waits for them, and re-layouts: 3.06 us -> 5.35 us
    all_to_all x3 -> x0, blocking collectives: 112 us -> none  [exchange(): lax.all_to_all(values, 'energy', split_axis=0, concat_axis=0, tiled=True)]
    ppermute x6 -> x65, waiting for transfers between devices: 2.46 us -> 85.2 us  [the longest x30 66.8 us: along_outer(): lax.ppermute(b, 'energy', [(e, (e + s * inner) % devices) for e in range(...]
    ppermute x6 -> x65, starting transfers between devices: 15.7 us -> 88.3 us  [the longest x30 41.5 us: along_outer(): lax.ppermute(b, 'energy', [(e, (e + s * inner) % devices) for e in range(...]
    all_to_all x1 -> x0, waiting for transfers between devices: 19.7 us -> none  [exchange(): lax.all_to_all(values, 'energy', split_axis=0, concat_axis=0, tiled=True)]
    pallas_call x4 -> x22, Pallas kernels: 12 us -> 26.5 us  [call(): pl.pallas_call(kernel, out_shape=outs, in_specs=[pl.BlockSpec(memory_spac...]
    all_to_all x1 -> x0, starting transfers between devices: 4.82 us -> none  [exchange(): lax.all_to_all(values, 'energy', split_axis=0, concat_axis=0, tiled=True)]
  transfers between devices with their start and end apart: 7 -> 65, of which waited for: 3 -> 15; matrix products, arithmetic and copies ran while one was open for 1% -> 1% of each run, Pallas kernels for 0% -> 11%
where the time goes in v2:
time: 206 us
  starting transfers between devices  88.3 us (43%)
  waiting for transfers between devices  85.2 us (41%)
  Pallas kernels  26.5 us (13%)
  local copies, waits for them, and re-layouts  5.35 us (3%)
    ppermute x30, waiting for transfers between devices, along_outer(): lax.ppermute(b, 'energy', [(e, (e + s * inner) % devices) for e in range(...  66.8 us
    ppermute x30, starting transfers between devices, along_outer(): lax.ppermute(b, 'energy', [(e, (e + s * inner) % devices) for e in range(...  41.5 us
    ppermute x30, starting transfers between devices, along_inner(): lax.ppermute(b, 'energy', [(e, e - e % inner + (e + t) % inner) for e in...  31.8 us
    pallas_call x22, Pallas kernels, call(): pl.pallas_call(kernel, out_shape=outs, in_specs=[pl.BlockSpec(memory_spac...  26.5 us
    ppermute x30, waiting for transfers between devices, along_inner(): lax.ppermute(b, 'energy', [(e, e - e % inner + (e + t) % inner) for e in...  18.4 us
    ppermute x3, starting transfers between devices, from_neighbours(): return [lax.ppermute(edges[0], 'cell', [(0, 1), (1, 0)])]  12.5 us
  transfers between devices with their start and end apart: 65, of which 15 were waited for; matrix products, arithmetic and copies ran while one was open for 1% of the time, Pallas kernels for 11%

profile of v2, /device:TPU:1, one launch (start us, length us, event | category | flops | bytes accessed | tf_op | source)
XLA Modules:
  0.0 206.0 jit_solution(14084461426578037532)
XLA Ops:
  0.0 1.8 fusion
  1.8 0.9 constant_dynamic-slice_fusion
  2.7 2.1 %collective-permute-start.12 = (f32[4,4,16,256]{3,2,1,0:T(8,128)}, f32[4,4,16,256]{3,2,1,0:T(8,128)S(1)}, u32[]{:S(2)}, u32[]{:S(2)}) collective-permute-start(f32[4,4,16,256]{3,2,1,0:T(8,128)} %get-tuple-element.165), channel_id=1, source_target_pairs={{0,8},{2,10},{4,12},{6,14},{8,16},{10,18},{12,20},{14,22},{16,24},... | collective-permute-start | bytes 786440 | tf_op jit(solution)/shard_map/ppermute | solution.py:85
  4.8 2.3 %collective-permute-start.13 = (f32[4,4,16,256]{3,2,1,0:T(8,128)}, f32[4,4,16,256]{3,2,1,0:T(8,128)S(1)}, u32[]{:S(2)}, u32[]{:S(2)}) collective-permute-start(f32[4,4,16,256]{3,2,1,0:T(8,128)} %get-tuple-element.164), channel_id=1, source_target_pairs={{0,16},{2,18},{4,20},{6,22},{8,24},{10,26},{12,28},{14,30},{16,0},... | collective-permute-start | bytes 786440 | tf_op jit(solution)/shard_map/ppermute | solution.py:85
  7.1 1.1 collective-permute-start.14
  9.5 3.7 %collective-permute-done.12.refs_1_ = f32[4,4,16,256]{3,2,1,0:T(8,128)S(1)} collective-permute-done((f32[4,4,16,256]{3,2,1,0:T(8,128)}, f32[4,4,16,256]{3,2,1,0:T(8,128)S(1)}, u32[]{:S(2)}, u32[]{:S(2)}) %collective-permute-start.12) | collective-permute-done | bytes 262176 | tf_op jit(solution)/shard_map/ppermute | solution.py:85
  13.2 1.1 collective-permute-start.2
  14.3 11.6 %collective-permute-done.13.refs_2_ = f32[4,4,16,256]{3,2,1,0:T(8,128)S(1)} collective-permute-done((f32[4,4,16,256]{3,2,1,0:T(8,128)}, f32[4,4,16,256]{3,2,1,0:T(8,128)S(1)}, u32[]{:S(2)}, u32[]{:S(2)}) %collective-permute-start.13) | collective-permute-done | bytes 262176 | tf_op jit(solution)/shard_map/ppermute | solution.py:85
  26.5 1.5 collective-permute-start.15
  28.0 1.2 collective-permute-start.16
  30.1 1.9 collective-permute-start.17
  32.0 15.6 %collective-permute-done.1.refs_2_ = f32[4,4,16,256]{3,2,1,0:T(8,128)S(1)} collective-permute-done((f32[4,4,16,256]{3,2,1,0:T(8,128)S(1)}, f32[4,4,16,256]{3,2,1,0:T(8,128)S(1)}, u32[]{:S(2)}, u32[]{:S(2)}) %collective-permute-start.1) | collective-permute-done | bytes 262176 | tf_op jit(solution)/shard_map/ppermute | solution.py:85
  48.3 1.3 collective-permute-start.3
  49.5 1.2 collective-permute-start.4
  50.8 1.2 collective-permute-start.5
  51.9 1.6 shard_map.59
  53.5 5.9 %collective-permute-start.18 = (f32[1,4,16,256]{3,2,1,0:T(8,128)S(1)}, f32[1,4,16,256]{3,2,1,0:T(8,128)S(1)}, u32[]{:S(2)}, u32[]{:S(2)}) collective-permute-start(f32[1,4,16,256]{3,2,1,0:T(8,128)S(1)} %get-tuple-element.100), channel_id=1, source_target_pairs={{0,8},{2,10},{4,12},{6,14},{8,16},{10,18},{12,20},{14,22},{16,24},... | collective-permute-start | bytes 196616 | tf_op jit(solution)/shard_map/ppermute | solution.py:85
  59.5 3.6 %collective-permute-done.4.refs_2_ = f32[4,4,16,256]{3,2,1,0:T(8,128)S(1)} collective-permute-done((f32[4,4,16,256]{3,2,1,0:T(8,128)S(1)}, f32[4,4,16,256]{3,2,1,0:T(8,128)S(1)}, u32[]{:S(2)}, u32[]{:S(2)}) %collective-permute-start.4) | collective-permute-done | bytes 262176 | tf_op jit(solution)/shard_map/ppermute | solution.py:93
  63.1 1.7 shard_map.56
  64.7 6.0 %collective-permute-start.6 = (f32[2,4,16,256]{3,2,1,0:T(8,128)}, f32[2,4,16,256]{3,2,1,0:T(8,128)S(1)}, u32[]{:S(2)}, u32[]{:S(2)}) collective-permute-start(f32[2,4,16,256]{3,2,1,0:T(8,128)} %get-tuple-element.88), channel_id=1, source_target_pairs={{0,8},{2,10},{4,12},{6,14},{8,16},{10,18},{12,20},{14,22},{16,24},... | collective-permute-start | bytes 393224 | tf_op jit(solution)/shard_map/ppermute | solution.py:85
  70.9 1.9 collective-permute-start.8
  73.0 1.4 collective-permute-start.34
  74.4 11.6 %collective-permute-done.33.refs_2_ = f32[1,4,16,256]{3,2,1,0:T(8,128)S(1)} collective-permute-done((f32[1,4,16,256]{3,2,1,0:T(8,128)S(1)}, f32[1,4,16,256]{3,2,1,0:T(8,128)S(1)}, u32[]{:S(2)}, u32[]{:S(2)}) %collective-permute-start.33) | collective-permute-done | bytes 65568 | tf_op jit(solution)/shard_map/ppermute | solution.py:85
  86.0 2.9 %collective-permute-start.20 = (f32[1,4,16,256]{3,2,1,0:T(8,128)}, f32[1,4,16,256]{3,2,1,0:T(8,128)S(1)}, u32[]{:S(2)}, u32[]{:S(2)}) collective-permute-start(f32[1,4,16,256]{3,2,1,0:T(8,128)} %get-tuple-element.102), channel_id=1, source_target_pairs={{0,24},{2,26},{4,28},{6,30},{8,0},{10,2},{12,4},{14,6},{16,8},{18,... | collective-permute-start | bytes 196616 | tf_op jit(solution)/shard_map/ppermute | solution.py:85
  88.9 0.8 copy.10
  89.8 1.3 collective-permute-start.25
  91.7 1.4 collective-permute-start.36
  93.8 1.3 collective-permute-start.9
  95.0 1.4 collective-permute-start.10
  96.4 1.9 collective-permute-start.37
  98.8 4.2 %collective-permute-done.37.refs_7_ = f32[4,1,16,256]{3,2,1,0:T(8,128)S(1)} collective-permute-done((f32[4,1,16,256]{3,2,1,0:T(8,128)S(1)}, f32[4,1,16,256]{3,2,1,0:T(8,128)S(1)}, u32[]{:S(2)}, u32[]{:S(2)}) %collective-permute-start.37) | collective-permute-done | bytes 65568 | tf_op jit(solution)/shard_map/ppermute | solution.py:93
  103.6 2.0 collective-permute-start.23
  106.2 3.8 %collective-permute-start.38 = (f32[16,16,256]{2,1,0:T(8,128)S(1)}, f32[16,16,256]{2,1,0:T(8,128)S(1)}, u32[]{:S(2)}, u32[]{:S(2)}) collective-permute-start(f32[16,16,256]{2,1,0:T(8,128)S(1)} %get-tuple-element.126), channel_id=1, source_target_pairs={{0,1},{1,0},{2,3},{3,2},{4,5},{5,4},{6,7},{7,6},{8,9},{9,8},{10,11... | collective-permute-start | bytes 786440 | tf_op jit(solution)/shard_map/ppermute | solution.py:344
  110.6 2.6 %collective-permute-start.24 = (f32[16,16,256]{2,1,0:T(8,128)S(1)}, f32[16,16,256]{2,1,0:T(8,128)S(1)}, u32[]{:S(2)}, u32[]{:S(2)}) collective-permute-start(f32[16,16,256]{2,1,0:T(8,128)S(1)} %get-tuple-element.108), channel_id=1, source_target_pairs={{0,1},{1,0},{2,3},{3,2},{4,5},{5,4},{6,7},{7,6},{8,9},{9,8},{10,11... | collective-permute-start | bytes 786440 | tf_op jit(solution)/shard_map/ppermute | solution.py:344
  113.3 2.0 shard_map.66
  115.7 2.0 shard_map.62
  117.7 2.4 %collective-permute-start.26 = (f32[2,4,16,256]{3,2,1,0:T(8,128)S(1)}, f32[2,4,16,256]{3,2,1,0:T(8,128)S(1)}, u32[]{:S(2)}, u32[]{:S(2)}) collective-permute-start(f32[2,4,16,256]{3,2,1,0:T(8,128)S(1)} %get-tuple-element.110), channel_id=1, source_target_pairs={{0,8},{2,10},{4,12},{6,14},{8,16},{10,18},{12,20},{14,22},{16,24},... | collective-permute-start | bytes 393224 | tf_op jit(solution)/shard_map/ppermute | solution.py:85
  120.1 0.9 collective-permute-start.27
  121.0 1.3 collective-permute-start.28
  122.5 2.1 %collective-permute-start.41 = (f32[1,4,16,256]{3,2,1,0:T(8,128)S(1)}, f32[1,4,16,256]{3,2,1,0:T(8,128)S(1)}, u32[]{:S(2)}, u32[]{:S(2)}) collective-permute-start(f32[1,4,16,256]{3,2,1,0:T(8,128)S(1)} %get-tuple-element.130), channel_id=1, source_target_pairs={{0,24},{2,26},{4,28},{6,30},{8,0},{10,2},{12,4},{14,6},{16,8},{18,... | collective-permute-start | bytes 196616 | tf_op jit(solution)/shard_map/ppermute | solution.py:85
  124.6 11.7 %collective-permute-done.40.refs_2_ = f32[1,4,16,256]{3,2,1,0:T(8,128)S(1)} collective-permute-done((f32[1,4,16,256]{3,2,1,0:T(8,128)S(1)}, f32[1,4,16,256]{3,2,1,0:T(8,128)S(1)}, u32[]{:S(2)}, u32[]{:S(2)}) %collective-permute-start.40) | collective-permute-done | bytes 65568 | tf_op jit(solution)/shard_map/ppermute | solution.py:85
  136.3 2.5 %collective-permute-start.52 = (f32[1,4,16,256]{3,2,1,0:T(8,128)S(1)}, f32[1,4,16,256]{3,2,1,0:T(8,128)S(1)}, u32[]{:S(2)}, u32[]{:S(2)}) collective-permute-start(f32[1,4,16,256]{3,2,1,0:T(8,128)S(1)} %get-tuple-element.146), channel_id=1, source_target_pairs={{0,16},{2,18},{4,20},{6,22},{8,24},{10,26},{12,28},{14,30},{16,0},... | collective-permute-start | bytes 196616 | tf_op jit(solution)/shard_map/ppermute | solution.py:85
  139.4 1.3 collective-permute-start.53
  140.7 1.9 collective-permute-start.42
  144.0 1.7 collective-permute-start.31
  145.7 1.4 collective-permute-start.43
  147.8 5.3 %collective-permute-done.43.refs_6_ = f32[4,1,16,256]{3,2,1,0:T(8,128)S(1)} collective-permute-done((f32[4,1,16,256]{3,2,1,0:T(8,128)S(1)}, f32[4,1,16,256]{3,2,1,0:T(8,128)S(1)}, u32[]{:S(2)}, u32[]{:S(2)}) %collective-permute-start.43) | collective-permute-done | bytes 65568 | tf_op jit(solution)/shard_map/ppermute | solution.py:93
  153.1 2.3 %collective-permute-start.55 = (f32[4,1,16,256]{3,2,1,0:T(8,128)S(1)}, f32[4,1,16,256]{3,2,1,0:T(8,128)S(1)}, u32[]{:S(2)}, u32[]{:S(2)}) collective-permute-start(f32[4,1,16,256]{3,2,1,0:T(8,128)S(1)} %get-tuple-element.150), channel_id=1, source_target_pairs={{0,4},{2,6},{4,0},{6,2},{8,12},{10,14},{12,8},{14,10},{16,20},{18,... | collective-permute-start | bytes 196616 | tf_op jit(solution)/shard_map/ppermute | solution.py:93
  155.9 0.9 shard_map.68
  158.2 2.3 %collective-permute-start.47 = (f32[2,4,16,256]{3,2,1,0:T(8,128)S(1)}, f32[2,4,16,256]{3,2,1,0:T(8,128)S(1)}, u32[]{:S(2)}, u32[]{:S(2)}) collective-permute-start(f32[2,4,16,256]{3,2,1,0:T(8,128)S(1)} %get-tuple-element.139), channel_id=1, source_target_pairs={{0,24},{2,26},{4,28},{6,30},{8,0},{10,2},{12,4},{14,6},{16,8},{18,... | collective-permute-start | bytes 393224 | tf_op jit(solution)/shard_map/ppermute | solution.py:85
  160.5 0.9 shard_map.71
  161.5 1.0 copy.11
  162.5 1.3 collective-permute-start.64
  163.8 1.1 collective-permute-start.58
  164.9 6.2 %collective-permute-done.46.refs_2_ = f32[2,4,16,256]{3,2,1,0:T(8,128)S(1)} collective-permute-done((f32[2,4,16,256]{3,2,1,0:T(8,128)S(1)}, f32[2,4,16,256]{3,2,1,0:T(8,128)S(1)}, u32[]{:S(2)}, u32[]{:S(2)}) %collective-permute-start.46) | collective-permute-done | bytes 131104 | tf_op jit(solution)/shard_map/ppermute | solution.py:85
  171.7 3.1 %collective-permute-start.49 = (f32[4,2,16,256]{3,2,1,0:T(8,128)S(1)}, f32[4,2,16,256]{3,2,1,0:T(8,128)S(1)}, u32[]{:S(2)}, u32[]{:S(2)}) collective-permute-start(f32[4,2,16,256]{3,2,1,0:T(8,128)S(1)} %get-tuple-element.142), channel_id=1, source_target_pairs={{0,4},{2,6},{4,0},{6,2},{8,12},{10,14},{12,8},{14,10},{16,20},{18,... | collective-permute-start | bytes 393224 | tf_op jit(solution)/shard_map/ppermute | solution.py:93
  174.9 5.5 %collective-permute-done.58.refs_2_ = f32[2,4,16,256]{3,2,1,0:T(8,128)S(1)} collective-permute-done((f32[2,4,16,256]{3,2,1,0:T(8,128)S(1)}, f32[2,4,16,256]{3,2,1,0:T(8,128)S(1)}, u32[]{:S(2)}, u32[]{:S(2)}) %collective-permute-start.58) | collective-permute-done | bytes 131104 | tf_op jit(solution)/shard_map/ppermute | solution.py:85
  182.5 1.9 collective-permute-start.62
  184.5 3.4 %collective-permute-done.60.refs_1_ = f32[4,2,16,256]{3,2,1,0:T(8,128)S(1)} collective-permute-done((f32[4,2,16,256]{3,2,1,0:T(8,128)S(1)}, f32[4,2,16,256]{3,2,1,0:T(8,128)S(1)}, u32[]{:S(2)}, u32[]{:S(2)}) %collective-permute-start.60) | collective-permute-done | bytes 131104 | tf_op jit(solution)/shard_map/ppermute | solution.py:93
  187.9 1.4 collective-permute-done.61.refs_2_
  190.1 6.2 %collective-permute-start.63 = (f32[2,16,16,256]{3,2,1,0:T(8,128)S(1)}, f32[2,16,16,256]{3,2,1,0:T(8,128)S(1)}, u32[]{:S(2)}, u32[]{:S(2)}) collective-permute-start(f32[2,16,16,256]{3,2,1,0:T(8,128)S(1)} %shard_map.75), channel_id=1, source_target_pairs={{0,1},{1,0},{2,3},{3,2},{4,5},{5,4},{6,7},{7,6},{8,9},{9,8},{10,11... | collective-permute-start | bytes 1572872 | tf_op jit(solution)/shard_map/ppermute | solution.py:344
  196.4 3.2 %shard_map.73.refs_6_ = f32[2,1,2,256,256]{4,3,2,1,0:T(8,128)S(1)} custom-call(s32[4]{0:T(128)S(1)} %pad_add_fusion.place, f32[4,2,16,256]{3,2,1,0:T(8,128)S(1)} %get-tuple-element.157.refs_0_, f32[4,2,16,256]{3,2,1,0:T(8,128)S(1)} %collective-permute-done.60.refs_1_, f32[4,2,16,256]{3,2,1,0:T(8,128)S(1)} %collective-permute-done.61.refs_2_, ...), custom_call_target="tpu_custom_call" | custom-call | tf_op jit(solution)/shard_map/pallas_call | solution.py:312
  199.5 3.2 %shard_map.74.refs_0_ = f32[2,1,2,256,256]{4,3,2,1,0:T(8,128)S(1)} custom-call(s32[4]{0:T(128)S(1)} %pad_add_fusion.place, f32[4,2,16,256]{3,2,1,0:T(8,128)S(1)} %get-tuple-element.140.refs_0_.refs_4_, f32[4,2,16,256]{3,2,1,0:T(8,128)S(1)} %collective-permute-done.48.refs_1_.refs_5_, f32[4,2,16,256]{3,2,1,0:T(8,128)S(1)} %collective-permute-done.49.refs_2_.refs_6_, ...), custom_call_target="tpu_custom_call" | custom-call | tf_op jit(solution)/shard_map/pallas_call | solution.py:312
  202.7 3.3 %shard_map.76 = f32[2,1,2,256,256]{4,3,2,1,0:T(8,128)} custom-call(s32[4]{0:T(128)S(1)} %pad_add_fusion.place, f32[2,1,2,256,256]{4,3,2,1,0:T(8,128)S(1)} %shard_map.74.refs_0_, f32[2,16,16,256]{3,2,1,0:T(8,128)S(1)} %collective-permute-done.63.refs_1_, f32[2,256,256]{2,1,0:T(8,128)S(1)} %bitcast_select_fusion.refs_2_), custom_call_target="tpu_custom_call" | custom-call | tf_op jit(solution)/shard_map/pallas_call | solution.py:312
  (108 shorter events, 16.5 us)
Async XLA Ops:
  2.7 10.5 %collective-permute-start.12 = (f32[4,4,16,256]{3,2,1,0:T(8,128)}, f32[4,4,16,256]{3,2,1,0:T(8,128)S(1)}, u32[]{:S(2)}, u32[]{:S(2)}) collective-permute-start(f32[4,4,16,256]{3,2,1,0:T(8,128)} %get-tuple-element.165), channel_id=1, source_target_pairs={{0,8},{2,10},{4,12},{6,14},{8,16},{10,18},{12,20},{14,22},{16,24},... | collective-permute-start | bytes 786440 | tf_op jit(solution)/shard_map/ppermute | solution.py:85
  4.8 21.1 %collective-permute-start.13 = (f32[4,4,16,256]{3,2,1,0:T(8,128)}, f32[4,4,16,256]{3,2,1,0:T(8,128)S(1)}, u32[]{:S(2)}, u32[]{:S(2)}) collective-permute-start(f32[4,4,16,256]{3,2,1,0:T(8,128)} %get-tuple-element.164), channel_id=1, source_target_pairs={{0,16},{2,18},{4,20},{6,22},{8,24},{10,26},{12,28},{14,30},{16,0},... | collective-permute-start | bytes 786440 | tf_op jit(solution)/shard_map/ppermute | solution.py:85
  7.1 18.7 %collective-permute-start.14 = (f32[4,4,16,256]{3,2,1,0:T(8,128)}, f32[4,4,16,256]{3,2,1,0:T(8,128)S(1)}, u32[]{:S(2)}, u32[]{:S(2)}) collective-permute-start(f32[4,4,16,256]{3,2,1,0:T(8,128)} %get-tuple-element.163), channel_id=1, source_target_pairs={{0,24},{2,26},{4,28},{6,30},{8,0},{10,2},{12,4},{14,6},{16,8},{18,... | collective-permute-start | bytes 786440 | tf_op jit(solution)/shard_map/ppermute | solution.py:85
  9.0 21.1 %collective-permute-start = (f32[4,4,16,256]{3,2,1,0:T(8,128)}, f32[4,4,16,256]{3,2,1,0:T(8,128)S(1)}, u32[]{:S(2)}, u32[]{:S(2)}) collective-permute-start(f32[4,4,16,256]{3,2,1,0:T(8,128)} %get-tuple-element.169), channel_id=1, source_target_pairs={{0,8},{2,10},{4,12},{6,14},{8,16},{10,18},{12,20},{14,22},{16,24},... | collective-permute-start | bytes 786440 | tf_op jit(solution)/shard_map/ppermute | solution.py:85
  9.4 38.2 %collective-permute-start.1 = (f32[4,4,16,256]{3,2,1,0:T(8,128)S(1)}, f32[4,4,16,256]{3,2,1,0:T(8,128)S(1)}, u32[]{:S(2)}, u32[]{:S(2)}) collective-permute-start(f32[4,4,16,256]{3,2,1,0:T(8,128)S(1)} %get-tuple-element.168), channel_id=1, source_target_pairs={{0,16},{2,18},{4,20},{6,22},{8,24},{10,26},{12,28},{14,30},{16,0},... | collective-permute-start | bytes 786440 | tf_op jit(solution)/shard_map/ppermute | solution.py:85
  13.2 34.4 %collective-permute-start.2 = (f32[4,4,16,256]{3,2,1,0:T(8,128)S(1)}, f32[4,4,16,256]{3,2,1,0:T(8,128)S(1)}, u32[]{:S(2)}, u32[]{:S(2)}) collective-permute-start(f32[4,4,16,256]{3,2,1,0:T(8,128)S(1)} %get-tuple-element.167), channel_id=1, source_target_pairs={{0,24},{2,26},{4,28},{6,30},{8,0},{10,2},{12,4},{14,6},{16,8},{18,... | collective-permute-start | bytes 786440 | tf_op jit(solution)/shard_map/ppermute | solution.py:85
  26.5 24.2 %collective-permute-start.15 = (f32[4,4,16,256]{3,2,1,0:T(8,128)S(1)}, f32[4,4,16,256]{3,2,1,0:T(8,128)S(1)}, u32[]{:S(2)}, u32[]{:S(2)}) collective-permute-start(f32[4,4,16,256]{3,2,1,0:T(8,128)S(1)} %get-tuple-element.96), channel_id=1, source_target_pairs={{0,2},{2,4},{4,6},{6,0},{8,10},{10,12},{12,14},{14,8},{16,18},{18,... | collective-permute-start | bytes 786440 | tf_op jit(solution)/shard_map/ppermute | solution.py:93
  28.0 23.9 %collective-permute-start.16 = (f32[4,4,16,256]{3,2,1,0:T(8,128)S(1)}, f32[4,4,16,256]{3,2,1,0:T(8,128)S(1)}, u32[]{:S(2)}, u32[]{:S(2)}) collective-permute-start(f32[4,4,16,256]{3,2,1,0:T(8,128)S(1)} %get-tuple-element.97), channel_id=1, source_target_pairs={{0,4},{2,6},{4,0},{6,2},{8,12},{10,14},{12,8},{14,10},{16,20},{18,... | collective-permute-start | bytes 786440 | tf_op jit(solution)/shard_map/ppermute | solution.py:93
  30.1 21.8 %collective-permute-start.17 = (f32[4,4,16,256]{3,2,1,0:T(8,128)S(1)}, f32[4,4,16,256]{3,2,1,0:T(8,128)S(1)}, u32[]{:S(2)}, u32[]{:S(2)}) collective-permute-start(f32[4,4,16,256]{3,2,1,0:T(8,128)S(1)} %get-tuple-element.98), channel_id=1, source_target_pairs={{0,6},{2,0},{4,2},{6,4},{8,14},{10,8},{12,10},{14,12},{16,22},{18,... | collective-permute-start | bytes 786440 | tf_op jit(solution)/shard_map/ppermute | solution.py:93
  48.3 11.2 %collective-permute-start.3 = (f32[4,4,16,256]{3,2,1,0:T(8,128)S(1)}, f32[4,4,16,256]{3,2,1,0:T(8,128)S(1)}, u32[]{:S(2)}, u32[]{:S(2)}) collective-permute-start(f32[4,4,16,256]{3,2,1,0:T(8,128)S(1)} %get-tuple-element.84), channel_id=1, source_target_pairs={{0,2},{2,4},{4,6},{6,0},{8,10},{10,12},{12,14},{14,8},{16,18},{18,... | collective-permute-start | bytes 786440 | tf_op jit(solution)/shard_map/ppermute | solution.py:93
  49.5 13.5 %collective-permute-start.4 = (f32[4,4,16,256]{3,2,1,0:T(8,128)S(1)}, f32[4,4,16,256]{3,2,1,0:T(8,128)S(1)}, u32[]{:S(2)}, u32[]{:S(2)}) collective-permute-start(f32[4,4,16,256]{3,2,1,0:T(8,128)S(1)} %get-tuple-element.85), channel_id=1, source_target_pairs={{0,4},{2,6},{4,0},{6,2},{8,12},{10,14},{12,8},{14,10},{16,20},{18,... | collective-permute-start | bytes 786440 | tf_op jit(solution)/shard_map/ppermute | solution.py:93
  50.8 12.3 %collective-permute-start.5 = (f32[4,4,16,256]{3,2,1,0:T(8,128)S(1)}, f32[4,4,16,256]{3,2,1,0:T(8,128)S(1)}, u32[]{:S(2)}, u32[]{:S(2)}) collective-permute-start(f32[4,4,16,256]{3,2,1,0:T(8,128)S(1)} %get-tuple-element.86), channel_id=1, source_target_pairs={{0,6},{2,0},{4,2},{6,4},{8,14},{10,8},{12,10},{14,12},{16,22},{18,... | collective-permute-start | bytes 786440 | tf_op jit(solution)/shard_map/ppermute | solution.py:93
  53.5 19.2 %collective-permute-start.18 = (f32[1,4,16,256]{3,2,1,0:T(8,128)S(1)}, f32[1,4,16,256]{3,2,1,0:T(8,128)S(1)}, u32[]{:S(2)}, u32[]{:S(2)}) collective-permute-start(f32[1,4,16,256]{3,2,1,0:T(8,128)S(1)} %get-tuple-element.100), channel_id=1, source_target_pairs={{0,8},{2,10},{4,12},{6,14},{8,16},{10,18},{12,20},{14,22},{16,24},... | collective-permute-start | bytes 196616 | tf_op jit(solution)/shard_map/ppermute | solution.py:85
  59.4 13.6 %collective-permute-start.32 = (f32[1,4,16,256]{3,2,1,0:T(8,128)S(1)}, f32[1,4,16,256]{3,2,1,0:T(8,128)S(1)}, u32[]{:S(2)}, u32[]{:S(2)}) collective-permute-start(f32[1,4,16,256]{3,2,1,0:T(8,128)S(1)} %get-tuple-element.118), channel_id=1, source_target_pairs={{0,8},{2,10},{4,12},{6,14},{8,16},{10,18},{12,20},{14,22},{16,24},... | collective-permute-start | bytes 196616 | tf_op jit(solution)/shard_map/ppermute | solution.py:85
  64.7 25.1 %collective-permute-start.6 = (f32[2,4,16,256]{3,2,1,0:T(8,128)}, f32[2,4,16,256]{3,2,1,0:T(8,128)S(1)}, u32[]{:S(2)}, u32[]{:S(2)}) collective-permute-start(f32[2,4,16,256]{3,2,1,0:T(8,128)} %get-tuple-element.88), channel_id=1, source_target_pairs={{0,8},{2,10},{4,12},{6,14},{8,16},{10,18},{12,20},{14,22},{16,24},... | collective-permute-start | bytes 393224 | tf_op jit(solution)/shard_map/ppermute | solution.py:85
  70.7 21.0 %collective-permute-start.7 = (f32[2,4,16,256]{3,2,1,0:T(8,128)}, f32[2,4,16,256]{3,2,1,0:T(8,128)S(1)}, u32[]{:S(2)}, u32[]{:S(2)}) collective-permute-start(f32[2,4,16,256]{3,2,1,0:T(8,128)} %get-tuple-element.89), channel_id=1, source_target_pairs={{0,16},{2,18},{4,20},{6,22},{8,24},{10,26},{12,28},{14,30},{16,0},... | collective-permute-start | bytes 393224 | tf_op jit(solution)/shard_map/ppermute | solution.py:85
  70.9 20.9 %collective-permute-start.8 = (f32[2,4,16,256]{3,2,1,0:T(8,128)S(1)}, f32[2,4,16,256]{3,2,1,0:T(8,128)S(1)}, u32[]{:S(2)}, u32[]{:S(2)}) collective-permute-start(f32[2,4,16,256]{3,2,1,0:T(8,128)S(1)} %get-tuple-element.90), channel_id=1, source_target_pairs={{0,24},{2,26},{4,28},{6,30},{8,0},{10,2},{12,4},{14,6},{16,8},{18,... | collective-permute-start | bytes 393224 | tf_op jit(solution)/shard_map/ppermute | solution.py:85
  72.8 13.3 %collective-permute-start.33 = (f32[1,4,16,256]{3,2,1,0:T(8,128)S(1)}, f32[1,4,16,256]{3,2,1,0:T(8,128)S(1)}, u32[]{:S(2)}, u32[]{:S(2)}) collective-permute-start(f32[1,4,16,256]{3,2,1,0:T(8,128)S(1)} %get-tuple-element.119), channel_id=1, source_target_pairs={{0,16},{2,18},{4,20},{6,22},{8,24},{10,26},{12,28},{14,30},{16,0},... | collective-permute-start | bytes 196616 | tf_op jit(solution)/shard_map/ppermute | solution.py:85
  73.0 13.0 %collective-permute-start.34 = (f32[1,4,16,256]{3,2,1,0:T(8,128)S(1)}, f32[1,4,16,256]{3,2,1,0:T(8,128)S(1)}, u32[]{:S(2)}, u32[]{:S(2)}) collective-permute-start(f32[1,4,16,256]{3,2,1,0:T(8,128)S(1)} %get-tuple-element.120), channel_id=1, source_target_pairs={{0,24},{2,26},{4,28},{6,30},{8,0},{10,2},{12,4},{14,6},{16,8},{18,... | collective-permute-start | bytes 196616 | tf_op jit(solution)/shard_map/ppermute | solution.py:85
  86.0 7.7 %collective-permute-start.19 = (f32[1,4,16,256]{3,2,1,0:T(8,128)}, f32[1,4,16,256]{3,2,1,0:T(8,128)S(1)}, u32[]{:S(2)}, u32[]{:S(2)}) collective-permute-start(f32[1,4,16,256]{3,2,1,0:T(8,128)} %get-tuple-element.101), channel_id=1, source_target_pairs={{0,16},{2,18},{4,20},{6,22},{8,24},{10,26},{12,28},{14,30},{16,0},... | collective-permute-start | bytes 196616 | tf_op jit(solution)/shard_map/ppermute | solution.py:85
  86.0 9.0 %collective-permute-start.20 = (f32[1,4,16,256]{3,2,1,0:T(8,128)}, f32[1,4,16,256]{3,2,1,0:T(8,128)S(1)}, u32[]{:S(2)}, u32[]{:S(2)}) collective-permute-start(f32[1,4,16,256]{3,2,1,0:T(8,128)} %get-tuple-element.102), channel_id=1, source_target_pairs={{0,24},{2,26},{4,28},{6,30},{8,0},{10,2},{12,4},{14,6},{16,8},{18,... | collective-permute-start | bytes 196616 | tf_op jit(solution)/shard_map/ppermute | solution.py:85
  89.8 23.5 %collective-permute-start.25 = (f32[256,256]{0,1:T(8,128)}, f32[256,256]{0,1:T(8,128)S(1)}, u32[]{:S(2)}, u32[]{:S(2)}) collective-permute-start(f32[256,256]{0,1:T(8,128)} %bitcast.18), channel_id=1, source_target_pairs={{0,1},{2,3},{4,5},{6,7},{8,9},{10,11},{12,13},{14,15},{16,17},{18,... | collective-permute-start | bytes 786440 | tf_op jit(solution)/shard_map/ppermute | solution.py:329
  91.7 4.7 %collective-permute-start.35 = (f32[4,1,16,256]{3,2,1,0:T(8,128)S(1)}, f32[4,1,16,256]{3,2,1,0:T(8,128)S(1)}, u32[]{:S(2)}, u32[]{:S(2)}) collective-permute-start(f32[4,1,16,256]{3,2,1,0:T(8,128)S(1)} %get-tuple-element.122), channel_id=1, source_target_pairs={{0,2},{2,4},{4,6},{6,0},{8,10},{10,12},{12,14},{14,8},{16,18},{18,... | collective-permute-start | bytes 196616 | tf_op jit(solution)/shard_map/ppermute | solution.py:93
  91.7 4.7 %collective-permute-start.36 = (f32[4,1,16,256]{3,2,1,0:T(8,128)S(1)}, f32[4,1,16,256]{3,2,1,0:T(8,128)S(1)}, u32[]{:S(2)}, u32[]{:S(2)}) collective-permute-start(f32[4,1,16,256]{3,2,1,0:T(8,128)S(1)} %get-tuple-element.123), channel_id=1, source_target_pairs={{0,4},{2,6},{4,0},{6,2},{8,12},{10,14},{12,8},{14,10},{16,20},{18,... | collective-permute-start | bytes 196616 | tf_op jit(solution)/shard_map/ppermute | solution.py:93
  93.8 9.4 %collective-permute-start.9 = (f32[4,2,16,256]{3,2,1,0:T(8,128)S(1)}, f32[4,2,16,256]{3,2,1,0:T(8,128)S(1)}, u32[]{:S(2)}, u32[]{:S(2)}) collective-permute-start(f32[4,2,16,256]{3,2,1,0:T(8,128)S(1)} %get-tuple-element.92), channel_id=1, source_target_pairs={{0,2},{2,4},{4,6},{6,0},{8,10},{10,12},{12,14},{14,8},{16,18},{18,... | collective-permute-start | bytes 393224 | tf_op jit(solution)/shard_map/ppermute | solution.py:93
  95.0 8.6 %collective-permute-start.10 = (f32[4,2,16,256]{3,2,1,0:T(8,128)S(1)}, f32[4,2,16,256]{3,2,1,0:T(8,128)S(1)}, u32[]{:S(2)}, u32[]{:S(2)}) collective-permute-start(f32[4,2,16,256]{3,2,1,0:T(8,128)S(1)} %get-tuple-element.93), channel_id=1, source_target_pairs={{0,4},{2,6},{4,0},{6,2},{8,12},{10,14},{12,8},{14,10},{16,20},{18,... | collective-permute-start | bytes 393224 | tf_op jit(solution)/shard_map/ppermute | solution.py:93
  96.4 9.3 %collective-permute-start.11 = (f32[4,2,16,256]{3,2,1,0:T(8,128)S(1)}, f32[4,2,16,256]{3,2,1,0:T(8,128)S(1)}, u32[]{:S(2)}, u32[]{:S(2)}) collective-permute-start(f32[4,2,16,256]{3,2,1,0:T(8,128)S(1)} %get-tuple-element.94), channel_id=1, source_target_pairs={{0,6},{2,0},{4,2},{6,4},{8,14},{10,8},{12,10},{14,12},{16,22},{18,... | collective-permute-start | bytes 393224 | tf_op jit(solution)/shard_map/ppermute | solution.py:93
  96.4 6.7 %collective-permute-start.37 = (f32[4,1,16,256]{3,2,1,0:T(8,128)S(1)}, f32[4,1,16,256]{3,2,1,0:T(8,128)S(1)}, u32[]{:S(2)}, u32[]{:S(2)}) collective-permute-start(f32[4,1,16,256]{3,2,1,0:T(8,128)S(1)} %get-tuple-element.124), channel_id=1, source_target_pairs={{0,6},{2,0},{4,2},{6,4},{8,14},{10,8},{12,10},{14,12},{16,22},{18,... | collective-permute-start | bytes 196616 | tf_op jit(solution)/shard_map/ppermute | solution.py:93
  103.1 6.9 %collective-permute-start.21 = (f32[4,1,16,256]{3,2,1,0:T(8,128)S(1)}, f32[4,1,16,256]{3,2,1,0:T(8,128)S(1)}, u32[]{:S(2)}, u32[]{:S(2)}) collective-permute-start(f32[4,1,16,256]{3,2,1,0:T(8,128)S(1)} %get-tuple-element.104), channel_id=1, source_target_pairs={{0,2},{2,4},{4,6},{6,0},{8,10},{10,12},{12,14},{14,8},{16,18},{18,... | collective-permute-start | bytes 196616 | tf_op jit(solution)/shard_map/ppermute | solution.py:93
  103.1 6.9 %collective-permute-start.22 = (f32[4,1,16,256]{3,2,1,0:T(8,128)S(1)}, f32[4,1,16,256]{3,2,1,0:T(8,128)S(1)}, u32[]{:S(2)}, u32[]{:S(2)}) collective-permute-start(f32[4,1,16,256]{3,2,1,0:T(8,128)S(1)} %get-tuple-element.105), channel_id=1, source_target_pairs={{0,4},{2,6},{4,0},{6,2},{8,12},{10,14},{12,8},{14,10},{16,20},{18,... | collective-permute-start | bytes 196616 | tf_op jit(solution)/shard_map/ppermute | solution.py:93
  103.6 6.4 %collective-permute-start.23 = (f32[4,1,16,256]{3,2,1,0:T(8,128)S(1)}, f32[4,1,16,256]{3,2,1,0:T(8,128)S(1)}, u32[]{:S(2)}, u32[]{:S(2)}) collective-permute-start(f32[4,1,16,256]{3,2,1,0:T(8,128)S(1)} %get-tuple-element.106), channel_id=1, source_target_pairs={{0,6},{2,0},{4,2},{6,4},{8,14},{10,8},{12,10},{14,12},{16,22},{18,... | collective-permute-start | bytes 196616 | tf_op jit(solution)/shard_map/ppermute | solution.py:93
  106.2 7.0 %collective-permute-start.38 = (f32[16,16,256]{2,1,0:T(8,128)S(1)}, f32[16,16,256]{2,1,0:T(8,128)S(1)}, u32[]{:S(2)}, u32[]{:S(2)}) collective-permute-start(f32[16,16,256]{2,1,0:T(8,128)S(1)} %get-tuple-element.126), channel_id=1, source_target_pairs={{0,1},{1,0},{2,3},{3,2},{4,5},{5,4},{6,7},{7,6},{8,9},{9,8},{10,11... | collective-permute-start | bytes 786440 | tf_op jit(solution)/shard_map/ppermute | solution.py:344
  110.6 5.1 %collective-permute-start.24 = (f32[16,16,256]{2,1,0:T(8,128)S(1)}, f32[16,16,256]{2,1,0:T(8,128)S(1)}, u32[]{:S(2)}, u32[]{:S(2)}) collective-permute-start(f32[16,16,256]{2,1,0:T(8,128)S(1)} %get-tuple-element.108), channel_id=1, source_target_pairs={{0,1},{1,0},{2,3},{3,2},{4,5},{5,4},{6,7},{7,6},{8,9},{9,8},{10,11... | collective-permute-start | bytes 786440 | tf_op jit(solution)/shard_map/ppermute | solution.py:344
  115.3 7.2 %collective-permute-start.39 = (f32[1,4,16,256]{3,2,1,0:T(8,128)S(1)}, f32[1,4,16,256]{3,2,1,0:T(8,128)S(1)}, u32[]{:S(2)}, u32[]{:S(2)}) collective-permute-start(f32[1,4,16,256]{3,2,1,0:T(8,128)S(1)} %get-tuple-element.128), channel_id=1, source_target_pairs={{0,8},{2,10},{4,12},{6,14},{8,16},{10,18},{12,20},{14,22},{16,24},... | collective-permute-start | bytes 196616 | tf_op jit(solution)/shard_map/ppermute | solution.py:85
  117.7 21.7 %collective-permute-start.26 = (f32[2,4,16,256]{3,2,1,0:T(8,128)S(1)}, f32[2,4,16,256]{3,2,1,0:T(8,128)S(1)}, u32[]{:S(2)}, u32[]{:S(2)}) collective-permute-start(f32[2,4,16,256]{3,2,1,0:T(8,128)S(1)} %get-tuple-element.110), channel_id=1, source_target_pairs={{0,8},{2,10},{4,12},{6,14},{8,16},{10,18},{12,20},{14,22},{16,24},... | collective-permute-start | bytes 393224 | tf_op jit(solution)/shard_map/ppermute | solution.py:85
  120.1 20.6 %collective-permute-start.27 = (f32[2,4,16,256]{3,2,1,0:T(8,128)S(1)}, f32[2,4,16,256]{3,2,1,0:T(8,128)S(1)}, u32[]{:S(2)}, u32[]{:S(2)}) collective-permute-start(f32[2,4,16,256]{3,2,1,0:T(8,128)S(1)} %get-tuple-element.111), channel_id=1, source_target_pairs={{0,16},{2,18},{4,20},{6,22},{8,24},{10,26},{12,28},{14,30},{16,0},... | collective-permute-start | bytes 393224 | tf_op jit(solution)/shard_map/ppermute | solution.py:85
  121.0 21.6 %collective-permute-start.28 = (f32[2,4,16,256]{3,2,1,0:T(8,128)S(1)}, f32[2,4,16,256]{3,2,1,0:T(8,128)S(1)}, u32[]{:S(2)}, u32[]{:S(2)}) collective-permute-start(f32[2,4,16,256]{3,2,1,0:T(8,128)S(1)} %get-tuple-element.112), channel_id=1, source_target_pairs={{0,24},{2,26},{4,28},{6,30},{8,0},{10,2},{12,4},{14,6},{16,8},{18,... | collective-permute-start | bytes 393224 | tf_op jit(solution)/shard_map/ppermute | solution.py:85
  122.3 14.0 %collective-permute-start.40 = (f32[1,4,16,256]{3,2,1,0:T(8,128)S(1)}, f32[1,4,16,256]{3,2,1,0:T(8,128)S(1)}, u32[]{:S(2)}, u32[]{:S(2)}) collective-permute-start(f32[1,4,16,256]{3,2,1,0:T(8,128)S(1)} %get-tuple-element.129), channel_id=1, source_target_pairs={{0,16},{2,18},{4,20},{6,22},{8,24},{10,26},{12,28},{14,30},{16,0},... | collective-permute-start | bytes 196616 | tf_op jit(solution)/shard_map/ppermute | solution.py:85
  122.5 13.8 %collective-permute-start.41 = (f32[1,4,16,256]{3,2,1,0:T(8,128)S(1)}, f32[1,4,16,256]{3,2,1,0:T(8,128)S(1)}, u32[]{:S(2)}, u32[]{:S(2)}) collective-permute-start(f32[1,4,16,256]{3,2,1,0:T(8,128)S(1)} %get-tuple-element.130), channel_id=1, source_target_pairs={{0,24},{2,26},{4,28},{6,30},{8,0},{10,2},{12,4},{14,6},{16,8},{18,... | collective-permute-start | bytes 196616 | tf_op jit(solution)/shard_map/ppermute | solution.py:85
  136.3 7.0 %collective-permute-start.51 = (f32[1,4,16,256]{3,2,1,0:T(8,128)S(1)}, f32[1,4,16,256]{3,2,1,0:T(8,128)S(1)}, u32[]{:S(2)}, u32[]{:S(2)}) collective-permute-start(f32[1,4,16,256]{3,2,1,0:T(8,128)S(1)} %get-tuple-element.145), channel_id=1, source_target_pairs={{0,8},{2,10},{4,12},{6,14},{8,16},{10,18},{12,20},{14,22},{16,24},... | collective-permute-start | bytes 196616 | tf_op jit(solution)/shard_map/ppermute | solution.py:85
  136.3 7.7 %collective-permute-start.52 = (f32[1,4,16,256]{3,2,1,0:T(8,128)S(1)}, f32[1,4,16,256]{3,2,1,0:T(8,128)S(1)}, u32[]{:S(2)}, u32[]{:S(2)}) collective-permute-start(f32[1,4,16,256]{3,2,1,0:T(8,128)S(1)} %get-tuple-element.146), channel_id=1, source_target_pairs={{0,16},{2,18},{4,20},{6,22},{8,24},{10,26},{12,28},{14,30},{16,0},... | collective-permute-start | bytes 196616 | tf_op jit(solution)/shard_map/ppermute | solution.py:85
  139.4 6.3 %collective-permute-start.53 = (f32[1,4,16,256]{3,2,1,0:T(8,128)S(1)}, f32[1,4,16,256]{3,2,1,0:T(8,128)S(1)}, u32[]{:S(2)}, u32[]{:S(2)}) collective-permute-start(f32[1,4,16,256]{3,2,1,0:T(8,128)S(1)} %get-tuple-element.147), channel_id=1, source_target_pairs={{0,24},{2,26},{4,28},{6,30},{8,0},{10,2},{12,4},{14,6},{16,8},{18,... | collective-permute-start | bytes 196616 | tf_op jit(solution)/shard_map/ppermute | solution.py:85
  140.7 6.4 %collective-permute-start.42 = (f32[4,1,16,256]{3,2,1,0:T(8,128)S(1)}, f32[4,1,16,256]{3,2,1,0:T(8,128)S(1)}, u32[]{:S(2)}, u32[]{:S(2)}) collective-permute-start(f32[4,1,16,256]{3,2,1,0:T(8,128)S(1)} %get-tuple-element.132), channel_id=1, source_target_pairs={{0,2},{2,4},{4,6},{6,0},{8,10},{10,12},{12,14},{14,8},{16,18},{18,... | collective-permute-start | bytes 196616 | tf_op jit(solution)/shard_map/ppermute | solution.py:93
  143.2 12.2 %collective-permute-start.29 = (f32[4,2,16,256]{3,2,1,0:T(8,128)S(1)}, f32[4,2,16,256]{3,2,1,0:T(8,128)S(1)}, u32[]{:S(2)}, u32[]{:S(2)}) collective-permute-start(f32[4,2,16,256]{3,2,1,0:T(8,128)S(1)} %get-tuple-element.114), channel_id=1, source_target_pairs={{0,2},{2,4},{4,6},{6,0},{8,10},{10,12},{12,14},{14,8},{16,18},{18,... | collective-permute-start | bytes 393224 | tf_op jit(solution)/shard_map/ppermute | solution.py:93
  143.3 12.6 %collective-permute-start.30 = (f32[4,2,16,256]{3,2,1,0:T(8,128)S(1)}, f32[4,2,16,256]{3,2,1,0:T(8,128)S(1)}, u32[]{:S(2)}, u32[]{:S(2)}) collective-permute-start(f32[4,2,16,256]{3,2,1,0:T(8,128)S(1)} %get-tuple-element.115), channel_id=1, source_target_pairs={{0,4},{2,6},{4,0},{6,2},{8,12},{10,14},{12,8},{14,10},{16,20},{18,... | collective-permute-start | bytes 393224 | tf_op jit(solution)/shard_map/ppermute | solution.py:93
  144.0 11.9 %collective-permute-start.31 = (f32[4,2,16,256]{3,2,1,0:T(8,128)S(1)}, f32[4,2,16,256]{3,2,1,0:T(8,128)S(1)}, u32[]{:S(2)}, u32[]{:S(2)}) collective-permute-start(f32[4,2,16,256]{3,2,1,0:T(8,128)S(1)} %get-tuple-element.116), channel_id=1, source_target_pairs={{0,6},{2,0},{4,2},{6,4},{8,14},{10,8},{12,10},{14,12},{16,22},{18,... | collective-permute-start | bytes 393224 | tf_op jit(solution)/shard_map/ppermute | solution.py:93
  145.7 7.4 %collective-permute-start.43 = (f32[4,1,16,256]{3,2,1,0:T(8,128)S(1)}, f32[4,1,16,256]{3,2,1,0:T(8,128)S(1)}, u32[]{:S(2)}, u32[]{:S(2)}) collective-permute-start(f32[4,1,16,256]{3,2,1,0:T(8,128)S(1)} %get-tuple-element.133), channel_id=1, source_target_pairs={{0,4},{2,6},{4,0},{6,2},{8,12},{10,14},{12,8},{14,10},{16,20},{18,... | collective-permute-start | bytes 196616 | tf_op jit(solution)/shard_map/ppermute | solution.py:93
  147.1 6.0 %collective-permute-start.44 = (f32[4,1,16,256]{3,2,1,0:T(8,128)S(1)}, f32[4,1,16,256]{3,2,1,0:T(8,128)S(1)}, u32[]{:S(2)}, u32[]{:S(2)}) collective-permute-start(f32[4,1,16,256]{3,2,1,0:T(8,128)S(1)} %get-tuple-element.134), channel_id=1, source_target_pairs={{0,6},{2,0},{4,2},{6,4},{8,14},{10,8},{12,10},{14,12},{16,22},{18,... | collective-permute-start | bytes 196616 | tf_op jit(solution)/shard_map/ppermute | solution.py:93
  153.1 5.2 %collective-permute-start.54 = (f32[4,1,16,256]{3,2,1,0:T(8,128)S(1)}, f32[4,1,16,256]{3,2,1,0:T(8,128)S(1)}, u32[]{:S(2)}, u32[]{:S(2)}) collective-permute-start(f32[4,1,16,256]{3,2,1,0:T(8,128)S(1)} %get-tuple-element.149), channel_id=1, source_target_pairs={{0,2},{2,4},{4,6},{6,0},{8,10},{10,12},{12,14},{14,8},{16,18},{18,... | collective-permute-start | bytes 196616 | tf_op jit(solution)/shard_map/ppermute | solution.py:93
  153.1 7.4 %collective-permute-start.55 = (f32[4,1,16,256]{3,2,1,0:T(8,128)S(1)}, f32[4,1,16,256]{3,2,1,0:T(8,128)S(1)}, u32[]{:S(2)}, u32[]{:S(2)}) collective-permute-start(f32[4,1,16,256]{3,2,1,0:T(8,128)S(1)} %get-tuple-element.150), channel_id=1, source_target_pairs={{0,4},{2,6},{4,0},{6,2},{8,12},{10,14},{12,8},{14,10},{16,20},{18,... | collective-permute-start | bytes 196616 | tf_op jit(solution)/shard_map/ppermute | solution.py:93
  155.5 5.1 %collective-permute-start.56 = (f32[4,1,16,256]{3,2,1,0:T(8,128)S(1)}, f32[4,1,16,256]{3,2,1,0:T(8,128)S(1)}, u32[]{:S(2)}, u32[]{:S(2)}) collective-permute-start(f32[4,1,16,256]{3,2,1,0:T(8,128)S(1)} %get-tuple-element.151), channel_id=1, source_target_pairs={{0,6},{2,0},{4,2},{6,4},{8,14},{10,8},{12,10},{14,12},{16,22},{18,... | collective-permute-start | bytes 196616 | tf_op jit(solution)/shard_map/ppermute | solution.py:93
  156.8 7.0 %collective-permute-start.45 = (f32[2,4,16,256]{3,2,1,0:T(8,128)S(1)}, f32[2,4,16,256]{3,2,1,0:T(8,128)S(1)}, u32[]{:S(2)}, u32[]{:S(2)}) collective-permute-start(f32[2,4,16,256]{3,2,1,0:T(8,128)S(1)} %get-tuple-element.137), channel_id=1, source_target_pairs={{0,8},{2,10},{4,12},{6,14},{8,16},{10,18},{12,20},{14,22},{16,24},... | collective-permute-start | bytes 393224 | tf_op jit(solution)/shard_map/ppermute | solution.py:85
  157.5 13.6 %collective-permute-start.46 = (f32[2,4,16,256]{3,2,1,0:T(8,128)S(1)}, f32[2,4,16,256]{3,2,1,0:T(8,128)S(1)}, u32[]{:S(2)}, u32[]{:S(2)}) collective-permute-start(f32[2,4,16,256]{3,2,1,0:T(8,128)S(1)} %get-tuple-element.138), channel_id=1, source_target_pairs={{0,16},{2,18},{4,20},{6,22},{8,24},{10,26},{12,28},{14,30},{16,0},... | collective-permute-start | bytes 393224 | tf_op jit(solution)/shard_map/ppermute | solution.py:85
  158.2 12.8 %collective-permute-start.47 = (f32[2,4,16,256]{3,2,1,0:T(8,128)S(1)}, f32[2,4,16,256]{3,2,1,0:T(8,128)S(1)}, u32[]{:S(2)}, u32[]{:S(2)}) collective-permute-start(f32[2,4,16,256]{3,2,1,0:T(8,128)S(1)} %get-tuple-element.139), channel_id=1, source_target_pairs={{0,24},{2,26},{4,28},{6,30},{8,0},{10,2},{12,4},{14,6},{16,8},{18,... | collective-permute-start | bytes 393224 | tf_op jit(solution)/shard_map/ppermute | solution.py:85
  161.4 10.3 %collective-permute-start.57 = (f32[2,4,16,256]{3,2,1,0:T(8,128)S(1)}, f32[2,4,16,256]{3,2,1,0:T(8,128)S(1)}, u32[]{:S(2)}, u32[]{:S(2)}) collective-permute-start(f32[2,4,16,256]{3,2,1,0:T(8,128)S(1)} %get-tuple-element.154), channel_id=1, source_target_pairs={{0,8},{2,10},{4,12},{6,14},{8,16},{10,18},{12,20},{14,22},{16,24},... | collective-permute-start | bytes 393224 | tf_op jit(solution)/shard_map/ppermute | solution.py:85
  162.5 33.8 %collective-permute-start.64 = (f32[2,256,256]{1,2,0:T(8,128)}, f32[2,256,256]{1,2,0:T(8,128)S(1)}, u32[]{:S(2)}, u32[]{:S(2)}) collective-permute-start(f32[2,256,256]{1,2,0:T(8,128)} %bitcast.17), channel_id=1, source_target_pairs={{0,1},{2,3},{4,5},{6,7},{8,9},{10,11},{12,13},{14,15},{16,17},{18,... | collective-permute-start | bytes 1572872 | tf_op jit(solution)/shard_map/ppermute | solution.py:329
  163.8 16.6 %collective-permute-start.58 = (f32[2,4,16,256]{3,2,1,0:T(8,128)S(1)}, f32[2,4,16,256]{3,2,1,0:T(8,128)S(1)}, u32[]{:S(2)}, u32[]{:S(2)}) collective-permute-start(f32[2,4,16,256]{3,2,1,0:T(8,128)S(1)} %get-tuple-element.155), channel_id=1, source_target_pairs={{0,16},{2,18},{4,20},{6,22},{8,24},{10,26},{12,28},{14,30},{16,0},... | collective-permute-start | bytes 393224 | tf_op jit(solution)/shard_map/ppermute | solution.py:85
  171.1 10.1 %collective-permute-start.59 = (f32[2,4,16,256]{3,2,1,0:T(8,128)S(1)}, f32[2,4,16,256]{3,2,1,0:T(8,128)S(1)}, u32[]{:S(2)}, u32[]{:S(2)}) collective-permute-start(f32[2,4,16,256]{3,2,1,0:T(8,128)S(1)} %get-tuple-element.156), channel_id=1, source_target_pairs={{0,24},{2,26},{4,28},{6,30},{8,0},{10,2},{12,4},{14,6},{16,8},{18,... | collective-permute-start | bytes 393224 | tf_op jit(solution)/shard_map/ppermute | solution.py:85
  171.7 10.9 %collective-permute-start.48 = (f32[4,2,16,256]{3,2,1,0:T(8,128)S(1)}, f32[4,2,16,256]{3,2,1,0:T(8,128)S(1)}, u32[]{:S(2)}, u32[]{:S(2)}) collective-permute-start(f32[4,2,16,256]{3,2,1,0:T(8,128)S(1)} %get-tuple-element.141), channel_id=1, source_target_pairs={{0,2},{2,4},{4,6},{6,0},{8,10},{10,12},{12,14},{14,8},{16,18},{18,... | collective-permute-start | bytes 393224 | tf_op jit(solution)/shard_map/ppermute | solution.py:93
  171.7 10.8 %collective-permute-start.49 = (f32[4,2,16,256]{3,2,1,0:T(8,128)S(1)}, f32[4,2,16,256]{3,2,1,0:T(8,128)S(1)}, u32[]{:S(2)}, u32[]{:S(2)}) collective-permute-start(f32[4,2,16,256]{3,2,1,0:T(8,128)S(1)} %get-tuple-element.142), channel_id=1, source_target_pairs={{0,4},{2,6},{4,0},{6,2},{8,12},{10,14},{12,8},{14,10},{16,20},{18,... | collective-permute-start | bytes 393224 | tf_op jit(solution)/shard_map/ppermute | solution.py:93
  181.7 6.2 %collective-permute-start.60 = (f32[4,2,16,256]{3,2,1,0:T(8,128)S(1)}, f32[4,2,16,256]{3,2,1,0:T(8,128)S(1)}, u32[]{:S(2)}, u32[]{:S(2)}) collective-permute-start(f32[4,2,16,256]{3,2,1,0:T(8,128)S(1)} %get-tuple-element.158), channel_id=1, source_target_pairs={{0,2},{2,4},{4,6},{6,0},{8,10},{10,12},{12,14},{14,8},{16,18},{18,... | collective-permute-start | bytes 393224 | tf_op jit(solution)/shard_map/ppermute | solution.py:93
  182.5 6.8 %collective-permute-start.61 = (f32[4,2,16,256]{3,2,1,0:T(8,128)S(1)}, f32[4,2,16,256]{3,2,1,0:T(8,128)S(1)}, u32[]{:S(2)}, u32[]{:S(2)}) collective-permute-start(f32[4,2,16,256]{3,2,1,0:T(8,128)S(1)} %get-tuple-element.159), channel_id=1, source_target_pairs={{0,4},{2,6},{4,0},{6,2},{8,12},{10,14},{12,8},{14,10},{16,20},{18,... | collective-permute-start | bytes 393224 | tf_op jit(solution)/shard_map/ppermute | solution.py:93
  182.5 6.8 %collective-permute-start.62 = (f32[4,2,16,256]{3,2,1,0:T(8,128)S(1)}, f32[4,2,16,256]{3,2,1,0:T(8,128)S(1)}, u32[]{:S(2)}, u32[]{:S(2)}) collective-permute-start(f32[4,2,16,256]{3,2,1,0:T(8,128)S(1)} %get-tuple-element.160), channel_id=1, source_target_pairs={{0,6},{2,0},{4,2},{6,4},{8,14},{10,8},{12,10},{14,12},{16,22},{18,... | collective-permute-start | bytes 393224 | tf_op jit(solution)/shard_map/ppermute | solution.py:93
  190.1 12.6 %collective-permute-start.63 = (f32[2,16,16,256]{3,2,1,0:T(8,128)S(1)}, f32[2,16,16,256]{3,2,1,0:T(8,128)S(1)}, u32[]{:S(2)}, u32[]{:S(2)}) collective-permute-start(f32[2,16,16,256]{3,2,1,0:T(8,128)S(1)} %shard_map.75), channel_id=1, source_target_pairs={{0,1},{1,0},{2,3},{3,2},{4,5},{5,4},{6,7},{7,6},{8,9},{9,8},{10,11... | collective-permute-start | bytes 1572872 | tf_op jit(solution)/shard_map/ppermute | solution.py:344
  (7 other events, 217.8 us)

commit v3 on v0

--- a/solution.py
+++ b/solution.py
@@ -130,66 +130,126 @@
     return ref[:, plane, cell].reshape(slabs * rows, lanes)
 
 
-def neighbours(cells, here, before, after):
-    previous = [(before, 0)] + [(here, c) for c in range(cells - 1)]
-    following = [(here, c) for c in range(1, cells)] + [(after, 0)]
-    return previous, following
-
-
-def screen_kernel(here, before, after, diag, upper, lower, out):
+def local_terms(cells):
+    terms = [(c, c, c) for c in range(cells)]
+    for c in range(cells - 1):
+        terms.append((c, c + 1, cells + 2 * c))
+        terms.append((c + 1, c, cells + 2 * c + 1))
+    return sorted(terms)
+
+
+def matrices_kernel(cells, halos, place, *refs):
+    c_diag, c_upper, r_diag, r_upper, c_edge, r_edge = refs[:6]
+    c_high, c_low, r_high, r_low = refs[6:]
+
+    def store(ref, i, matrix):
+        for out, part in zip(ref, parts(matrix), strict=True):
+            out[i] = part
+
+    def fill(refs, read_diag, read_upper, edge):
+        for c in range(cells):
+            store(refs, c, read_diag(c))
+        for c in range(cells - 1):
+            store(refs, cells + 2 * c, read_upper(c))
+            store(refs, cells + 2 * c + 1, read_upper(c).T)
+        first = 3 * cells - 2
+        if halos == 1:
+            store(refs, first, jnp.where(place[1] == 0, read_upper(cells - 1), edge.T))
+        if halos == 2:
+            store(refs, first, edge.T)
+            store(refs, first + 1, read_upper(cells - 1))
+
+    fill((c_high, c_low), lambda c: (c_diag[c] + c_diag[c].T) * 0.5, lambda c: c_upper[c], c_edge[...])
+    for p in range(2):
+        fill(
+            (r_high.at[p], r_low.at[p]),
+            lambda c, p=p: r_diag[p, 0, c],
+            lambda c, p=p: r_upper[p, 0, c],
+            r_edge[p],
+        )
+
+
+def real_terms(high, low, terms, read, planes):
+    lefts, inners = [], []
+    for source, i in terms:
+        left = (high[i], low[i])
+        stacked = parts(jnp.concatenate([read(p, source) for p in range(planes)], 0))
+        lefts.append(left)
+        inners.append(parts(product(stacked, left, True)))
+    left = join(lefts, 1)
+    lanes = high.shape[-1]
+    return [
+        product(left, join([tuple(q[p * lanes : (p + 1) * lanes] for q in i) for i in inners], 0))
+        for p in range(planes)
+    ]
+
+
+def complex_terms(high, low, terms, read):
+    total = None
+    for source, i in terms:
+        re, im = (high[0, i], low[0, i]), (high[1, i], low[1, i])
+        lanes = re[0].shape[0]
+        middle = parts(jnp.concatenate([read(p, source) for p in range(2)], 0))
+        left = join([join([re, negative(im)], 1), join([im, re], 1)], 0)
+        inner = parts(product(left, middle))
+        inner_re = tuple(q[:lanes] for q in inner)
+        inner_im = tuple(q[lanes:] for q in inner)
+        rows = join([join([inner_re, inner_im], 1), join([inner_im, negative(inner_re)], 1)], 0)
+        term = product(rows, join([re, im], 1), True)
+        total = term if total is None else total + term
+    return total
+
+
+def screen_kernel(here, high, low, out):
     slabs, planes, cells, rows, lanes = here.shape
-    previous, following = neighbours(cells, here, before, after)
     for c in range(cells):
-        symmetric = (diag[c] + diag[c].T) * 0.5
-        lefts, inners = [], []
-        for matrix, (ref, cell) in (
-            (symmetric, (here, c)),
-            (upper[c], following[c]),
-            (lower[c].T, previous[c]),
-        ):
-            left = parts(matrix)
-            lefts.append(left)
-            stacked = jnp.concatenate([block_of(ref, p, cell) for p in range(planes)], 0)
-            inners.append(parts(product(parts(stacked), left, True)))
-        left = join(lefts, 1)
-        for p in range(planes):
-            inner = join([tuple(q[p * lanes : (p + 1) * lanes] for q in i) for i in inners], 0)
-            out[:, p, c] = product(left, inner).reshape(slabs, rows, lanes)
-
-
-def output_kernel(here, before, after, diag, upper, lower, out):
-    _, planes, cells, _, lanes = here.shape
-    previous, following = neighbours(cells, here, before, after)
+        terms = [(source, i) for target, source, i in local_terms(cells) if target == c]
+        sums = real_terms(high, low, terms, lambda p, source: block_of(here, p, source), planes)
+        for p, total in enumerate(sums):
+            out[:, p, c] = total.reshape(slabs, rows, lanes)
+
+
+def screen_halo_kernel(halos, place, before, *refs):
+    received, high, low, out = refs[:halos], refs[halos], refs[halos + 1], refs[halos + 2]
+    slabs, planes, cells, rows, lanes = out.shape
+    for h in range(halos):
+        terms = [(0, 3 * cells - 2 + h)]
+        sums = real_terms(high, low, terms, lambda p, source, h=h: block_of(received[h], p, source), planes)
+        c = place[2 + h]
+        for p, total in enumerate(sums):
+            out[:, p, c] = before[:, p, c] + total.reshape(slabs, rows, lanes)
+
+
+def output_kernel(here, high, low, out):
+    cells, lanes = here.shape[2], here.shape[4]
     for c in range(cells):
-        total = None
-        for matrix, turned, (ref, cell) in (
-            (diag, False, (here, c)),
-            (upper, False, following[c]),
-            (lower, True, previous[c]),
-        ):
-            re, im = matrix[0, 0, c], matrix[1, 0, c]
-            if turned:
-                re, im = re.T, im.T
-            re, im = parts(re), parts(im)
-            middle = parts(jnp.concatenate([block_of(ref, p, cell) for p in range(planes)], 0))
-            left = join([join([re, negative(im)], 1), join([im, re], 1)], 0)
-            inner = parts(product(left, middle))
-            inner_re = tuple(q[:lanes] for q in inner)
-            inner_im = tuple(q[lanes:] for q in inner)
-            rows = join([join([inner_re, inner_im], 1), join([inner_im, negative(inner_re)], 1)], 0)
-            term = product(rows, join([re, im], 1), True)
-            total = term if total is None else total + term
-        out[0, 0, c] = total[:lanes]
-        out[1, 0, c] = total[lanes:]
-
-
-def call(kernel, outs, *args):
+        terms = [(source, i) for target, source, i in local_terms(cells) if target == c]
+        total = complex_terms(high, low, terms, lambda p, source: block_of(here, p, source))
+        for p in range(2):
+            out[p, 0, c] = total[p * lanes : (p + 1) * lanes]
+
+
+def output_halo_kernel(halos, place, before, *refs):
+    received, high, low, out = refs[:halos], refs[halos], refs[halos + 1], refs[halos + 2]
+    cells, lanes = out.shape[2], out.shape[4]
+    out[...] = before[...]
+    for h in range(halos):
+        terms = [(0, 3 * cells - 2 + h)]
+        total = complex_terms(high, low, terms, lambda p, source, h=h: block_of(received[h], p, source))
+        c = place[2 + h]
+        for p in range(2):
+            out[p, 0, c] = out[p, 0, c] + total[p * lanes : (p + 1) * lanes]
+
+
+def call(kernel, outs, *args, scalars=False, **more):
+    first = [pl.BlockSpec(memory_space=pltpu.SMEM)] if scalars else []
     return pl.pallas_call(
         kernel,
         out_shape=outs,
-        in_specs=[VMEM] * len(args),
+        in_specs=first + [VMEM] * (len(args) - len(first)),
         out_specs=jax.tree.map(lambda _: VMEM, outs),
-        compiler_params=pltpu.CompilerParams(vmem_limit_bytes=48 * 1024 * 1024),
+        compiler_params=pltpu.CompilerParams(vmem_limit_bytes=24 * 1024 * 1024),
+        **more,
     )(*args)
 
 
@@ -207,8 +267,29 @@
     return lax.ppermute(block, axis, route)
 
 
+def swapped(block):
+    return lax.ppermute(block, "cell", [(0, 1), (1, 0)])
+
+
 def halo(values):
-    return (shifted(values[:, :, -1:], "cell", 1), shifted(values[:, :, :1], "cell", -1))
+    count = lax.axis_size("cell")
+    if count == 1:
+        return []
+    head, tail = values[:, :, :1], values[:, :, -1:]
+    if count == 2:
+        return [swapped(jnp.where(lax.axis_index("cell") == 0, tail, head))]
+    return [shifted(tail, "cell", 1), shifted(head, "cell", -1)]
+
+
+def place_of(cells):
+    count, index = lax.axis_size("cell"), lax.axis_index("cell")
+    if count == 1:
+        targets = []
+    elif count == 2:
+        targets = [jnp.where(index == 0, cells - 1, 0)]
+    else:
+        targets = [0, cells - 1]
+    return len(targets), jnp.stack([jnp.asarray(v, jnp.int32) for v in [len(targets), index, *targets]])
 
 
 def per_device(green_pair, retarded_diag, retarded_upper, coulomb_diag, coulomb_upper):
@@ -217,28 +298,51 @@
     points = devices * held
     scaling = 1.0 / math.sqrt(points)
     rows = orbitals // devices
-    coulomb_edge = shifted(coulomb_upper[-1:], "cell", 1)
-    retarded_edge = shifted(retarded_upper[:, :, -1:], "cell", 1)
-    coulomb_before = jnp.concatenate([coulomb_edge, coulomb_upper[:-1]], 0)
-    retarded_before = jnp.concatenate([retarded_edge, retarded_upper[:, :, :-1]], 2)
+    halos, place = place_of(cells)
+    count = 3 * cells - 2 + halos
+    part = jax.ShapeDtypeStruct((count, orbitals, orbitals), bf16)
+    pair = jax.ShapeDtypeStruct((2, count, orbitals, orbitals), bf16)
+    matrices = call(
+        functools.partial(matrices_kernel, cells, halos),
+        (part, part, pair, pair),
+        place,
+        coulomb_diag,
+        coulomb_upper,
+        retarded_diag,
+        retarded_upper,
+        shifted(coulomb_upper[-1], "cell", 1),
+        shifted(retarded_upper[:, 0, -1], "cell", 1),
+        scalars=True,
+        cost_estimate=pl.CostEstimate(flops=10**9, bytes_accessed=16 * count * orbitals**2 * 4, transcendentals=0),
+    )
     slabs = green_pair.reshape(4, cells, devices, rows, orbitals).transpose(2, 0, 1, 3, 4)
-    entries = exchange(slabs)
+    entries, matrices = lax.optimization_barrier((exchange(slabs), matrices))
+    coulomb, retarded = matrices[:2], matrices[2:]
     half = shape((points, 2, cells, rows, orbitals))
     lesser_hat, polar_hat = call(functools.partial(polarize_kernel, scaling), (half, half), entries)
     polar = exchange(polar_hat)
-    screened = call(screen_kernel, half, polar, *halo(polar), coulomb_diag, coulomb_upper, coulomb_before)
+    received = halo(polar)
+    screened = call(screen_kernel, half, polar, *coulomb)
+    if halos:
+        screened = call(
+            functools.partial(screen_halo_kernel, halos),
+            half,
+            place,
+            screened,
+            *received,
+            *coulomb,
+            scalars=True,
+            input_output_aliases={1: 0},
+        )
     screened_hat = exchange(screened)
-    sigma_entries = call(functools.partial(convolve_kernel, scaling / points), half, lesser_hat, screened_hat)
-    sigma = exchange(sigma_entries)
-    return call(
-        output_kernel,
-        shape(retarded_diag.shape),
-        sigma,
-        *halo(sigma),
-        retarded_diag,
-        retarded_upper,
-        retarded_before,
-    )
+    sigma = exchange(call(functools.partial(convolve_kernel, scaling / points), half, lesser_hat, screened_hat))
+    received = halo(sigma)
+    out = call(output_kernel, shape(retarded_diag.shape), sigma, *retarded)
+    if halos:
+        out = call(
+            functools.partial(output_halo_kernel, halos), shape(out.shape), place, out, *received, *retarded, scalars=True
+        )
+    return out
 
 
 def solution(mesh):

time: 172 us -> 164 us (0.953)
  blocking collectives: 112 us -> 92.4 us
  local copies, waits for them, and re-layouts: 3.06 us -> 15.7 us
  starting transfers between devices: 20.5 us -> 16.2 us
  waiting for transfers between devices: 22.2 us -> 24.6 us
    all_to_all x3, blocking collectives: 112 us -> 92.4 us  [exchange(): lax.all_to_all(values, 'energy', split_axis=0, concat_axis=0, tiled=True)]
    ppermute x6 -> x2, starting transfers between devices: 15.7 us -> 2.57 us  [shifted(): return lax.ppermute(block, axis, route)]
    unnamed x10 -> x30, local copies, waits for them, and re-layouts: 0.02 us -> 10.8 us
    ppermute x0 -> x2, starting transfers between devices: none -> 6.04 us  [swapped(): return lax.ppermute(block, 'cell', [(0, 1), (1, 0)])]
    all_to_all x1, waiting for transfers between devices: 19.7 us -> 22.5 us  [exchange(): lax.all_to_all(values, 'energy', split_axis=0, concat_axis=0, tiled=True)]
    all_to_all x1, starting transfers between devices: 4.82 us -> 7.55 us  [exchange(): lax.all_to_all(values, 'energy', split_axis=0, concat_axis=0, tiled=True)]
    squeeze x0 -> x2, local copies, waits for them, and re-layouts: none -> 1.8 us  [the longest x1 0.97 us: per_device(): coulomb_upper[-1]]
    pallas_call x4 -> x7, Pallas kernels: 12 us -> 13.7 us  [call(): pl.pallas_call(kernel, out_shape=outs, in_specs=first + [VMEM] * (len(arg...]
  transfers between devices with their start and end apart: 7 -> 5, of which waited for: 3 -> 2; matrix products, arithmetic and copies ran while one was open for 1% -> 1% of each run, Pallas kernels for 0% -> 5%
where the time goes in v3:
time: 164 us; the launch traced here: 163 us
  blocking collectives  92.4 us (56%)
  waiting for transfers between devices  24.6 us (15%)
  starting transfers between devices  16.2 us (10%)
  local copies, waits for them, and re-layouts  15.7 us (10%)
  Pallas kernels  13.7 us (8%)
    all_to_all x3, blocking collectives, exchange(): lax.all_to_all(values, 'energy', split_axis=0, concat_axis=0, tiled=True)  92.4 us
    all_to_all x1, waiting for transfers between devices, exchange(): lax.all_to_all(values, 'energy', split_axis=0, concat_axis=0, tiled=True)  22.5 us
    pallas_call x7, Pallas kernels, call(): pl.pallas_call(kernel, out_shape=outs, in_specs=first + [VMEM] * (len(arg...  13.7 us
    unnamed x30, local copies, waits for them, and re-layouts  10.8 us
    all_to_all x1, starting transfers between devices, exchange(): lax.all_to_all(values, 'energy', split_axis=0, concat_axis=0, tiled=True)  7.55 us
    ppermute x2, starting transfers between devices, swapped(): return lax.ppermute(block, 'cell', [(0, 1), (1, 0)])  6.04 us
  transfers between devices with their start and end apart: 5, of which 2 were waited for; matrix products, arithmetic and copies ran while one was open for 1% of the time, Pallas kernels for 5%

profile of v3, /device:TPU:1, one launch (start us, length us, event | category | flops | bytes accessed | tf_op | source)
XLA Modules:
  0.0 163.0 jit_solution(13465859830868776823)
XLA Ops:
  0.0 3.2 %copy.12 = f32[4,2,16,16,256]{4,3,1,0,2:T(8,128)} copy(f32[4,2,16,16,256]{4,3,2,1,0:T(8,128)} %bitcast.13) | data formatting | bytes 4194304 | tf_op jit(solution)/shard_map/reshape | solution.py:318
  3.2 0.0 copy-start.6
  3.2 7.5 %all-to-all-start = ((f32[16,4,2,16,256]{4,3,2,1,0:T(8,128)}), f32[16,4,2,16,256]{4,3,2,1,0:T(8,128)S(1)}, u32[]{:S(2)}, u32[]{:S(2)}) async-start(f32[16,4,2,16,256]{4,3,2,1,0:T(8,128)} %bitcast.12), calls=%async_computation | async-start | bytes 4194304 | tf_op jit(solution)/shard_map/all_to_all | solution.py:261
  10.7 0.0 copy-done.6
  10.7 0.8 slice_bitcast_fusion
  11.6 1.3 collective-permute-start.1
  12.8 1.0 slice_bitcast_fusion.1
  13.8 1.3 collective-permute-start
  15.1 0.1 pad_add_fusion.place
  15.2 2.1 %collective-permute-done.refs_4_ = f32[256,256]{1,0:T(8,128)S(1)} collective-permute-done((f32[256,256]{1,0:T(8,128)S(1)}, f32[256,256]{1,0:T(8,128)S(1)}, u32[]{:S(2)}, u32[]{:S(2)}) %collective-permute-start) | collective-permute-done | bytes 262176 | tf_op jit(solution)/shard_map/ppermute | solution.py:267
  17.3 0.0 copy-start.13
  17.3 0.7 copy-done.13
  18.0 0.0 collective-permute-done.1.refs_5_
  18.0 0.0 copy-start.11
  18.0 0.8 copy-done.11
  18.8 0.0 copy-start.7
  18.8 1.2 copy-done.7
  20.0 0.0 copy-start.8
  20.0 1.0 copy-done.8
  21.1 0.0 copy-start.9
  21.1 1.2 copy-done.9
  22.3 0.0 copy-start.10
  22.3 1.0 copy-done.10
  23.3 0.0 copy-start.12
  23.3 1.0 copy-done.12
  24.4 0.0 copy-start.14
  24.4 0.9 copy-done.14
  25.3 1.5 shard_map.55
  26.8 0.0 copy-start
  26.8 1.1 copy-done
  27.9 0.0 copy-start.2
  27.9 0.8 copy-done.2
  28.7 0.0 copy-start.4
  28.7 0.8 copy-done.4
  29.6 22.5 %all-to-all-done.entries = f32[16,4,2,16,256]{4,3,2,1,0:T(8,128)S(1)} async-done(((f32[16,4,2,16,256]{4,3,2,1,0:T(8,128)}), f32[16,4,2,16,256]{4,3,2,1,0:T(8,128)S(1)}, u32[]{:S(2)}, u32[]{:S(2)}) %all-to-all-start) | async-done | bytes 2097184 | tf_op jit(solution)/shard_map/all_to_all | solution.py:261
  52.1 0.6 shard_map.56
  52.7 0.0 copy-start.3
  52.7 0.0 copy-start.5
  52.8 35.1 %all_to_all.20.here = f32[16,2,2,16,256]{4,3,2,1,0:T(8,128)S(1)} all-to-all(f32[16,2,2,16,256]{4,3,2,1,0:T(8,128)S(1)} %get-tuple-element.22), channel_id=1, replica_groups=mesh['energy'=16,'cell'=2] {'energy'}, dimensions={0} | all-to-all | bytes 2097152 | tf_op jit(solution)/shard_map/all_to_all | solution.py:261
  87.8 0.1 slice_select_fusion.1
  87.9 3.1 %collective-permute-start.2 = (f32[16,2,1,16,256]{4,3,2,1,0:T(8,128)S(1)}, f32[16,2,1,16,256]{4,3,2,1,0:T(8,128)S(1)}, u32[]{:S(2)}, u32[]{:S(2)}) collective-permute-start(f32[16,2,1,16,256]{4,3,2,1,0:T(8,128)S(1)} %slice_select_fusion.1), channel_id=1, source_target_pairs={{0,1},{1,0},{2,3},{3,2},{4,5},{5,4},{6,7},{7,6},{8,9},{9,8},{10,11... | collective-permute-start | bytes 1572872 | tf_op jit(solution)/shard_map/ppermute | solution.py:271
  91.0 0.0 copy-done.3
  91.0 0.0 copy-done.5
  91.0 2.0 %shard_map.57.before = f32[16,2,2,16,256]{4,3,2,1,0:T(8,128)S(1)} custom-call(f32[16,2,2,16,256]{4,3,2,1,0:T(8,128)S(1)} %all_to_all.20.here, bf16[5,256,256]{2,1,0:T(8,128)(2,1)S(1)} %copy-done.3, bf16[5,256,256]{2,1,0:T(8,128)(2,1)S(1)} %copy-done.5), custom_call_target="tpu_custom_call" | custom-call | tf_op jit(solution)/shard_map/pallas_call | solution.py:246
  93.0 0.0 collective-permute-done.2.refs_0_
  93.0 1.6 shard_map.58
  94.6 28.2 %all_to_all.21.screened_hat = f32[16,2,2,16,256]{4,3,2,1,0:T(8,128)S(1)} all-to-all(f32[16,2,2,16,256]{4,3,2,1,0:T(8,128)S(1)} %shard_map.58), channel_id=1, replica_groups=mesh['energy'=16,'cell'=2] {'energy'}, dimensions={0} | all-to-all | bytes 2097152 | tf_op jit(solution)/shard_map/all_to_all | solution.py:261
  122.8 0.5 shard_map.59
  123.4 0.0 copy-start.1
  123.4 29.1 %all_to_all.22.here = f32[16,2,2,16,256]{4,3,2,1,0:T(8,128)S(1)} all-to-all(f32[16,2,2,16,256]{4,3,2,1,0:T(8,128)S(1)} %shard_map.59), channel_id=1, replica_groups=mesh['energy'=16,'cell'=2] {'energy'}, dimensions={0} | all-to-all | bytes 2097152 | tf_op jit(solution)/shard_map/all_to_all | solution.py:261
  152.5 0.1 slice_select_fusion
  152.6 3.0 %collective-permute-start.3 = (f32[16,2,1,16,256]{4,3,2,1,0:T(8,128)S(1)}, f32[16,2,1,16,256]{4,3,2,1,0:T(8,128)S(1)}, u32[]{:S(2)}, u32[]{:S(2)}) collective-permute-start(f32[16,2,1,16,256]{4,3,2,1,0:T(8,128)S(1)} %slice_select_fusion), channel_id=1, source_target_pairs={{0,1},{1,0},{2,3},{3,2},{4,5},{5,4},{6,7},{7,6},{8,9},{9,8},{10,11... | collective-permute-start | bytes 1572872 | tf_op jit(solution)/shard_map/ppermute | solution.py:271
  155.5 0.0 copy-done.1
  155.5 4.2 %shard_map.60.before = f32[2,1,2,256,256]{4,3,2,1,0:T(8,128)S(1)} custom-call(f32[16,2,2,16,256]{4,3,2,1,0:T(8,128)S(1)} %all_to_all.22.here, bf16[2,5,256,256]{3,2,1,0:T(8,128)(2,1)S(1)} %get-tuple-element.25.high.refs_1_, bf16[2,5,256,256]{3,2,1,0:T(8,128)(2,1)S(1)} %copy-done.1), custom_call_target="tpu_custom_call" | custom-call | tf_op jit(solution)/shard_map/pallas_call | solution.py:246
  159.8 0.0 collective-permute-done.3.refs_0_
  159.8 3.3 %shard_map.61 = f32[2,1,2,256,256]{4,3,2,1,0:T(8,128)} custom-call(s32[3]{0:T(128)S(1)} %pad_add_fusion.place, f32[2,1,2,256,256]{4,3,2,1,0:T(8,128)S(1)} %shard_map.60.before, f32[16,2,1,16,256]{4,3,2,1,0:T(8,128)S(1)} %collective-permute-done.3.refs_0_, bf16[2,5,256,256]{3,2,1,0:T(8,128)(2,1)S(1)} %get-tuple-element.25.high.refs_1_, ...), custom_call_target="tpu_custom_call" | custom-call | tf_op jit(solution)/shard_map/pallas_call | solution.py:246
Async XLA Ops:
  3.2 7.6 %copy-start.6 = (f32[2,1,2,256,256]{4,3,2,1,0:T(8,128)S(1)}, f32[2,1,2,256,256]{4,3,2,1,0:T(8,128)}, u32[]{:S(2)}) copy-start(f32[2,1,2,256,256]{4,3,2,1,0:T(8,128)} %refs_3_.1) | copy-start | bytes 3145732
  3.2 49.0 %all-to-all-start = ((f32[16,4,2,16,256]{4,3,2,1,0:T(8,128)}), f32[16,4,2,16,256]{4,3,2,1,0:T(8,128)S(1)}, u32[]{:S(2)}, u32[]{:S(2)}) async-start(f32[16,4,2,16,256]{4,3,2,1,0:T(8,128)} %bitcast.12), calls=%async_computation | async-start | bytes 4194304 | tf_op jit(solution)/shard_map/all_to_all | solution.py:261
  11.6 6.4 %collective-permute-start.1 = (f32[2,256,256]{2,1,0:T(8,128)}, f32[2,256,256]{2,1,0:T(8,128)S(1)}, u32[]{:S(2)}, u32[]{:S(2)}) collective-permute-start(f32[2,256,256]{2,1,0:T(8,128)} %slice_bitcast_fusion), channel_id=1, source_target_pairs={{0,1},{2,3},{4,5},{6,7},{8,9},{10,11},{12,13},{14,15},{16,17},{18,... | collective-permute-start | bytes 1572872 | tf_op jit(solution)/shard_map/ppermute | solution.py:267
  13.8 3.5 %collective-permute-start = (f32[256,256]{1,0:T(8,128)S(1)}, f32[256,256]{1,0:T(8,128)S(1)}, u32[]{:S(2)}, u32[]{:S(2)}) collective-permute-start(f32[256,256]{1,0:T(8,128)S(1)} %slice_bitcast_fusion.1), channel_id=1, source_target_pairs={{0,1},{2,3},{4,5},{6,7},{8,9},{10,11},{12,13},{14,15},{16,17},{18,... | collective-permute-start | bytes 786440 | tf_op jit(solution)/shard_map/ppermute | solution.py:267
  17.3 0.7 copy-start.13
  18.0 0.8 copy-start.11
  18.8 1.2 copy-start.7
  20.0 1.0 copy-start.8
  21.1 1.2 copy-start.9
  22.3 1.0 copy-start.10
  23.3 1.0 copy-start.12
  24.4 0.9 copy-start.14
  26.8 1.1 copy-start
  27.9 0.8 copy-start.2
  28.7 0.8 copy-start.4
  52.7 38.3 %copy-start.3 = (bf16[5,256,256]{2,1,0:T(8,128)(2,1)S(1)}, bf16[5,256,256]{2,1,0:T(8,128)(2,1)}, u32[]{:S(2)}) copy-start(bf16[5,256,256]{2,1,0:T(8,128)(2,1)} %copy-done.2) | copy-start | bytes 1966084
  52.7 38.3 %copy-start.5 = (bf16[5,256,256]{2,1,0:T(8,128)(2,1)S(1)}, bf16[5,256,256]{2,1,0:T(8,128)(2,1)}, u32[]{:S(2)}) copy-start(bf16[5,256,256]{2,1,0:T(8,128)(2,1)} %copy-done.4) | copy-start | bytes 1966084
  87.9 5.1 %collective-permute-start.2 = (f32[16,2,1,16,256]{4,3,2,1,0:T(8,128)S(1)}, f32[16,2,1,16,256]{4,3,2,1,0:T(8,128)S(1)}, u32[]{:S(2)}, u32[]{:S(2)}) collective-permute-start(f32[16,2,1,16,256]{4,3,2,1,0:T(8,128)S(1)} %slice_select_fusion.1), channel_id=1, source_target_pairs={{0,1},{1,0},{2,3},{3,2},{4,5},{5,4},{6,7},{7,6},{8,9},{9,8},{10,11... | collective-permute-start | bytes 1572872 | tf_op jit(solution)/shard_map/ppermute | solution.py:271
  123.4 32.2 %copy-start.1 = (bf16[2,5,256,256]{3,2,1,0:T(8,128)(2,1)S(1)}, bf16[2,5,256,256]{3,2,1,0:T(8,128)(2,1)}, u32[]{:S(2)}) copy-start(bf16[2,5,256,256]{3,2,1,0:T(8,128)(2,1)} %copy-done) | copy-start | bytes 3932164
  152.6 7.2 %collective-permute-start.3 = (f32[16,2,1,16,256]{4,3,2,1,0:T(8,128)S(1)}, f32[16,2,1,16,256]{4,3,2,1,0:T(8,128)S(1)}, u32[]{:S(2)}, u32[]{:S(2)}) collective-permute-start(f32[16,2,1,16,256]{4,3,2,1,0:T(8,128)S(1)} %slice_select_fusion), channel_id=1, source_target_pairs={{0,1},{1,0},{2,3},{3,2},{4,5},{5,4},{6,7},{7,6},{8,9},{9,8},{10,11... | collective-permute-start | bytes 1572872 | tf_op jit(solution)/shard_map/ppermute | solution.py:271

commit v4 on v3

--- a/solution.py
+++ b/solution.py
@@ -9,6 +9,7 @@
 from jax.sharding import PartitionSpec as P
 
 VMEM = pl.BlockSpec(memory_space=pltpu.VMEM)
+ANY = pl.BlockSpec(memory_space=pl.ANY)
 f32 = jnp.float32
 bf16 = jnp.bfloat16
 
@@ -185,19 +186,20 @@
 
 
 def complex_terms(high, low, terms, read):
-    total = None
+    out_re, out_im = None, None
     for source, i in terms:
-        re, im = (high[0, i], low[0, i]), (high[1, i], low[1, i])
-        lanes = re[0].shape[0]
-        middle = parts(jnp.concatenate([read(p, source) for p in range(2)], 0))
-        left = join([join([re, negative(im)], 1), join([im, re], 1)], 0)
-        inner = parts(product(left, middle))
-        inner_re = tuple(q[:lanes] for q in inner)
-        inner_im = tuple(q[lanes:] for q in inner)
-        rows = join([join([inner_re, inner_im], 1), join([inner_im, negative(inner_re)], 1)], 0)
-        term = product(rows, join([re, im], 1), True)
-        total = term if total is None else total + term
-    return total
+        re, im = ((high[p, i], low[p, i]) for p in range(2))
+        whole_re, whole_im = (sum(q.astype(f32) for q in pair) for pair in (re, im))
+        both, apart = parts(whole_re + whole_im), parts(whole_re - whole_im)
+        x_re, x_im = read(0, source), read(1, source)
+        a, b = product(re, parts(x_re)), product(im, parts(x_im))
+        c = product(both, parts(x_re + x_im))
+        t_re, t_im = a - b, c - a - b
+        a, b = product(parts(t_re), re, True), product(parts(t_im), im, True)
+        c = product(parts(t_re + t_im), apart, True)
+        out_re = a + b if out_re is None else out_re + (a + b)
+        out_im = c - a + b if out_im is None else out_im + (c - a + b)
+    return out_re, out_im
 
 
 def screen_kernel(here, high, low, out):
@@ -221,34 +223,71 @@
 
 
 def output_kernel(here, high, low, out):
-    cells, lanes = here.shape[2], here.shape[4]
+    cells = here.shape[2]
     for c in range(cells):
         terms = [(source, i) for target, source, i in local_terms(cells) if target == c]
-        total = complex_terms(high, low, terms, lambda p, source: block_of(here, p, source))
-        for p in range(2):
-            out[p, 0, c] = total[p * lanes : (p + 1) * lanes]
+        out[0, 0, c], out[1, 0, c] = complex_terms(high, low, terms, lambda p, source: block_of(here, p, source))
 
 
 def output_halo_kernel(halos, place, before, *refs):
     received, high, low, out = refs[:halos], refs[halos], refs[halos + 1], refs[halos + 2]
-    cells, lanes = out.shape[2], out.shape[4]
-    out[...] = before[...]
+    total, sems = refs[halos + 3 :]
+    cells = out.shape[2]
+
+    def touched(c):
+        return functools.reduce(jnp.logical_or, [place[2 + h] == c for h in range(halos)])
+
+    def copy_of(ref, c, i):
+        return pltpu.make_async_copy(ref, out.at[:, :, c], sems.at[i])
+
+    for c in range(cells):
+
+        @pl.when(jnp.logical_not(touched(c)))
+        def _(c=c):
+            copy_of(before.at[:, :, c], c, c).start()
+
     for h in range(halos):
         terms = [(0, 3 * cells - 2 + h)]
-        total = complex_terms(high, low, terms, lambda p, source, h=h: block_of(received[h], p, source))
+        sums = complex_terms(high, low, terms, lambda p, source, h=h: block_of(received[h], p, source))
         c = place[2 + h]
         for p in range(2):
-            out[p, 0, c] = out[p, 0, c] + total[p * lanes : (p + 1) * lanes]
-
-
-def call(kernel, outs, *args, scalars=False, **more):
+            total[h, p, 0] = before[p, 0, c] + sums[p]
+        copy_of(total.at[h], c, cells + h).start()
+    for c in range(cells):
+
+        @pl.when(jnp.logical_not(touched(c)))
+        def _(c=c):
+            copy_of(before.at[:, :, c], c, c).wait()
+
+    for h in range(halos):
+        copy_of(total.at[h], place[2 + h], cells + h).wait()
+
+
+def slabs_kernel(green, slabs, stage, sems_in, sems_out):
+    devices, planes, cells, rows, lanes = slabs.shape
+    blocks = [(p, c) for p in range(planes) for c in range(cells)]
+    into = [
+        pltpu.make_async_copy(green.at[p, 0, c].reshape(devices, rows, lanes), stage.at[i], sems_in.at[i])
+        for i, (p, c) in enumerate(blocks)
+    ]
+    out = [pltpu.make_async_copy(stage.at[i], slabs.at[:, p, c], sems_out.at[i]) for i, (p, c) in enumerate(blocks)]
+    for copy in into:
+        copy.start()
+    for first, second in zip(into, out, strict=True):
+        first.wait()
+        second.start()
+    for copy in out:
+        copy.wait()
+
+
+def call(kernel, outs, *args, scalars=False, out_specs=None, **more):
     first = [pl.BlockSpec(memory_space=pltpu.SMEM)] if scalars else []
     return pl.pallas_call(
         kernel,
         out_shape=outs,
         in_specs=first + [VMEM] * (len(args) - len(first)),
-        out_specs=jax.tree.map(lambda _: VMEM, outs),
-        compiler_params=pltpu.CompilerParams(vmem_limit_bytes=24 * 1024 * 1024),
+        out_specs=out_specs or jax.tree.map(lambda _: VMEM, outs),
+        compiler_params=pltpu.CompilerParams(vmem_limit_bytes=16 * 1024 * 1024),
         **more,
     )(*args)
 
@@ -315,7 +354,17 @@
         scalars=True,
         cost_estimate=pl.CostEstimate(flops=10**9, bytes_accessed=16 * count * orbitals**2 * 4, transcendentals=0),
     )
-    slabs = green_pair.reshape(4, cells, devices, rows, orbitals).transpose(2, 0, 1, 3, 4)
+    slabs = pl.pallas_call(
+        slabs_kernel,
+        out_shape=shape((devices, 4, cells, rows, orbitals)),
+        in_specs=[ANY],
+        out_specs=ANY,
+        scratch_shapes=[
+            pltpu.VMEM((4 * cells, devices, rows, orbitals), f32),
+            pltpu.SemaphoreType.DMA((4 * cells,)),
+            pltpu.SemaphoreType.DMA((4 * cells,)),
+        ],
+    )(green_pair)
     entries, matrices = lax.optimization_barrier((exchange(slabs), matrices))
     coulomb, retarded = matrices[:2], matrices[2:]
     half = shape((points, 2, cells, rows, orbitals))
@@ -340,7 +389,18 @@
     out = call(output_kernel, shape(retarded_diag.shape), sigma, *retarded)
     if halos:
         out = call(
-            functools.partial(output_halo_kernel, halos), shape(out.shape), place, out, *received, *retarded, scalars=True
+            functools.partial(output_halo_kernel, halos),
+            shape(out.shape),
+            place,
+            out,
+            *received,
+            *retarded,
+            scalars=True,
+            out_specs=ANY,
+            scratch_shapes=[
+                pltpu.VMEM((halos, 2, 1, orbitals, orbitals), f32),
+                pltpu.SemaphoreType.DMA((cells + halos,)),
+            ],
         )
     return out
 

time: 164 us -> 161 us (0.982)
  local copies, waits for them, and re-layouts: 15.7 us -> 12.6 us
    reshape x1 -> x0, local copies, waits for them, and re-layouts: 3.16 us -> none  [per_device(): green_pair.reshape(4, cells, devices, rows, orbitals)]
    pallas_call x0 -> x1, Pallas kernels: none -> 2.45 us  [per_device(): pl.pallas_call(slabs_kernel, out_shape=shape((devices, 4, cells, rows, or...]
    pallas_call x7, Pallas kernels: 13.7 us -> 11.7 us  [call(): pl.pallas_call(kernel, out_shape=outs, in_specs=first + [VMEM] * (len(arg...]
  transfers between devices with their start and end apart: 5 -> 5, of which waited for: 2 -> 2; matrix products, arithmetic and copies ran while one was open for 1% -> 1% of each run, Pallas kernels for 5% -> 4%
where the time goes in v4:
time: 161 us; the launch traced here: 160 us
  blocking collectives  92.4 us (57%)
  waiting for transfers between devices  24.6 us (15%)
  starting transfers between devices  16.2 us (10%)
  Pallas kernels  14.2 us (9%)
  local copies, waits for them, and re-layouts  12.6 us (8%)
    all_to_all x3, blocking collectives, exchange(): lax.all_to_all(values, 'energy', split_axis=0, concat_axis=0, tiled=True)  92.4 us
    all_to_all x1, waiting for transfers between devices, exchange(): lax.all_to_all(values, 'energy', split_axis=0, concat_axis=0, tiled=True)  22.5 us
    pallas_call x7, Pallas kernels, call(): pl.pallas_call(kernel, out_shape=outs, in_specs=first + [VMEM] * (len(arg...  11.7 us
    unnamed x30, local copies, waits for them, and re-layouts  10.8 us
    all_to_all x1, starting transfers between devices, exchange(): lax.all_to_all(values, 'energy', split_axis=0, concat_axis=0, tiled=True)  7.56 us
    ppermute x2, starting transfers between devices, swapped(): return lax.ppermute(block, 'cell', [(0, 1), (1, 0)])  6.04 us
  transfers between devices with their start and end apart: 5, of which 2 were waited for; matrix products, arithmetic and copies ran while one was open for 1% of the time, Pallas kernels for 4%

profile of v4, /device:TPU:1, one launch (start us, length us, event | category | flops | bytes accessed | tf_op | source)
XLA Modules:
  0.0 160.3 jit_solution(3105508502944762427)
XLA Ops:
  0.0 2.5 %shard_map.55 = f32[16,4,2,16,256]{4,3,2,1,0:T(8,128)} custom-call(f32[4,1,2,256,256]{4,3,2,1,0:T(8,128)} %green.1), custom_call_target="tpu_custom_call" | custom-call | tf_op jit(solution)/shard_map/pallas_call | solution.py:357
  2.5 0.0 copy-start.6
  2.5 7.6 %all-to-all-start = ((f32[16,4,2,16,256]{4,3,2,1,0:T(8,128)}), f32[16,4,2,16,256]{4,3,2,1,0:T(8,128)S(1)}, u32[]{:S(2)}, u32[]{:S(2)}) async-start(f32[16,4,2,16,256]{4,3,2,1,0:T(8,128)} %shard_map.55), calls=%async_computation | async-start | bytes 4194304 | tf_op jit(solution)/shard_map/all_to_all | solution.py:300
  10.0 0.0 copy-done.6
  10.0 0.8 slice_bitcast_fusion
  10.9 1.3 collective-permute-start.1
  12.2 1.0 slice_bitcast_fusion.1
  13.1 1.3 collective-permute-start
  14.4 0.1 pad_add_fusion.place
  14.5 2.1 %collective-permute-done.refs_4_ = f32[256,256]{1,0:T(8,128)S(1)} collective-permute-done((f32[256,256]{1,0:T(8,128)S(1)}, f32[256,256]{1,0:T(8,128)S(1)}, u32[]{:S(2)}, u32[]{:S(2)}) %collective-permute-start) | collective-permute-done | bytes 262176 | tf_op jit(solution)/shard_map/ppermute | solution.py:306
  16.6 0.0 copy-start.13
  16.6 0.7 copy-done.13
  17.3 0.0 collective-permute-done.1.refs_5_
  17.3 0.0 copy-start.11
  17.3 0.8 copy-done.11
  18.1 0.0 copy-start.7
  18.1 1.2 copy-done.7
  19.3 0.0 copy-start.8
  19.3 1.0 copy-done.8
  20.4 0.0 copy-start.9
  20.4 1.2 copy-done.9
  21.6 0.0 copy-start.10
  21.6 1.0 copy-done.10
  22.6 0.0 copy-start.12
  22.6 1.0 copy-done.12
  23.7 0.0 copy-start.14
  23.7 0.9 copy-done.14
  24.6 1.6 shard_map.56
  26.2 0.0 copy-start
  26.2 1.1 copy-done
  27.3 0.0 copy-start.2
  27.3 0.8 copy-done.2
  28.1 0.0 copy-start.4
  28.1 0.8 copy-done.4
  28.9 22.5 %all-to-all-done.entries = f32[16,4,2,16,256]{4,3,2,1,0:T(8,128)S(1)} async-done(((f32[16,4,2,16,256]{4,3,2,1,0:T(8,128)}), f32[16,4,2,16,256]{4,3,2,1,0:T(8,128)S(1)}, u32[]{:S(2)}, u32[]{:S(2)}) %all-to-all-start) | async-done | bytes 2097184 | tf_op jit(solution)/shard_map/all_to_all | solution.py:300
  51.4 0.6 shard_map.57
  52.1 0.0 copy-start.3
  52.1 0.0 copy-start.5
  52.1 35.1 %all_to_all.20.here = f32[16,2,2,16,256]{4,3,2,1,0:T(8,128)S(1)} all-to-all(f32[16,2,2,16,256]{4,3,2,1,0:T(8,128)S(1)} %get-tuple-element.22), channel_id=1, replica_groups=mesh['energy'=16,'cell'=2] {'energy'}, dimensions={0} | all-to-all | bytes 2097152 | tf_op jit(solution)/shard_map/all_to_all | solution.py:300
  87.2 0.1 slice_select_fusion.1
  87.3 3.1 %collective-permute-start.2 = (f32[16,2,1,16,256]{4,3,2,1,0:T(8,128)S(1)}, f32[16,2,1,16,256]{4,3,2,1,0:T(8,128)S(1)}, u32[]{:S(2)}, u32[]{:S(2)}) collective-permute-start(f32[16,2,1,16,256]{4,3,2,1,0:T(8,128)S(1)} %slice_select_fusion.1), channel_id=1, source_target_pairs={{0,1},{1,0},{2,3},{3,2},{4,5},{5,4},{6,7},{7,6},{8,9},{9,8},{10,11... | collective-permute-start | bytes 1572872 | tf_op jit(solution)/shard_map/ppermute | solution.py:310
  90.3 0.0 copy-done.3
  90.3 0.0 copy-done.5
  90.3 2.0 %shard_map.58.before = f32[16,2,2,16,256]{4,3,2,1,0:T(8,128)S(1)} custom-call(f32[16,2,2,16,256]{4,3,2,1,0:T(8,128)S(1)} %all_to_all.20.here, bf16[5,256,256]{2,1,0:T(8,128)(2,1)S(1)} %copy-done.3, bf16[5,256,256]{2,1,0:T(8,128)(2,1)S(1)} %copy-done.5), custom_call_target="tpu_custom_call" | custom-call | tf_op jit(solution)/shard_map/pallas_call | solution.py:285
  92.4 0.0 collective-permute-done.2.refs_0_
  92.4 1.6 shard_map.59
  94.0 28.2 %all_to_all.21.screened_hat = f32[16,2,2,16,256]{4,3,2,1,0:T(8,128)S(1)} all-to-all(f32[16,2,2,16,256]{4,3,2,1,0:T(8,128)S(1)} %shard_map.59), channel_id=1, replica_groups=mesh['energy'=16,'cell'=2] {'energy'}, dimensions={0} | all-to-all | bytes 2097152 | tf_op jit(solution)/shard_map/all_to_all | solution.py:300
  122.2 0.5 shard_map.60
  122.7 0.0 copy-start.1
  122.7 29.1 %all_to_all.22.here = f32[16,2,2,16,256]{4,3,2,1,0:T(8,128)S(1)} all-to-all(f32[16,2,2,16,256]{4,3,2,1,0:T(8,128)S(1)} %shard_map.60), channel_id=1, replica_groups=mesh['energy'=16,'cell'=2] {'energy'}, dimensions={0} | all-to-all | bytes 2097152 | tf_op jit(solution)/shard_map/all_to_all | solution.py:300
  151.8 0.1 slice_select_fusion
  151.9 3.0 %collective-permute-start.3 = (f32[16,2,1,16,256]{4,3,2,1,0:T(8,128)S(1)}, f32[16,2,1,16,256]{4,3,2,1,0:T(8,128)S(1)}, u32[]{:S(2)}, u32[]{:S(2)}) collective-permute-start(f32[16,2,1,16,256]{4,3,2,1,0:T(8,128)S(1)} %slice_select_fusion), channel_id=1, source_target_pairs={{0,1},{1,0},{2,3},{3,2},{4,5},{5,4},{6,7},{7,6},{8,9},{9,8},{10,11... | collective-permute-start | bytes 1572872 | tf_op jit(solution)/shard_map/ppermute | solution.py:310
  154.9 0.0 copy-done.1
  154.9 3.1 %shard_map.61.before = f32[2,1,2,256,256]{4,3,2,1,0:T(8,128)S(1)} custom-call(f32[16,2,2,16,256]{4,3,2,1,0:T(8,128)S(1)} %all_to_all.22.here, bf16[2,5,256,256]{3,2,1,0:T(8,128)(2,1)S(1)} %get-tuple-element.25.high.refs_1_, bf16[2,5,256,256]{3,2,1,0:T(8,128)(2,1)S(1)} %copy-done.1), custom_call_target="tpu_custom_call" | custom-call | tf_op jit(solution)/shard_map/pallas_call | solution.py:285
  158.0 0.0 collective-permute-done.3.refs_0_
  158.0 2.3 %shard_map.62 = f32[2,1,2,256,256]{4,3,2,1,0:T(8,128)} custom-call(s32[3]{0:T(128)S(1)} %pad_add_fusion.place, f32[2,1,2,256,256]{4,3,2,1,0:T(8,128)S(1)} %shard_map.61.before, f32[16,2,1,16,256]{4,3,2,1,0:T(8,128)S(1)} %collective-permute-done.3.refs_0_, bf16[2,5,256,256]{3,2,1,0:T(8,128)(2,1)S(1)} %get-tuple-element.25.high.refs_1_, ...), custom_call_target="tpu_custom_call" | custom-call | tf_op jit(solution)/shard_map/pallas_call | solution.py:285
Async XLA Ops:
  2.5 7.6 %copy-start.6 = (f32[2,1,2,256,256]{4,3,2,1,0:T(8,128)S(1)}, f32[2,1,2,256,256]{4,3,2,1,0:T(8,128)}, u32[]{:S(2)}) copy-start(f32[2,1,2,256,256]{4,3,2,1,0:T(8,128)} %refs_3_.1) | copy-start | bytes 3145732
  2.5 49.0 %all-to-all-start = ((f32[16,4,2,16,256]{4,3,2,1,0:T(8,128)}), f32[16,4,2,16,256]{4,3,2,1,0:T(8,128)S(1)}, u32[]{:S(2)}, u32[]{:S(2)}) async-start(f32[16,4,2,16,256]{4,3,2,1,0:T(8,128)} %shard_map.55), calls=%async_computation | async-start | bytes 4194304 | tf_op jit(solution)/shard_map/all_to_all | solution.py:300
  10.9 6.4 %collective-permute-start.1 = (f32[2,256,256]{2,1,0:T(8,128)}, f32[2,256,256]{2,1,0:T(8,128)S(1)}, u32[]{:S(2)}, u32[]{:S(2)}) collective-permute-start(f32[2,256,256]{2,1,0:T(8,128)} %slice_bitcast_fusion), channel_id=1, source_target_pairs={{0,1},{2,3},{4,5},{6,7},{8,9},{10,11},{12,13},{14,15},{16,17},{18,... | collective-permute-start | bytes 1572872 | tf_op jit(solution)/shard_map/ppermute | solution.py:306
  13.1 3.5 %collective-permute-start = (f32[256,256]{1,0:T(8,128)S(1)}, f32[256,256]{1,0:T(8,128)S(1)}, u32[]{:S(2)}, u32[]{:S(2)}) collective-permute-start(f32[256,256]{1,0:T(8,128)S(1)} %slice_bitcast_fusion.1), channel_id=1, source_target_pairs={{0,1},{2,3},{4,5},{6,7},{8,9},{10,11},{12,13},{14,15},{16,17},{18,... | collective-permute-start | bytes 786440 | tf_op jit(solution)/shard_map/ppermute | solution.py:306
  16.6 0.7 copy-start.13
  17.3 0.8 copy-start.11
  18.1 1.2 copy-start.7
  19.3 1.0 copy-start.8
  20.4 1.2 copy-start.9
  21.6 1.0 copy-start.10
  22.6 1.0 copy-start.12
  23.7 0.9 copy-start.14
  26.2 1.1 copy-start
  27.3 0.8 copy-start.2
  28.1 0.8 copy-start.4
  52.1 38.3 %copy-start.3 = (bf16[5,256,256]{2,1,0:T(8,128)(2,1)S(1)}, bf16[5,256,256]{2,1,0:T(8,128)(2,1)}, u32[]{:S(2)}) copy-start(bf16[5,256,256]{2,1,0:T(8,128)(2,1)} %copy-done.2) | copy-start | bytes 1966084
  52.1 38.3 %copy-start.5 = (bf16[5,256,256]{2,1,0:T(8,128)(2,1)S(1)}, bf16[5,256,256]{2,1,0:T(8,128)(2,1)}, u32[]{:S(2)}) copy-start(bf16[5,256,256]{2,1,0:T(8,128)(2,1)} %copy-done.4) | copy-start | bytes 1966084
  87.3 5.1 %collective-permute-start.2 = (f32[16,2,1,16,256]{4,3,2,1,0:T(8,128)S(1)}, f32[16,2,1,16,256]{4,3,2,1,0:T(8,128)S(1)}, u32[]{:S(2)}, u32[]{:S(2)}) collective-permute-start(f32[16,2,1,16,256]{4,3,2,1,0:T(8,128)S(1)} %slice_select_fusion.1), channel_id=1, source_target_pairs={{0,1},{1,0},{2,3},{3,2},{4,5},{5,4},{6,7},{7,6},{8,9},{9,8},{10,11... | collective-permute-start | bytes 1572872 | tf_op jit(solution)/shard_map/ppermute | solution.py:310
  122.7 32.2 %copy-start.1 = (bf16[2,5,256,256]{3,2,1,0:T(8,128)(2,1)S(1)}, bf16[2,5,256,256]{3,2,1,0:T(8,128)(2,1)}, u32[]{:S(2)}) copy-start(bf16[2,5,256,256]{3,2,1,0:T(8,128)(2,1)} %copy-done) | copy-start | bytes 3932164
  151.9 6.1 %collective-permute-start.3 = (f32[16,2,1,16,256]{4,3,2,1,0:T(8,128)S(1)}, f32[16,2,1,16,256]{4,3,2,1,0:T(8,128)S(1)}, u32[]{:S(2)}, u32[]{:S(2)}) collective-permute-start(f32[16,2,1,16,256]{4,3,2,1,0:T(8,128)S(1)} %slice_select_fusion), channel_id=1, source_target_pairs={{0,1},{1,0},{2,3},{3,2},{4,5},{5,4},{6,7},{7,6},{8,9},{9,8},{10,11... | collective-permute-start | bytes 1572872 | tf_op jit(solution)/shard_map/ppermute | solution.py:310

commit v5 on v4

--- a/solution.py
+++ b/solution.py
@@ -74,12 +74,11 @@
 
 def polarize_kernel(scaling, entries, lesser_hat, polar_hat):
     points, _, cells, rows, lanes = entries.shape
+    at = places_of(points)
     for c, r, b in tiles_of(cells, rows, lanes):
         hats = []
         for pair in (0, 2):
-            hats.append(
-                fourier([(entries[n, pair, c, r, b], entries[n, pair + 1, c, r, b]) for n in range(points)], -1)
-            )
+            hats.append(fourier([(entries[i, pair, c, r, b], entries[i, pair + 1, c, r, b]) for i in at], -1))
             if pair == 0:
                 for k in range(points):
                     lesser_hat[k, 0, c, r, b] = hats[0][k][0]
@@ -88,23 +87,24 @@
             greater_re, greater_im = hats[1][k]
             lesser_re = lesser_hat[k, 0, c, r, b]
             lesser_im = lesser_hat[k, 1, c, r, b]
-            polar_hat[k, 0, c, r, b] = (lesser_re * greater_im - lesser_im * greater_re) * scaling
-            polar_hat[k, 1, c, r, b] = (lesser_re * greater_re + lesser_im * greater_im) * scaling
+            polar_hat[at[k], 0, c, r, b] = (lesser_re * greater_im - lesser_im * greater_re) * scaling
+            polar_hat[at[k], 1, c, r, b] = (lesser_re * greater_re + lesser_im * greater_im) * scaling
 
 
 def convolve_kernel(factor, lesser_hat, screened_hat, sigma):
     points, _, cells, rows, lanes = screened_hat.shape
+    at = places_of(points)
     for c, r, b in tiles_of(cells, rows, lanes):
         spectral = []
         for k in range(points):
             lesser_re, lesser_im = lesser_hat[k, 0, c, r, b], lesser_hat[k, 1, c, r, b]
-            w_re, w_im = screened_hat[k, 0, c, r, b], screened_hat[k, 1, c, r, b]
+            w_re, w_im = screened_hat[at[k], 0, c, r, b], screened_hat[at[k], 1, c, r, b]
             spectral.append(
                 ((lesser_re * w_re - lesser_im * w_im) * factor, (lesser_re * w_im + lesser_im * w_re) * factor)
             )
         for n, (re, im) in enumerate(fourier(spectral, 1)):
-            sigma[n, 0, c, r, b] = -im
-            sigma[n, 1, c, r, b] = re
+            sigma[at[n], 0, c, r, b] = -im
+            sigma[at[n], 1, c, r, b] = re
 
 
 def parts(matrix):
@@ -296,8 +296,22 @@
     return jax.ShapeDtypeStruct(tuple(dims), f32)
 
 
+def order_of(devices):
+    middle = devices // 2
+    ends = [e for i in range((devices + 1) // 2) for e in sorted({i, devices - 1 - i})]
+    return [middle] + [e for e in ends if e != middle]
+
+
+def places_of(points):
+    order = order_of(points)
+    return [order.index(e) for e in range(points)]
+
+
 def exchange(values):
-    return lax.all_to_all(values, "energy", split_axis=0, concat_axis=0, tiled=True)
+    order = order_of(lax.axis_size("energy"))
+    return lax.all_to_all(
+        values, "energy", split_axis=0, concat_axis=0, axis_index_groups=[order], tiled=True
+    )
 
 
 def shifted(block, axis, step):

time: 161 us -> 158 us (0.981)
  starting transfers between devices: 16.2 us -> 23.2 us
  blocking collectives: 92.4 us -> 87.2 us
  waiting for transfers between devices: 24.6 us -> 19.7 us
    ppermute x2, starting transfers between devices: 6.04 us -> 12.9 us  [swapped(): return lax.ppermute(block, 'cell', [(0, 1), (1, 0)])]
    all_to_all x3, blocking collectives: 92.4 us -> 87.2 us  [exchange(): lax.all_to_all(values, 'energy', split_axis=0, concat_axis=0, axis_index_...]
    all_to_all x1, waiting for transfers between devices: 22.5 us -> 17.5 us  [exchange(): lax.all_to_all(values, 'energy', split_axis=0, concat_axis=0, axis_index_...]
where the time goes in v5:
time: 158 us; the launch traced here: 157 us
  blocking collectives  87.2 us (55%)
  starting transfers between devices  23.2 us (15%)
  waiting for transfers between devices  19.7 us (12%)
  Pallas kernels  14.2 us (9%)
  local copies, waits for them, and re-layouts  12.6 us (8%)
    all_to_all x3, blocking collectives, exchange(): lax.all_to_all(values, 'energy', split_axis=0, concat_axis=0, axis_index_...  87.2 us
    all_to_all x1, waiting for transfers between devices, exchange(): lax.all_to_all(values, 'energy', split_axis=0, concat_axis=0, axis_index_...  17.5 us
    ppermute x2, starting transfers between devices, swapped(): return lax.ppermute(block, 'cell', [(0, 1), (1, 0)])  12.9 us
    pallas_call x7, Pallas kernels, call(): pl.pallas_call(kernel, out_shape=outs, in_specs=first + [VMEM] * (len(arg...  11.7 us
    unnamed x30, local copies, waits for them, and re-layouts  10.8 us
    all_to_all x1, starting transfers between devices, exchange(): lax.all_to_all(values, 'energy', split_axis=0, concat_axis=0, axis_index_...  7.75 us
  transfers between devices with their start and end apart: 5, of which 2 were waited for; matrix products, arithmetic and copies ran while one was open for 1% of the time, Pallas kernels for 4%

profile of v5, /device:TPU:1, one launch (start us, length us, event | category | flops | bytes accessed | tf_op | source)
XLA Modules:
  0.0 157.2 jit_solution(13835788288305543366)
XLA Ops:
  0.0 2.5 %shard_map.55 = f32[16,4,2,16,256]{4,3,2,1,0:T(8,128)} custom-call(f32[4,1,2,256,256]{4,3,2,1,0:T(8,128)} %green.1), custom_call_target="tpu_custom_call" | custom-call | tf_op jit(solution)/shard_map/pallas_call | solution.py:371
  2.5 0.0 copy-start.6
  2.5 7.7 %all-to-all-start = ((f32[16,4,2,16,256]{4,3,2,1,0:T(8,128)}), f32[16,4,2,16,256]{4,3,2,1,0:T(8,128)S(1)}, u32[]{:S(2)}, u32[]{:S(2)}) async-start(f32[16,4,2,16,256]{4,3,2,1,0:T(8,128)} %shard_map.55), calls=%async_computation | async-start | bytes 4194304 | tf_op jit(solution)/shard_map/all_to_all | solution.py:312
  10.2 0.0 copy-done.6
  10.2 0.8 slice_bitcast_fusion
  11.1 1.3 collective-permute-start.1
  12.3 1.0 slice_bitcast_fusion.1
  13.3 1.3 collective-permute-start
  14.6 0.1 pad_add_fusion.place
  14.7 2.2 %collective-permute-done.refs_4_ = f32[256,256]{1,0:T(8,128)S(1)} collective-permute-done((f32[256,256]{1,0:T(8,128)S(1)}, f32[256,256]{1,0:T(8,128)S(1)}, u32[]{:S(2)}, u32[]{:S(2)}) %collective-permute-start) | collective-permute-done | bytes 262176 | tf_op jit(solution)/shard_map/ppermute | solution.py:320
  16.9 0.0 copy-start.13
  16.9 0.7 copy-done.13
  17.6 0.0 collective-permute-done.1.refs_5_
  17.6 0.0 copy-start.11
  17.6 0.8 copy-done.11
  18.4 0.0 copy-start.7
  18.4 1.2 copy-done.7
  19.6 0.0 copy-start.8
  19.6 1.0 copy-done.8
  20.7 0.0 copy-start.9
  20.7 1.2 copy-done.9
  21.9 0.0 copy-start.10
  21.9 1.0 copy-done.10
  22.9 0.0 copy-start.12
  22.9 1.0 copy-done.12
  24.0 0.0 copy-start.14
  24.0 0.9 copy-done.14
  24.9 1.6 shard_map.56
  26.5 0.0 copy-start
  26.5 1.1 copy-done
  27.6 0.0 copy-start.2
  27.6 0.8 copy-done.2
  28.4 0.0 copy-start.4
  28.4 0.8 copy-done.4
  29.2 17.5 %all-to-all-done.entries = f32[16,4,2,16,256]{4,3,2,1,0:T(8,128)S(1)} async-done(((f32[16,4,2,16,256]{4,3,2,1,0:T(8,128)}), f32[16,4,2,16,256]{4,3,2,1,0:T(8,128)S(1)}, u32[]{:S(2)}, u32[]{:S(2)}) %all-to-all-start) | async-done | bytes 2097184 | tf_op jit(solution)/shard_map/all_to_all | solution.py:312
  46.7 0.6 shard_map.57
  47.3 0.0 copy-start.3
  47.3 0.0 copy-start.5
  47.3 35.8 %all_to_all.20.here = f32[16,2,2,16,256]{4,3,2,1,0:T(8,128)S(1)} all-to-all(f32[16,2,2,16,256]{4,3,2,1,0:T(8,128)S(1)} %get-tuple-element.22), channel_id=1, replica_groups={{16,0,30,2,28,4,26,6,24,8,22,10,20,12,18,14},{17,1,31,3,29,5,27,7,25,9,..., dimensions={0} | all-to-all | bytes 2097152 | tf_op jit(solution)/shard_map/all_to_all | solution.py:312
  83.2 0.1 slice_select_fusion.1
  83.2 6.4 %collective-permute-start.2 = (f32[16,2,1,16,256]{4,3,2,1,0:T(8,128)S(1)}, f32[16,2,1,16,256]{4,3,2,1,0:T(8,128)S(1)}, u32[]{:S(2)}, u32[]{:S(2)}) collective-permute-start(f32[16,2,1,16,256]{4,3,2,1,0:T(8,128)S(1)} %slice_select_fusion.1), channel_id=1, source_target_pairs={{0,1},{1,0},{2,3},{3,2},{4,5},{5,4},{6,7},{7,6},{8,9},{9,8},{10,11... | collective-permute-start | bytes 1572872 | tf_op jit(solution)/shard_map/ppermute | solution.py:324
  89.7 0.0 copy-done.3
  89.7 0.0 copy-done.5
  89.7 2.0 %shard_map.58.before = f32[16,2,2,16,256]{4,3,2,1,0:T(8,128)S(1)} custom-call(f32[16,2,2,16,256]{4,3,2,1,0:T(8,128)S(1)} %all_to_all.20.here, bf16[5,256,256]{2,1,0:T(8,128)(2,1)S(1)} %copy-done.3, bf16[5,256,256]{2,1,0:T(8,128)(2,1)S(1)} %copy-done.5), custom_call_target="tpu_custom_call" | custom-call | tf_op jit(solution)/shard_map/pallas_call | solution.py:285
  91.7 0.0 collective-permute-done.2.refs_0_
  91.7 1.6 %shard_map.59 = f32[16,2,2,16,256]{4,3,2,1,0:T(8,128)S(1)} custom-call(s32[3]{0:T(128)S(1)} %pad_add_fusion.place, f32[16,2,2,16,256]{4,3,2,1,0:T(8,128)S(1)} %shard_map.58.before, f32[16,2,1,16,256]{4,3,2,1,0:T(8,128)S(1)} %collective-permute-done.2.refs_0_, bf16[5,256,256]{2,1,0:T(8,128)(2,1)S(1)} %copy-done.3, ...), custom_call_target="tpu_custom_call", output_to_operand_aliasing={{}: (1, {})} | custom-call | tf_op jit(solution)/shard_map/pallas_call | solution.py:285
  93.3 26.7 %all_to_all.21.screened_hat = f32[16,2,2,16,256]{4,3,2,1,0:T(8,128)S(1)} all-to-all(f32[16,2,2,16,256]{4,3,2,1,0:T(8,128)S(1)} %shard_map.59), channel_id=1, replica_groups={{16,0,30,2,28,4,26,6,24,8,22,10,20,12,18,14},{17,1,31,3,29,5,27,7,25,9,..., dimensions={0} | all-to-all | bytes 2097152 | tf_op jit(solution)/shard_map/all_to_all | solution.py:312
  120.0 0.5 shard_map.60
  120.6 0.0 copy-start.1
  120.6 24.7 %all_to_all.22.here = f32[16,2,2,16,256]{4,3,2,1,0:T(8,128)S(1)} all-to-all(f32[16,2,2,16,256]{4,3,2,1,0:T(8,128)S(1)} %shard_map.60), channel_id=1, replica_groups={{16,0,30,2,28,4,26,6,24,8,22,10,20,12,18,14},{17,1,31,3,29,5,27,7,25,9,..., dimensions={0} | all-to-all | bytes 2097152 | tf_op jit(solution)/shard_map/all_to_all | solution.py:312
  145.3 0.1 slice_select_fusion
  145.4 6.4 %collective-permute-start.3 = (f32[16,2,1,16,256]{4,3,2,1,0:T(8,128)S(1)}, f32[16,2,1,16,256]{4,3,2,1,0:T(8,128)S(1)}, u32[]{:S(2)}, u32[]{:S(2)}) collective-permute-start(f32[16,2,1,16,256]{4,3,2,1,0:T(8,128)S(1)} %slice_select_fusion), channel_id=1, source_target_pairs={{0,1},{1,0},{2,3},{3,2},{4,5},{5,4},{6,7},{7,6},{8,9},{9,8},{10,11... | collective-permute-start | bytes 1572872 | tf_op jit(solution)/shard_map/ppermute | solution.py:324
  151.8 0.0 copy-done.1
  151.8 3.1 %shard_map.61.before = f32[2,1,2,256,256]{4,3,2,1,0:T(8,128)S(1)} custom-call(f32[16,2,2,16,256]{4,3,2,1,0:T(8,128)S(1)} %all_to_all.22.here, bf16[2,5,256,256]{3,2,1,0:T(8,128)(2,1)S(1)} %get-tuple-element.25.high.refs_1_, bf16[2,5,256,256]{3,2,1,0:T(8,128)(2,1)S(1)} %copy-done.1), custom_call_target="tpu_custom_call" | custom-call | tf_op jit(solution)/shard_map/pallas_call | solution.py:285
  154.9 0.0 collective-permute-done.3.refs_0_
  154.9 2.3 %shard_map.62 = f32[2,1,2,256,256]{4,3,2,1,0:T(8,128)} custom-call(s32[3]{0:T(128)S(1)} %pad_add_fusion.place, f32[2,1,2,256,256]{4,3,2,1,0:T(8,128)S(1)} %shard_map.61.before, f32[16,2,1,16,256]{4,3,2,1,0:T(8,128)S(1)} %collective-permute-done.3.refs_0_, bf16[2,5,256,256]{3,2,1,0:T(8,128)(2,1)S(1)} %get-tuple-element.25.high.refs_1_, ...), custom_call_target="tpu_custom_call" | custom-call | tf_op jit(solution)/shard_map/pallas_call | solution.py:285
Async XLA Ops:
  2.5 7.8 %copy-start.6 = (f32[2,1,2,256,256]{4,3,2,1,0:T(8,128)S(1)}, f32[2,1,2,256,256]{4,3,2,1,0:T(8,128)}, u32[]{:S(2)}) copy-start(f32[2,1,2,256,256]{4,3,2,1,0:T(8,128)} %refs_3_.1) | copy-start | bytes 3145732
  2.5 44.2 %all-to-all-start = ((f32[16,4,2,16,256]{4,3,2,1,0:T(8,128)}), f32[16,4,2,16,256]{4,3,2,1,0:T(8,128)S(1)}, u32[]{:S(2)}, u32[]{:S(2)}) async-start(f32[16,4,2,16,256]{4,3,2,1,0:T(8,128)} %shard_map.55), calls=%async_computation | async-start | bytes 4194304 | tf_op jit(solution)/shard_map/all_to_all | solution.py:312
  11.1 6.5 %collective-permute-start.1 = (f32[2,256,256]{2,1,0:T(8,128)}, f32[2,256,256]{2,1,0:T(8,128)S(1)}, u32[]{:S(2)}, u32[]{:S(2)}) collective-permute-start(f32[2,256,256]{2,1,0:T(8,128)} %slice_bitcast_fusion), channel_id=1, source_target_pairs={{0,1},{2,3},{4,5},{6,7},{8,9},{10,11},{12,13},{14,15},{16,17},{18,... | collective-permute-start | bytes 1572872 | tf_op jit(solution)/shard_map/ppermute | solution.py:320
  13.3 3.6 %collective-permute-start = (f32[256,256]{1,0:T(8,128)S(1)}, f32[256,256]{1,0:T(8,128)S(1)}, u32[]{:S(2)}, u32[]{:S(2)}) collective-permute-start(f32[256,256]{1,0:T(8,128)S(1)} %slice_bitcast_fusion.1), channel_id=1, source_target_pairs={{0,1},{2,3},{4,5},{6,7},{8,9},{10,11},{12,13},{14,15},{16,17},{18,... | collective-permute-start | bytes 786440 | tf_op jit(solution)/shard_map/ppermute | solution.py:320
  16.9 0.7 copy-start.13
  17.6 0.8 copy-start.11
  18.4 1.2 copy-start.7
  19.6 1.0 copy-start.8
  20.7 1.2 copy-start.9
  21.9 1.0 copy-start.10
  22.9 1.0 copy-start.12
  24.0 0.9 copy-start.14
  26.5 1.1 copy-start
  27.6 0.8 copy-start.2
  28.4 0.8 copy-start.4
  47.3 42.4 %copy-start.3 = (bf16[5,256,256]{2,1,0:T(8,128)(2,1)S(1)}, bf16[5,256,256]{2,1,0:T(8,128)(2,1)}, u32[]{:S(2)}) copy-start(bf16[5,256,256]{2,1,0:T(8,128)(2,1)} %copy-done.2) | copy-start | bytes 1966084
  47.3 42.4 %copy-start.5 = (bf16[5,256,256]{2,1,0:T(8,128)(2,1)S(1)}, bf16[5,256,256]{2,1,0:T(8,128)(2,1)}, u32[]{:S(2)}) copy-start(bf16[5,256,256]{2,1,0:T(8,128)(2,1)} %copy-done.4) | copy-start | bytes 1966084
  83.2 8.5 %collective-permute-start.2 = (f32[16,2,1,16,256]{4,3,2,1,0:T(8,128)S(1)}, f32[16,2,1,16,256]{4,3,2,1,0:T(8,128)S(1)}, u32[]{:S(2)}, u32[]{:S(2)}) collective-permute-start(f32[16,2,1,16,256]{4,3,2,1,0:T(8,128)S(1)} %slice_select_fusion.1), channel_id=1, source_target_pairs={{0,1},{1,0},{2,3},{3,2},{4,5},{5,4},{6,7},{7,6},{8,9},{9,8},{10,11... | collective-permute-start | bytes 1572872 | tf_op jit(solution)/shard_map/ppermute | solution.py:324
  120.6 31.2 %copy-start.1 = (bf16[2,5,256,256]{3,2,1,0:T(8,128)(2,1)S(1)}, bf16[2,5,256,256]{3,2,1,0:T(8,128)(2,1)}, u32[]{:S(2)}) copy-start(bf16[2,5,256,256]{3,2,1,0:T(8,128)(2,1)} %copy-done) | copy-start | bytes 3932164
  145.4 9.6 %collective-permute-start.3 = (f32[16,2,1,16,256]{4,3,2,1,0:T(8,128)S(1)}, f32[16,2,1,16,256]{4,3,2,1,0:T(8,128)S(1)}, u32[]{:S(2)}, u32[]{:S(2)}) collective-permute-start(f32[16,2,1,16,256]{4,3,2,1,0:T(8,128)S(1)} %slice_select_fusion), channel_id=1, source_target_pairs={{0,1},{1,0},{2,3},{3,2},{4,5},{5,4},{6,7},{7,6},{8,9},{9,8},{10,11... | collective-permute-start | bytes 1572872 | tf_op jit(solution)/shard_map/ppermute | solution.py:324

commit v6 on v5

--- a/solution.py
+++ b/solution.py
@@ -202,6 +202,15 @@
     return out_re, out_im
 
 
+def real_term(left, blocks):
+    lanes = left[0].shape[-1]
+    first = parts(product(left, parts(jnp.concatenate(blocks, 1))))
+    count = len(blocks)
+    stacked = tuple(jnp.concatenate([q[:, p * lanes : (p + 1) * lanes] for p in range(count)], 0) for q in first)
+    total = product(stacked, left, True)
+    return [total[p * lanes : (p + 1) * lanes] for p in range(count)]
+
+
 def screen_kernel(here, high, low, out):
     slabs, planes, cells, rows, lanes = here.shape
     for c in range(cells):
@@ -215,8 +224,8 @@
     received, high, low, out = refs[:halos], refs[halos], refs[halos + 1], refs[halos + 2]
     slabs, planes, cells, rows, lanes = out.shape
     for h in range(halos):
-        terms = [(0, 3 * cells - 2 + h)]
-        sums = real_terms(high, low, terms, lambda p, source, h=h: block_of(received[h], p, source), planes)
+        i = 3 * cells - 2 + h
+        sums = real_term((high[i], low[i]), [block_of(received[h], p, 0) for p in range(planes)])
         c = place[2 + h]
         for p, total in enumerate(sums):
             out[:, p, c] = before[:, p, c] + total.reshape(slabs, rows, lanes)
@@ -297,9 +306,7 @@
 
 
 def order_of(devices):
-    middle = devices // 2
-    ends = [e for i in range((devices + 1) // 2) for e in sorted({i, devices - 1 - i})]
-    return [middle] + [e for e in ends if e != middle]
+    return [(e + devices // 2 + 1) % devices for e in range(devices)]
 
 
 def places_of(points):

time: 158 us -> 154 us (0.975)
  starting transfers between devices: 23.2 us -> 16.9 us
  blocking collectives: 87.2 us -> 89.7 us
    ppermute x2, starting transfers between devices: 12.9 us -> 6.62 us  [swapped(): return lax.ppermute(block, 'cell', [(0, 1), (1, 0)])]
    all_to_all x3, blocking collectives: 87.2 us -> 89.7 us  [exchange(): lax.all_to_all(values, 'energy', split_axis=0, concat_axis=0, axis_index_...]
where the time goes in v6:
time: 154 us
  blocking collectives  89.7 us (58%)
  waiting for transfers between devices  20.2 us (13%)
  starting transfers between devices  16.9 us (11%)
  Pallas kernels  13.8 us (9%)
  local copies, waits for them, and re-layouts  12.6 us (8%)
    all_to_all x3, blocking collectives, exchange(): lax.all_to_all(values, 'energy', split_axis=0, concat_axis=0, axis_index_...  89.7 us
    all_to_all x1, waiting for transfers between devices, exchange(): lax.all_to_all(values, 'energy', split_axis=0, concat_axis=0, axis_index_...  18.1 us
    pallas_call x7, Pallas kernels, call(): pl.pallas_call(kernel, out_shape=outs, in_specs=first + [VMEM] * (len(arg...  11.4 us
    unnamed x30, local copies, waits for them, and re-layouts  10.8 us
    all_to_all x1, starting transfers between devices, exchange(): lax.all_to_all(values, 'energy', split_axis=0, concat_axis=0, axis_index_...  7.76 us
    ppermute x2, starting transfers between devices, swapped(): return lax.ppermute(block, 'cell', [(0, 1), (1, 0)])  6.62 us
  transfers between devices with their start and end apart: 5, of which 2 were waited for; matrix products, arithmetic and copies ran while one was open for 1% of the time, Pallas kernels for 4%

profile of v6, /device:TPU:1, one launch (start us, length us, event | category | flops | bytes accessed | tf_op | source)
XLA Modules:
  0.0 153.7 jit_solution(12776256777680051606)
XLA Ops:
  0.0 2.5 %shard_map.55 = f32[16,4,2,16,256]{4,3,2,1,0:T(8,128)} custom-call(f32[4,1,2,256,256]{4,3,2,1,0:T(8,128)} %green.1), custom_call_target="tpu_custom_call" | custom-call | tf_op jit(solution)/shard_map/pallas_call | solution.py:378
  2.5 0.0 copy-start.6
  2.5 7.8 %all-to-all-start = ((f32[16,4,2,16,256]{4,3,2,1,0:T(8,128)}), f32[16,4,2,16,256]{4,3,2,1,0:T(8,128)S(1)}, u32[]{:S(2)}, u32[]{:S(2)}) async-start(f32[16,4,2,16,256]{4,3,2,1,0:T(8,128)} %shard_map.55), calls=%async_computation | async-start | bytes 4194304 | tf_op jit(solution)/shard_map/all_to_all | solution.py:319
  10.2 0.0 copy-done.6
  10.2 0.8 slice_bitcast_fusion
  11.1 1.3 collective-permute-start.1
  12.4 1.0 slice_bitcast_fusion.1
  13.3 1.3 collective-permute-start
  14.6 0.1 pad_add_fusion.place
  14.7 2.2 %collective-permute-done.refs_4_ = f32[256,256]{1,0:T(8,128)S(1)} collective-permute-done((f32[256,256]{1,0:T(8,128)S(1)}, f32[256,256]{1,0:T(8,128)S(1)}, u32[]{:S(2)}, u32[]{:S(2)}) %collective-permute-start) | collective-permute-done | bytes 262176 | tf_op jit(solution)/shard_map/ppermute | solution.py:327
  16.9 0.0 copy-start.13
  16.9 0.7 copy-done.13
  17.6 0.0 collective-permute-done.1.refs_5_
  17.6 0.0 copy-start.11
  17.6 0.8 copy-done.11
  18.4 0.0 copy-start.7
  18.4 1.2 copy-done.7
  19.6 0.0 copy-start.8
  19.6 1.0 copy-done.8
  20.7 0.0 copy-start.9
  20.7 1.2 copy-done.9
  21.9 0.0 copy-start.10
  21.9 1.0 copy-done.10
  22.9 0.0 copy-start.12
  22.9 1.0 copy-done.12
  24.0 0.0 copy-start.14
  24.0 0.9 copy-done.14
  24.9 1.6 %shard_map.56 = (bf16[5,256,256]{2,1,0:T(8,128)(2,1)S(1)}, bf16[5,256,256]{2,1,0:T(8,128)(2,1)S(1)}, bf16[2,5,256,256]{3,2,1,0:T(8,128)(2,1)S(1)}, bf16[2,5,256,256]{3,2,1,0:T(8,128)(2,1)S(1)}) custom-call(s32[3]{0:T(128)S(1)} %pad_add_fusion.place, f32[2,256,256]{2,1,0:T(8,128)S(1)} %copy-done.10, f32[2,256,256]{2,1,0:T(8,128)S(1)} %copy-done.8, ...), custom_call_target="tpu_custom_call" | custom-call | flops 1000000000 | bytes 20971520 | tf_op jit(solution)/shard_map/pallas_call | solution.py:294
  26.5 0.0 copy-start
  26.5 1.1 copy-done
  27.6 0.0 copy-start.2
  27.6 0.8 copy-done.2
  28.4 0.0 copy-start.4
  28.4 0.8 copy-done.4
  29.2 18.1 %all-to-all-done.entries = f32[16,4,2,16,256]{4,3,2,1,0:T(8,128)S(1)} async-done(((f32[16,4,2,16,256]{4,3,2,1,0:T(8,128)}), f32[16,4,2,16,256]{4,3,2,1,0:T(8,128)S(1)}, u32[]{:S(2)}, u32[]{:S(2)}) %all-to-all-start) | async-done | bytes 2097184 | tf_op jit(solution)/shard_map/all_to_all | solution.py:319
  47.3 0.6 shard_map.57
  47.9 0.0 copy-start.3
  47.9 0.0 copy-start.5
  47.9 34.2 %all_to_all.20.here = f32[16,2,2,16,256]{4,3,2,1,0:T(8,128)S(1)} all-to-all(f32[16,2,2,16,256]{4,3,2,1,0:T(8,128)S(1)} %get-tuple-element.22), channel_id=1, replica_groups={{18,20,22,24,26,28,30,0,2,4,6,8,10,12,14,16},{19,21,23,25,27,29,31,1,3,..., dimensions={0} | all-to-all | bytes 2097152 | tf_op jit(solution)/shard_map/all_to_all | solution.py:319
  82.1 0.1 slice_select_fusion.1
  82.2 3.6 %collective-permute-start.2 = (f32[16,2,1,16,256]{4,3,2,1,0:T(8,128)S(1)}, f32[16,2,1,16,256]{4,3,2,1,0:T(8,128)S(1)}, u32[]{:S(2)}, u32[]{:S(2)}) collective-permute-start(f32[16,2,1,16,256]{4,3,2,1,0:T(8,128)S(1)} %slice_select_fusion.1), channel_id=1, source_target_pairs={{0,1},{1,0},{2,3},{3,2},{4,5},{5,4},{6,7},{7,6},{8,9},{9,8},{10,11... | collective-permute-start | bytes 1572872 | tf_op jit(solution)/shard_map/ppermute | solution.py:331
  85.9 0.0 copy-done.3
  85.9 0.0 copy-done.5
  85.9 2.0 %shard_map.58.before = f32[16,2,2,16,256]{4,3,2,1,0:T(8,128)S(1)} custom-call(f32[16,2,2,16,256]{4,3,2,1,0:T(8,128)S(1)} %all_to_all.20.here, bf16[5,256,256]{2,1,0:T(8,128)(2,1)S(1)} %copy-done.3, bf16[5,256,256]{2,1,0:T(8,128)(2,1)S(1)} %copy-done.5), custom_call_target="tpu_custom_call" | custom-call | tf_op jit(solution)/shard_map/pallas_call | solution.py:294
  87.9 0.0 collective-permute-done.2.refs_0_
  87.9 1.2 shard_map.59
  89.1 27.3 %all_to_all.21.screened_hat = f32[16,2,2,16,256]{4,3,2,1,0:T(8,128)S(1)} all-to-all(f32[16,2,2,16,256]{4,3,2,1,0:T(8,128)S(1)} %shard_map.59), channel_id=1, replica_groups={{18,20,22,24,26,28,30,0,2,4,6,8,10,12,14,16},{19,21,23,25,27,29,31,1,3,..., dimensions={0} | all-to-all | bytes 2097152 | tf_op jit(solution)/shard_map/all_to_all | solution.py:319
  116.5 0.5 shard_map.60
  117.0 0.0 copy-start.1
  117.0 28.1 %all_to_all.22.here = f32[16,2,2,16,256]{4,3,2,1,0:T(8,128)S(1)} all-to-all(f32[16,2,2,16,256]{4,3,2,1,0:T(8,128)S(1)} %shard_map.60), channel_id=1, replica_groups={{18,20,22,24,26,28,30,0,2,4,6,8,10,12,14,16},{19,21,23,25,27,29,31,1,3,..., dimensions={0} | all-to-all | bytes 2097152 | tf_op jit(solution)/shard_map/all_to_all | solution.py:319
  145.2 0.1 slice_select_fusion
  145.3 3.0 %collective-permute-start.3 = (f32[16,2,1,16,256]{4,3,2,1,0:T(8,128)S(1)}, f32[16,2,1,16,256]{4,3,2,1,0:T(8,128)S(1)}, u32[]{:S(2)}, u32[]{:S(2)}) collective-permute-start(f32[16,2,1,16,256]{4,3,2,1,0:T(8,128)S(1)} %slice_select_fusion), channel_id=1, source_target_pairs={{0,1},{1,0},{2,3},{3,2},{4,5},{5,4},{6,7},{7,6},{8,9},{9,8},{10,11... | collective-permute-start | bytes 1572872 | tf_op jit(solution)/shard_map/ppermute | solution.py:331
  148.2 0.0 copy-done.1
  148.2 3.1 %shard_map.61.before = f32[2,1,2,256,256]{4,3,2,1,0:T(8,128)S(1)} custom-call(f32[16,2,2,16,256]{4,3,2,1,0:T(8,128)S(1)} %all_to_all.22.here, bf16[2,5,256,256]{3,2,1,0:T(8,128)(2,1)S(1)} %get-tuple-element.25.high.refs_1_, bf16[2,5,256,256]{3,2,1,0:T(8,128)(2,1)S(1)} %copy-done.1), custom_call_target="tpu_custom_call" | custom-call | tf_op jit(solution)/shard_map/pallas_call | solution.py:294
  151.4 0.0 collective-permute-done.3.refs_0_
  151.4 2.3 %shard_map.62 = f32[2,1,2,256,256]{4,3,2,1,0:T(8,128)} custom-call(s32[3]{0:T(128)S(1)} %pad_add_fusion.place, f32[2,1,2,256,256]{4,3,2,1,0:T(8,128)S(1)} %shard_map.61.before, f32[16,2,1,16,256]{4,3,2,1,0:T(8,128)S(1)} %collective-permute-done.3.refs_0_, bf16[2,5,256,256]{3,2,1,0:T(8,128)(2,1)S(1)} %get-tuple-element.25.high.refs_1_, ...), custom_call_target="tpu_custom_call" | custom-call | tf_op jit(solution)/shard_map/pallas_call | solution.py:294
Async XLA Ops:
  2.5 7.8 %copy-start.6 = (f32[2,1,2,256,256]{4,3,2,1,0:T(8,128)S(1)}, f32[2,1,2,256,256]{4,3,2,1,0:T(8,128)}, u32[]{:S(2)}) copy-start(f32[2,1,2,256,256]{4,3,2,1,0:T(8,128)} %refs_3_.1) | copy-start | bytes 3145732
  2.5 44.8 %all-to-all-start = ((f32[16,4,2,16,256]{4,3,2,1,0:T(8,128)}), f32[16,4,2,16,256]{4,3,2,1,0:T(8,128)S(1)}, u32[]{:S(2)}, u32[]{:S(2)}) async-start(f32[16,4,2,16,256]{4,3,2,1,0:T(8,128)} %shard_map.55), calls=%async_computation | async-start | bytes 4194304 | tf_op jit(solution)/shard_map/all_to_all | solution.py:319
  11.1 6.5 %collective-permute-start.1 = (f32[2,256,256]{2,1,0:T(8,128)}, f32[2,256,256]{2,1,0:T(8,128)S(1)}, u32[]{:S(2)}, u32[]{:S(2)}) collective-permute-start(f32[2,256,256]{2,1,0:T(8,128)} %slice_bitcast_fusion), channel_id=1, source_target_pairs={{0,1},{2,3},{4,5},{6,7},{8,9},{10,11},{12,13},{14,15},{16,17},{18,... | collective-permute-start | bytes 1572872 | tf_op jit(solution)/shard_map/ppermute | solution.py:327
  13.3 3.6 %collective-permute-start = (f32[256,256]{1,0:T(8,128)S(1)}, f32[256,256]{1,0:T(8,128)S(1)}, u32[]{:S(2)}, u32[]{:S(2)}) collective-permute-start(f32[256,256]{1,0:T(8,128)S(1)} %slice_bitcast_fusion.1), channel_id=1, source_target_pairs={{0,1},{2,3},{4,5},{6,7},{8,9},{10,11},{12,13},{14,15},{16,17},{18,... | collective-permute-start | bytes 786440 | tf_op jit(solution)/shard_map/ppermute | solution.py:327
  16.9 0.7 copy-start.13
  17.6 0.8 copy-start.11
  18.4 1.2 copy-start.7
  19.6 1.0 copy-start.8
  20.7 1.2 copy-start.9
  21.9 1.0 copy-start.10
  22.9 1.0 copy-start.12
  24.0 0.9 copy-start.14
  26.5 1.1 copy-start
  27.6 0.8 copy-start.2
  28.4 0.8 copy-start.4
  47.9 37.9 %copy-start.3 = (bf16[5,256,256]{2,1,0:T(8,128)(2,1)S(1)}, bf16[5,256,256]{2,1,0:T(8,128)(2,1)}, u32[]{:S(2)}) copy-start(bf16[5,256,256]{2,1,0:T(8,128)(2,1)} %copy-done.2) | copy-start | bytes 1966084
  47.9 37.9 %copy-start.5 = (bf16[5,256,256]{2,1,0:T(8,128)(2,1)S(1)}, bf16[5,256,256]{2,1,0:T(8,128)(2,1)}, u32[]{:S(2)}) copy-start(bf16[5,256,256]{2,1,0:T(8,128)(2,1)} %copy-done.4) | copy-start | bytes 1966084
  82.2 5.7 %collective-permute-start.2 = (f32[16,2,1,16,256]{4,3,2,1,0:T(8,128)S(1)}, f32[16,2,1,16,256]{4,3,2,1,0:T(8,128)S(1)}, u32[]{:S(2)}, u32[]{:S(2)}) collective-permute-start(f32[16,2,1,16,256]{4,3,2,1,0:T(8,128)S(1)} %slice_select_fusion.1), channel_id=1, source_target_pairs={{0,1},{1,0},{2,3},{3,2},{4,5},{5,4},{6,7},{7,6},{8,9},{9,8},{10,11... | collective-permute-start | bytes 1572872 | tf_op jit(solution)/shard_map/ppermute | solution.py:331
  117.0 31.2 %copy-start.1 = (bf16[2,5,256,256]{3,2,1,0:T(8,128)(2,1)S(1)}, bf16[2,5,256,256]{3,2,1,0:T(8,128)(2,1)}, u32[]{:S(2)}) copy-start(bf16[2,5,256,256]{3,2,1,0:T(8,128)(2,1)} %copy-done) | copy-start | bytes 3932164
  145.3 6.1 %collective-permute-start.3 = (f32[16,2,1,16,256]{4,3,2,1,0:T(8,128)S(1)}, f32[16,2,1,16,256]{4,3,2,1,0:T(8,128)S(1)}, u32[]{:S(2)}, u32[]{:S(2)}) collective-permute-start(f32[16,2,1,16,256]{4,3,2,1,0:T(8,128)S(1)} %slice_select_fusion), channel_id=1, source_target_pairs={{0,1},{1,0},{2,3},{3,2},{4,5},{5,4},{6,7},{7,6},{8,9},{9,8},{10,11... | collective-permute-start | bytes 1572872 | tf_op jit(solution)/shard_map/ppermute | solution.py:331

commit v7 on v6

--- a/solution.py
+++ b/solution.py
@@ -185,7 +185,7 @@
     ]
 
 
-def complex_terms(high, low, terms, read):
+def complex_terms(high, low, terms, read, on_real=None):
     out_re, out_im = None, None
     for source, i in terms:
         re, im = ((high[p, i], low[p, i]) for p in range(2))
@@ -196,8 +196,10 @@
         c = product(both, parts(x_re + x_im))
         t_re, t_im = a - b, c - a - b
         a, b = product(parts(t_re), re, True), product(parts(t_im), im, True)
+        out_re = a + b if out_re is None else out_re + (a + b)
+        if on_real is not None and (source, i) == terms[-1]:
+            on_real(out_re)
         c = product(parts(t_re + t_im), apart, True)
-        out_re = a + b if out_re is None else out_re + (a + b)
         out_im = c - a + b if out_im is None else out_im + (c - a + b)
     return out_re, out_im
 
@@ -223,6 +225,12 @@
 def screen_halo_kernel(halos, place, before, *refs):
     received, high, low, out = refs[:halos], refs[halos], refs[halos + 1], refs[halos + 2]
     slabs, planes, cells, rows, lanes = out.shape
+    for c in range(cells):
+
+        @pl.when(untouched(halos, place, c))
+        def _(c=c):
+            out[:, :, c] = before[:, :, c]
+
     for h in range(halos):
         i = 3 * cells - 2 + h
         sums = real_term((high[i], low[i]), [block_of(received[h], p, 0) for p in range(planes)])
@@ -231,6 +239,10 @@
             out[:, p, c] = before[:, p, c] + total.reshape(slabs, rows, lanes)
 
 
+def untouched(halos, place, c):
+    return functools.reduce(jnp.logical_and, [place[2 + h] != c for h in range(halos)])
+
+
 def output_kernel(here, high, low, out):
     cells = here.shape[2]
     for c in range(cells):
@@ -243,40 +255,55 @@
     total, sems = refs[halos + 3 :]
     cells = out.shape[2]
 
-    def touched(c):
-        return functools.reduce(jnp.logical_or, [place[2 + h] == c for h in range(halos)])
-
-    def copy_of(ref, c, i):
-        return pltpu.make_async_copy(ref, out.at[:, :, c], sems.at[i])
+    def copy_of(ref, p, c, i):
+        return pltpu.make_async_copy(ref, out.at[p, 0, c], sems.at[i])
+
+    def kept(c):
+        return [copy_of(before.at[p, 0, c], p, c, 2 * c + p) for p in range(2)]
+
+    def added(h):
+        return [copy_of(total.at[h, p], p, place[2 + h], 2 * (cells + h) + p) for p in range(2)]
 
     for c in range(cells):
 
-        @pl.when(jnp.logical_not(touched(c)))
+        @pl.when(untouched(halos, place, c))
         def _(c=c):
-            copy_of(before.at[:, :, c], c, c).start()
+            for copy in kept(c):
+                copy.start()
 
     for h in range(halos):
         terms = [(0, 3 * cells - 2 + h)]
-        sums = complex_terms(high, low, terms, lambda p, source, h=h: block_of(received[h], p, source))
         c = place[2 + h]
-        for p in range(2):
-            total[h, p, 0] = before[p, 0, c] + sums[p]
-        copy_of(total.at[h], c, cells + h).start()
+
+        def send(p, value, h=h, c=c):
+            total[h, p] = before[p, 0, c] + value
+            added(h)[p].start()
+
+        sums = complex_terms(
+            high,
+            low,
+            terms,
+            lambda p, source, h=h: block_of(received[h], p, source),
+            functools.partial(send, 0),
+        )
+        send(1, sums[1])
     for c in range(cells):
 
-        @pl.when(jnp.logical_not(touched(c)))
+        @pl.when(untouched(halos, place, c))
         def _(c=c):
-            copy_of(before.at[:, :, c], c, c).wait()
+            for copy in kept(c):
+                copy.wait()
 
     for h in range(halos):
-        copy_of(total.at[h], place[2 + h], cells + h).wait()
+        for copy in added(h):
+            copy.wait()
 
 
 def slabs_kernel(green, slabs, stage, sems_in, sems_out):
     devices, planes, cells, rows, lanes = slabs.shape
     blocks = [(p, c) for p in range(planes) for c in range(cells)]
     into = [
-        pltpu.make_async_copy(green.at[p, 0, c].reshape(devices, rows, lanes), stage.at[i], sems_in.at[i])
+        pltpu.make_async_copy(green.at[p, 0, c], stage.at[i], sems_in.at[i])
         for i, (p, c) in enumerate(blocks)
     ]
     out = [pltpu.make_async_copy(stage.at[i], slabs.at[:, p, c], sems_out.at[i]) for i, (p, c) in enumerate(blocks)]
@@ -385,7 +412,7 @@
             pltpu.SemaphoreType.DMA((4 * cells,)),
             pltpu.SemaphoreType.DMA((4 * cells,)),
         ],
-    )(green_pair)
+    )(green_pair.reshape(4, held, cells, devices, rows, orbitals))
     entries, matrices = lax.optimization_barrier((exchange(slabs), matrices))
     coulomb, retarded = matrices[:2], matrices[2:]
     half = shape((points, 2, cells, rows, orbitals))
@@ -402,7 +429,6 @@
             *received,
             *coulomb,
             scalars=True,
-            input_output_aliases={1: 0},
         )
     screened_hat = exchange(screened)
     sigma = exchange(call(functools.partial(convolve_kernel, scaling / points), half, lesser_hat, screened_hat))
@@ -419,8 +445,8 @@
             scalars=True,
             out_specs=ANY,
             scratch_shapes=[
-                pltpu.VMEM((halos, 2, 1, orbitals, orbitals), f32),
-                pltpu.SemaphoreType.DMA((cells + halos,)),
+                pltpu.VMEM((halos, 2, orbitals, orbitals), f32),
+                pltpu.SemaphoreType.DMA((2 * (cells + halos),)),
             ],
         )
     return out

time: 154 us -> 154 us (level)
  no operation moved by 1% of the time
where the time goes in v7:
time: 154 us
  blocking collectives  89.7 us (58%)
  waiting for transfers between devices  20.3 us (13%)
  starting transfers between devices  16.9 us (11%)
  Pallas kernels  13.8 us (9%)
  local copies, waits for them, and re-layouts  12.6 us (8%)
    all_to_all x3, blocking collectives, exchange(): lax.all_to_all(values, 'energy', split_axis=0, concat_axis=0, axis_index_...  89.7 us
    all_to_all x1, waiting for transfers between devices, exchange(): lax.all_to_all(values, 'energy', split_axis=0, concat_axis=0, axis_index_...  18.1 us
    pallas_call x7, Pallas kernels, call(): pl.pallas_call(kernel, out_shape=outs, in_specs=first + [VMEM] * (len(arg...  11.4 us
    unnamed x30, local copies, waits for them, and re-layouts  10.8 us
    all_to_all x1, starting transfers between devices, exchange(): lax.all_to_all(values, 'energy', split_axis=0, concat_axis=0, axis_index_...  7.76 us
    ppermute x2, starting transfers between devices, swapped(): return lax.ppermute(block, 'cell', [(0, 1), (1, 0)])  6.62 us
  transfers between devices with their start and end apart: 5, of which 2 were waited for; matrix products, arithmetic and copies ran while one was open for 1% of the time, Pallas kernels for 4%

profile of v7, /device:TPU:1, one launch (start us, length us, event | category | flops | bytes accessed | tf_op | source)
XLA Modules:
  0.0 153.7 jit_solution(17276796976373967727)
XLA Ops:
  0.0 2.5 %shard_map.55 = f32[16,4,2,16,256]{4,3,2,1,0:T(8,128)} custom-call(f32[4,1,2,16,16,256]{5,4,3,2,1,0:T(8,128)} %bitcast.9), custom_call_target="tpu_custom_call" | custom-call | tf_op jit(solution)/shard_map/pallas_call | solution.py:405
  2.5 0.0 copy-start.6
  2.5 7.8 %all-to-all-start = ((f32[16,4,2,16,256]{4,3,2,1,0:T(8,128)}), f32[16,4,2,16,256]{4,3,2,1,0:T(8,128)S(1)}, u32[]{:S(2)}, u32[]{:S(2)}) async-start(f32[16,4,2,16,256]{4,3,2,1,0:T(8,128)} %shard_map.55), calls=%async_computation | async-start | bytes 4194304 | tf_op jit(solution)/shard_map/all_to_all | solution.py:346
  10.2 0.0 copy-done.6
  10.2 0.8 slice_bitcast_fusion
  11.1 1.3 collective-permute-start.1
  12.4 1.0 slice_bitcast_fusion.1
  13.3 1.3 collective-permute-start
  14.6 0.1 pad_add_fusion.place
  14.7 2.2 %collective-permute-done.refs_4_ = f32[256,256]{1,0:T(8,128)S(1)} collective-permute-done((f32[256,256]{1,0:T(8,128)S(1)}, f32[256,256]{1,0:T(8,128)S(1)}, u32[]{:S(2)}, u32[]{:S(2)}) %collective-permute-start) | collective-permute-done | bytes 262176 | tf_op jit(solution)/shard_map/ppermute | solution.py:354
  16.9 0.0 copy-start.13
  16.9 0.7 copy-done.13
  17.6 0.0 collective-permute-done.1.refs_5_
  17.6 0.0 copy-start.11
  17.6 0.8 copy-done.11
  18.4 0.0 copy-start.7
  18.4 1.2 copy-done.7
  19.6 0.0 copy-start.8
  19.6 1.0 copy-done.8
  20.7 0.0 copy-start.9
  20.7 1.2 copy-done.9
  21.9 0.0 copy-start.10
  21.9 1.0 copy-done.10
  22.9 0.0 copy-start.12
  22.9 1.0 copy-done.12
  24.0 0.0 copy-start.14
  24.0 0.9 copy-done.14
  24.9 1.5 shard_map.56
  26.4 0.0 copy-start
  26.5 1.1 copy-done
  27.5 0.0 copy-start.2
  27.5 0.8 copy-done.2
  28.4 0.0 copy-start.4
  28.4 0.8 copy-done.4
  29.2 18.1 %all-to-all-done.entries = f32[16,4,2,16,256]{4,3,2,1,0:T(8,128)S(1)} async-done(((f32[16,4,2,16,256]{4,3,2,1,0:T(8,128)}), f32[16,4,2,16,256]{4,3,2,1,0:T(8,128)S(1)}, u32[]{:S(2)}, u32[]{:S(2)}) %all-to-all-start) | async-done | bytes 2097184 | tf_op jit(solution)/shard_map/all_to_all | solution.py:346
  47.3 0.6 shard_map.57
  47.9 0.0 copy-start.3
  47.9 0.0 copy-start.5
  47.9 34.2 %all_to_all.20.here = f32[16,2,2,16,256]{4,3,2,1,0:T(8,128)S(1)} all-to-all(f32[16,2,2,16,256]{4,3,2,1,0:T(8,128)S(1)} %get-tuple-element.22), channel_id=1, replica_groups={{18,20,22,24,26,28,30,0,2,4,6,8,10,12,14,16},{19,21,23,25,27,29,31,1,3,..., dimensions={0} | all-to-all | bytes 2097152 | tf_op jit(solution)/shard_map/all_to_all | solution.py:346
  82.1 0.1 slice_select_fusion.1
  82.2 3.6 %collective-permute-start.2 = (f32[16,2,1,16,256]{4,3,2,1,0:T(8,128)S(1)}, f32[16,2,1,16,256]{4,3,2,1,0:T(8,128)S(1)}, u32[]{:S(2)}, u32[]{:S(2)}) collective-permute-start(f32[16,2,1,16,256]{4,3,2,1,0:T(8,128)S(1)} %slice_select_fusion.1), channel_id=1, source_target_pairs={{0,1},{1,0},{2,3},{3,2},{4,5},{5,4},{6,7},{7,6},{8,9},{9,8},{10,11... | collective-permute-start | bytes 1572872 | tf_op jit(solution)/shard_map/ppermute | solution.py:358
  85.8 0.0 copy-done.3
  85.9 0.0 copy-done.5
  85.9 2.0 %shard_map.58.before = f32[16,2,2,16,256]{4,3,2,1,0:T(8,128)S(1)} custom-call(f32[16,2,2,16,256]{4,3,2,1,0:T(8,128)S(1)} %all_to_all.20.here, bf16[5,256,256]{2,1,0:T(8,128)(2,1)S(1)} %copy-done.3, bf16[5,256,256]{2,1,0:T(8,128)(2,1)S(1)} %copy-done.5), custom_call_target="tpu_custom_call" | custom-call | tf_op jit(solution)/shard_map/pallas_call | solution.py:321
  87.9 0.0 collective-permute-done.2.refs_0_
  87.9 1.3 shard_map.59
  89.2 27.3 %all_to_all.21.screened_hat = f32[16,2,2,16,256]{4,3,2,1,0:T(8,128)S(1)} all-to-all(f32[16,2,2,16,256]{4,3,2,1,0:T(8,128)S(1)} %shard_map.59), channel_id=1, replica_groups={{18,20,22,24,26,28,30,0,2,4,6,8,10,12,14,16},{19,21,23,25,27,29,31,1,3,..., dimensions={0} | all-to-all | bytes 2097152 | tf_op jit(solution)/shard_map/all_to_all | solution.py:346
  116.5 0.5 shard_map.60
  117.0 0.0 copy-start.1
  117.0 28.1 %all_to_all.22.here = f32[16,2,2,16,256]{4,3,2,1,0:T(8,128)S(1)} all-to-all(f32[16,2,2,16,256]{4,3,2,1,0:T(8,128)S(1)} %shard_map.60), channel_id=1, replica_groups={{18,20,22,24,26,28,30,0,2,4,6,8,10,12,14,16},{19,21,23,25,27,29,31,1,3,..., dimensions={0} | all-to-all | bytes 2097152 | tf_op jit(solution)/shard_map/all_to_all | solution.py:346
  145.2 0.1 slice_select_fusion
  145.3 3.0 %collective-permute-start.3 = (f32[16,2,1,16,256]{4,3,2,1,0:T(8,128)S(1)}, f32[16,2,1,16,256]{4,3,2,1,0:T(8,128)S(1)}, u32[]{:S(2)}, u32[]{:S(2)}) collective-permute-start(f32[16,2,1,16,256]{4,3,2,1,0:T(8,128)S(1)} %slice_select_fusion), channel_id=1, source_target_pairs={{0,1},{1,0},{2,3},{3,2},{4,5},{5,4},{6,7},{7,6},{8,9},{9,8},{10,11... | collective-permute-start | bytes 1572872 | tf_op jit(solution)/shard_map/ppermute | solution.py:358
  148.3 0.0 copy-done.1
  148.3 3.1 %shard_map.61.before = f32[2,1,2,256,256]{4,3,2,1,0:T(8,128)S(1)} custom-call(f32[16,2,2,16,256]{4,3,2,1,0:T(8,128)S(1)} %all_to_all.22.here, bf16[2,5,256,256]{3,2,1,0:T(8,128)(2,1)S(1)} %get-tuple-element.25.high.refs_1_, bf16[2,5,256,256]{3,2,1,0:T(8,128)(2,1)S(1)} %copy-done.1), custom_call_target="tpu_custom_call" | custom-call | tf_op jit(solution)/shard_map/pallas_call | solution.py:321
  151.4 0.0 collective-permute-done.3.refs_0_
  151.4 2.3 %shard_map.62 = f32[2,1,2,256,256]{4,3,2,1,0:T(8,128)} custom-call(s32[3]{0:T(128)S(1)} %pad_add_fusion.place, f32[2,1,2,256,256]{4,3,2,1,0:T(8,128)S(1)} %shard_map.61.before, f32[16,2,1,16,256]{4,3,2,1,0:T(8,128)S(1)} %collective-permute-done.3.refs_0_, bf16[2,5,256,256]{3,2,1,0:T(8,128)(2,1)S(1)} %get-tuple-element.25.high.refs_1_, ...), custom_call_target="tpu_custom_call" | custom-call | tf_op jit(solution)/shard_map/pallas_call | solution.py:321
Async XLA Ops:
  2.5 7.8 %copy-start.6 = (f32[2,1,2,256,256]{4,3,2,1,0:T(8,128)S(1)}, f32[2,1,2,256,256]{4,3,2,1,0:T(8,128)}, u32[]{:S(2)}) copy-start(f32[2,1,2,256,256]{4,3,2,1,0:T(8,128)} %refs_3_.1) | copy-start | bytes 3145732
  2.5 44.8 %all-to-all-start = ((f32[16,4,2,16,256]{4,3,2,1,0:T(8,128)}), f32[16,4,2,16,256]{4,3,2,1,0:T(8,128)S(1)}, u32[]{:S(2)}, u32[]{:S(2)}) async-start(f32[16,4,2,16,256]{4,3,2,1,0:T(8,128)} %shard_map.55), calls=%async_computation | async-start | bytes 4194304 | tf_op jit(solution)/shard_map/all_to_all | solution.py:346
  11.1 6.5 %collective-permute-start.1 = (f32[2,256,256]{2,1,0:T(8,128)}, f32[2,256,256]{2,1,0:T(8,128)S(1)}, u32[]{:S(2)}, u32[]{:S(2)}) collective-permute-start(f32[2,256,256]{2,1,0:T(8,128)} %slice_bitcast_fusion), channel_id=1, source_target_pairs={{0,1},{2,3},{4,5},{6,7},{8,9},{10,11},{12,13},{14,15},{16,17},{18,... | collective-permute-start | bytes 1572872 | tf_op jit(solution)/shard_map/ppermute | solution.py:354
  13.3 3.6 %collective-permute-start = (f32[256,256]{1,0:T(8,128)S(1)}, f32[256,256]{1,0:T(8,128)S(1)}, u32[]{:S(2)}, u32[]{:S(2)}) collective-permute-start(f32[256,256]{1,0:T(8,128)S(1)} %slice_bitcast_fusion.1), channel_id=1, source_target_pairs={{0,1},{2,3},{4,5},{6,7},{8,9},{10,11},{12,13},{14,15},{16,17},{18,... | collective-permute-start | bytes 786440 | tf_op jit(solution)/shard_map/ppermute | solution.py:354
  16.9 0.7 copy-start.13
  17.6 0.8 copy-start.11
  18.4 1.2 copy-start.7
  19.6 1.0 copy-start.8
  20.7 1.2 copy-start.9
  21.9 1.0 copy-start.10
  22.9 1.0 copy-start.12
  24.0 0.9 copy-start.14
  26.4 1.1 copy-start
  27.5 0.8 copy-start.2
  28.4 0.8 copy-start.4
  47.9 37.9 %copy-start.3 = (bf16[5,256,256]{2,1,0:T(8,128)(2,1)S(1)}, bf16[5,256,256]{2,1,0:T(8,128)(2,1)}, u32[]{:S(2)}) copy-start(bf16[5,256,256]{2,1,0:T(8,128)(2,1)} %copy-done.2) | copy-start | bytes 1966084
  47.9 37.9 %copy-start.5 = (bf16[5,256,256]{2,1,0:T(8,128)(2,1)S(1)}, bf16[5,256,256]{2,1,0:T(8,128)(2,1)}, u32[]{:S(2)}) copy-start(bf16[5,256,256]{2,1,0:T(8,128)(2,1)} %copy-done.4) | copy-start | bytes 1966084
  82.2 5.6 %collective-permute-start.2 = (f32[16,2,1,16,256]{4,3,2,1,0:T(8,128)S(1)}, f32[16,2,1,16,256]{4,3,2,1,0:T(8,128)S(1)}, u32[]{:S(2)}, u32[]{:S(2)}) collective-permute-start(f32[16,2,1,16,256]{4,3,2,1,0:T(8,128)S(1)} %slice_select_fusion.1), channel_id=1, source_target_pairs={{0,1},{1,0},{2,3},{3,2},{4,5},{5,4},{6,7},{7,6},{8,9},{9,8},{10,11... | collective-permute-start | bytes 1572872 | tf_op jit(solution)/shard_map/ppermute | solution.py:358
  117.0 31.2 %copy-start.1 = (bf16[2,5,256,256]{3,2,1,0:T(8,128)(2,1)S(1)}, bf16[2,5,256,256]{3,2,1,0:T(8,128)(2,1)}, u32[]{:S(2)}) copy-start(bf16[2,5,256,256]{3,2,1,0:T(8,128)(2,1)} %copy-done) | copy-start | bytes 3932164
  145.3 6.1 %collective-permute-start.3 = (f32[16,2,1,16,256]{4,3,2,1,0:T(8,128)S(1)}, f32[16,2,1,16,256]{4,3,2,1,0:T(8,128)S(1)}, u32[]{:S(2)}, u32[]{:S(2)}) collective-permute-start(f32[16,2,1,16,256]{4,3,2,1,0:T(8,128)S(1)} %slice_select_fusion), channel_id=1, source_target_pairs={{0,1},{1,0},{2,3},{3,2},{4,5},{5,4},{6,7},{7,6},{8,9},{9,8},{10,11... | collective-permute-start | bytes 1572872 | tf_op jit(solution)/shard_map/ppermute | solution.py:358

commit v8 on v7

--- a/solution.py
+++ b/solution.py
@@ -323,7 +323,7 @@
         out_shape=outs,
         in_specs=first + [VMEM] * (len(args) - len(first)),
         out_specs=out_specs or jax.tree.map(lambda _: VMEM, outs),
-        compiler_params=pltpu.CompilerParams(vmem_limit_bytes=16 * 1024 * 1024),
+        compiler_params=pltpu.CompilerParams(vmem_limit_bytes=32 * 1024 * 1024),
         **more,
     )(*args)
 

time: 154 us -> 154 us (level)
  no operation moved by 1% of the time
where the time goes in v8:
time: 154 us
  blocking collectives  89.7 us (58%)
  waiting for transfers between devices  20.3 us (13%)
  starting transfers between devices  16.9 us (11%)
  Pallas kernels  13.8 us (9%)
  local copies, waits for them, and re-layouts  12.6 us (8%)
    all_to_all x3, blocking collectives, exchange(): lax.all_to_all(values, 'energy', split_axis=0, concat_axis=0, axis_index_...  89.7 us
    all_to_all x1, waiting for transfers between devices, exchange(): lax.all_to_all(values, 'energy', split_axis=0, concat_axis=0, axis_index_...  18.1 us
    pallas_call x7, Pallas kernels, call(): pl.pallas_call(kernel, out_shape=outs, in_specs=first + [VMEM] * (len(arg...  11.4 us
    unnamed x30, local copies, waits for them, and re-layouts  10.8 us
    all_to_all x1, starting transfers between devices, exchange(): lax.all_to_all(values, 'energy', split_axis=0, concat_axis=0, axis_index_...  7.76 us
    ppermute x2, starting transfers between devices, swapped(): return lax.ppermute(block, 'cell', [(0, 1), (1, 0)])  6.62 us
  transfers between devices with their start and end apart: 5, of which 2 were waited for; matrix products, arithmetic and copies ran while one was open for 1% of the time, Pallas kernels for 4%

profile of v8, /device:TPU:1, one launch (start us, length us, event | category | flops | bytes accessed | tf_op | source)
XLA Modules:
  0.0 153.7 jit_solution(5286802362388026686)
XLA Ops:
  0.0 2.5 %shard_map.55 = f32[16,4,2,16,256]{4,3,2,1,0:T(8,128)} custom-call(f32[4,1,2,16,16,256]{5,4,3,2,1,0:T(8,128)} %bitcast.9), custom_call_target="tpu_custom_call" | custom-call | tf_op jit(solution)/shard_map/pallas_call | solution.py:405
  2.5 0.0 copy-start.6
  2.5 7.8 %all-to-all-start = ((f32[16,4,2,16,256]{4,3,2,1,0:T(8,128)}), f32[16,4,2,16,256]{4,3,2,1,0:T(8,128)S(1)}, u32[]{:S(2)}, u32[]{:S(2)}) async-start(f32[16,4,2,16,256]{4,3,2,1,0:T(8,128)} %shard_map.55), calls=%async_computation | async-start | bytes 4194304 | tf_op jit(solution)/shard_map/all_to_all | solution.py:346
  10.2 0.0 copy-done.6
  10.2 0.8 slice_bitcast_fusion
  11.1 1.3 collective-permute-start.1
  12.4 1.0 slice_bitcast_fusion.1
  13.3 1.3 collective-permute-start
  14.6 0.1 pad_add_fusion.place
  14.7 2.2 %collective-permute-done.refs_4_ = f32[256,256]{1,0:T(8,128)S(1)} collective-permute-done((f32[256,256]{1,0:T(8,128)S(1)}, f32[256,256]{1,0:T(8,128)S(1)}, u32[]{:S(2)}, u32[]{:S(2)}) %collective-permute-start) | collective-permute-done | bytes 262176 | tf_op jit(solution)/shard_map/ppermute | solution.py:354
  16.9 0.0 copy-start.13
  16.9 0.7 copy-done.13
  17.6 0.0 collective-permute-done.1.refs_5_
  17.6 0.0 copy-start.11
  17.6 0.8 copy-done.11
  18.4 0.0 copy-start.7
  18.4 1.2 copy-done.7
  19.6 0.0 copy-start.8
  19.6 1.0 copy-done.8
  20.7 0.0 copy-start.9
  20.7 1.2 copy-done.9
  21.9 0.0 copy-start.10
  21.9 1.0 copy-done.10
  22.9 0.0 copy-start.12
  22.9 1.0 copy-done.12
  24.0 0.0 copy-start.14
  24.0 0.9 copy-done.14
  24.9 1.5 shard_map.56
  26.4 0.0 copy-start
  26.5 1.1 copy-done
  27.5 0.0 copy-start.2
  27.5 0.8 copy-done.2
  28.4 0.0 copy-start.4
  28.4 0.8 copy-done.4
  29.2 18.1 %all-to-all-done.entries = f32[16,4,2,16,256]{4,3,2,1,0:T(8,128)S(1)} async-done(((f32[16,4,2,16,256]{4,3,2,1,0:T(8,128)}), f32[16,4,2,16,256]{4,3,2,1,0:T(8,128)S(1)}, u32[]{:S(2)}, u32[]{:S(2)}) %all-to-all-start) | async-done | bytes 2097184 | tf_op jit(solution)/shard_map/all_to_all | solution.py:346
  47.3 0.6 shard_map.57
  47.9 0.0 copy-start.3
  47.9 0.0 copy-start.5
  47.9 34.2 %all_to_all.20.here = f32[16,2,2,16,256]{4,3,2,1,0:T(8,128)S(1)} all-to-all(f32[16,2,2,16,256]{4,3,2,1,0:T(8,128)S(1)} %get-tuple-element.22), channel_id=1, replica_groups={{18,20,22,24,26,28,30,0,2,4,6,8,10,12,14,16},{19,21,23,25,27,29,31,1,3,..., dimensions={0} | all-to-all | bytes 2097152 | tf_op jit(solution)/shard_map/all_to_all | solution.py:346
  82.1 0.1 slice_select_fusion.1
  82.2 3.6 %collective-permute-start.2 = (f32[16,2,1,16,256]{4,3,2,1,0:T(8,128)S(1)}, f32[16,2,1,16,256]{4,3,2,1,0:T(8,128)S(1)}, u32[]{:S(2)}, u32[]{:S(2)}) collective-permute-start(f32[16,2,1,16,256]{4,3,2,1,0:T(8,128)S(1)} %slice_select_fusion.1), channel_id=1, source_target_pairs={{0,1},{1,0},{2,3},{3,2},{4,5},{5,4},{6,7},{7,6},{8,9},{9,8},{10,11... | collective-permute-start | bytes 1572872 | tf_op jit(solution)/shard_map/ppermute | solution.py:358
  85.8 0.0 copy-done.3
  85.9 0.0 copy-done.5
  85.9 2.0 %shard_map.58.before = f32[16,2,2,16,256]{4,3,2,1,0:T(8,128)S(1)} custom-call(f32[16,2,2,16,256]{4,3,2,1,0:T(8,128)S(1)} %all_to_all.20.here, bf16[5,256,256]{2,1,0:T(8,128)(2,1)S(1)} %copy-done.3, bf16[5,256,256]{2,1,0:T(8,128)(2,1)S(1)} %copy-done.5), custom_call_target="tpu_custom_call" | custom-call | tf_op jit(solution)/shard_map/pallas_call | solution.py:321
  87.9 0.0 collective-permute-done.2.refs_0_
  87.9 1.3 shard_map.59
  89.2 27.3 %all_to_all.21.screened_hat = f32[16,2,2,16,256]{4,3,2,1,0:T(8,128)S(1)} all-to-all(f32[16,2,2,16,256]{4,3,2,1,0:T(8,128)S(1)} %shard_map.59), channel_id=1, replica_groups={{18,20,22,24,26,28,30,0,2,4,6,8,10,12,14,16},{19,21,23,25,27,29,31,1,3,..., dimensions={0} | all-to-all | bytes 2097152 | tf_op jit(solution)/shard_map/all_to_all | solution.py:346
  116.5 0.5 shard_map.60
  117.0 0.0 copy-start.1
  117.0 28.1 %all_to_all.22.here = f32[16,2,2,16,256]{4,3,2,1,0:T(8,128)S(1)} all-to-all(f32[16,2,2,16,256]{4,3,2,1,0:T(8,128)S(1)} %shard_map.60), channel_id=1, replica_groups={{18,20,22,24,26,28,30,0,2,4,6,8,10,12,14,16},{19,21,23,25,27,29,31,1,3,..., dimensions={0} | all-to-all | bytes 2097152 | tf_op jit(solution)/shard_map/all_to_all | solution.py:346
  145.2 0.1 slice_select_fusion
  145.3 3.0 %collective-permute-start.3 = (f32[16,2,1,16,256]{4,3,2,1,0:T(8,128)S(1)}, f32[16,2,1,16,256]{4,3,2,1,0:T(8,128)S(1)}, u32[]{:S(2)}, u32[]{:S(2)}) collective-permute-start(f32[16,2,1,16,256]{4,3,2,1,0:T(8,128)S(1)} %slice_select_fusion), channel_id=1, source_target_pairs={{0,1},{1,0},{2,3},{3,2},{4,5},{5,4},{6,7},{7,6},{8,9},{9,8},{10,11... | collective-permute-start | bytes 1572872 | tf_op jit(solution)/shard_map/ppermute | solution.py:358
  148.3 0.0 copy-done.1
  148.3 3.1 %shard_map.61.before = f32[2,1,2,256,256]{4,3,2,1,0:T(8,128)S(1)} custom-call(f32[16,2,2,16,256]{4,3,2,1,0:T(8,128)S(1)} %all_to_all.22.here, bf16[2,5,256,256]{3,2,1,0:T(8,128)(2,1)S(1)} %get-tuple-element.25.high.refs_1_, bf16[2,5,256,256]{3,2,1,0:T(8,128)(2,1)S(1)} %copy-done.1), custom_call_target="tpu_custom_call" | custom-call | tf_op jit(solution)/shard_map/pallas_call | solution.py:321
  151.4 0.0 collective-permute-done.3.refs_0_
  151.4 2.3 %shard_map.62 = f32[2,1,2,256,256]{4,3,2,1,0:T(8,128)} custom-call(s32[3]{0:T(128)S(1)} %pad_add_fusion.place, f32[2,1,2,256,256]{4,3,2,1,0:T(8,128)S(1)} %shard_map.61.before, f32[16,2,1,16,256]{4,3,2,1,0:T(8,128)S(1)} %collective-permute-done.3.refs_0_, bf16[2,5,256,256]{3,2,1,0:T(8,128)(2,1)S(1)} %get-tuple-element.25.high.refs_1_, ...), custom_call_target="tpu_custom_call" | custom-call | tf_op jit(solution)/shard_map/pallas_call | solution.py:321
Async XLA Ops:
  2.5 7.8 %copy-start.6 = (f32[2,1,2,256,256]{4,3,2,1,0:T(8,128)S(1)}, f32[2,1,2,256,256]{4,3,2,1,0:T(8,128)}, u32[]{:S(2)}) copy-start(f32[2,1,2,256,256]{4,3,2,1,0:T(8,128)} %refs_3_.1) | copy-start | bytes 3145732
  2.5 44.8 %all-to-all-start = ((f32[16,4,2,16,256]{4,3,2,1,0:T(8,128)}), f32[16,4,2,16,256]{4,3,2,1,0:T(8,128)S(1)}, u32[]{:S(2)}, u32[]{:S(2)}) async-start(f32[16,4,2,16,256]{4,3,2,1,0:T(8,128)} %shard_map.55), calls=%async_computation | async-start | bytes 4194304 | tf_op jit(solution)/shard_map/all_to_all | solution.py:346
  11.1 6.5 %collective-permute-start.1 = (f32[2,256,256]{2,1,0:T(8,128)}, f32[2,256,256]{2,1,0:T(8,128)S(1)}, u32[]{:S(2)}, u32[]{:S(2)}) collective-permute-start(f32[2,256,256]{2,1,0:T(8,128)} %slice_bitcast_fusion), channel_id=1, source_target_pairs={{0,1},{2,3},{4,5},{6,7},{8,9},{10,11},{12,13},{14,15},{16,17},{18,... | collective-permute-start | bytes 1572872 | tf_op jit(solution)/shard_map/ppermute | solution.py:354
  13.3 3.6 %collective-permute-start = (f32[256,256]{1,0:T(8,128)S(1)}, f32[256,256]{1,0:T(8,128)S(1)}, u32[]{:S(2)}, u32[]{:S(2)}) collective-permute-start(f32[256,256]{1,0:T(8,128)S(1)} %slice_bitcast_fusion.1), channel_id=1, source_target_pairs={{0,1},{2,3},{4,5},{6,7},{8,9},{10,11},{12,13},{14,15},{16,17},{18,... | collective-permute-start | bytes 786440 | tf_op jit(solution)/shard_map/ppermute | solution.py:354
  16.9 0.7 copy-start.13
  17.6 0.8 copy-start.11
  18.4 1.2 copy-start.7
  19.6 1.0 copy-start.8
  20.7 1.2 copy-start.9
  21.9 1.0 copy-start.10
  22.9 1.0 copy-start.12
  24.0 0.9 copy-start.14
  26.4 1.1 copy-start
  27.5 0.8 copy-start.2
  28.4 0.8 copy-start.4
  47.9 37.9 %copy-start.3 = (bf16[5,256,256]{2,1,0:T(8,128)(2,1)S(1)}, bf16[5,256,256]{2,1,0:T(8,128)(2,1)}, u32[]{:S(2)}) copy-start(bf16[5,256,256]{2,1,0:T(8,128)(2,1)} %copy-done.2) | copy-start | bytes 1966084
  47.9 37.9 %copy-start.5 = (bf16[5,256,256]{2,1,0:T(8,128)(2,1)S(1)}, bf16[5,256,256]{2,1,0:T(8,128)(2,1)}, u32[]{:S(2)}) copy-start(bf16[5,256,256]{2,1,0:T(8,128)(2,1)} %copy-done.4) | copy-start | bytes 1966084
  82.2 5.6 %collective-permute-start.2 = (f32[16,2,1,16,256]{4,3,2,1,0:T(8,128)S(1)}, f32[16,2,1,16,256]{4,3,2,1,0:T(8,128)S(1)}, u32[]{:S(2)}, u32[]{:S(2)}) collective-permute-start(f32[16,2,1,16,256]{4,3,2,1,0:T(8,128)S(1)} %slice_select_fusion.1), channel_id=1, source_target_pairs={{0,1},{1,0},{2,3},{3,2},{4,5},{5,4},{6,7},{7,6},{8,9},{9,8},{10,11... | collective-permute-start | bytes 1572872 | tf_op jit(solution)/shard_map/ppermute | solution.py:358
  117.0 31.2 %copy-start.1 = (bf16[2,5,256,256]{3,2,1,0:T(8,128)(2,1)S(1)}, bf16[2,5,256,256]{3,2,1,0:T(8,128)(2,1)}, u32[]{:S(2)}) copy-start(bf16[2,5,256,256]{3,2,1,0:T(8,128)(2,1)} %copy-done) | copy-start | bytes 3932164
  145.3 6.1 %collective-permute-start.3 = (f32[16,2,1,16,256]{4,3,2,1,0:T(8,128)S(1)}, f32[16,2,1,16,256]{4,3,2,1,0:T(8,128)S(1)}, u32[]{:S(2)}, u32[]{:S(2)}) collective-permute-start(f32[16,2,1,16,256]{4,3,2,1,0:T(8,128)S(1)} %slice_select_fusion), channel_id=1, source_target_pairs={{0,1},{1,0},{2,3},{3,2},{4,5},{5,4},{6,7},{7,6},{8,9},{9,8},{10,11... | collective-permute-start | bytes 1572872 | tf_op jit(solution)/shard_map/ppermute | solution.py:358

commit v9 on v7

--- a/solution.py
+++ b/solution.py
@@ -259,17 +259,16 @@
         return pltpu.make_async_copy(ref, out.at[p, 0, c], sems.at[i])
 
     def kept(c):
-        return [copy_of(before.at[p, 0, c], p, c, 2 * c + p) for p in range(2)]
-
-    def added(h):
-        return [copy_of(total.at[h, p], p, place[2 + h], 2 * (cells + h) + p) for p in range(2)]
+        return pltpu.make_async_copy(before.at[:, :, c], out.at[:, :, c], sems.at[c])
+
+    def added(h, p):
+        return copy_of(total.at[h, p], p, place[2 + h], cells + 2 * h + p)
 
     for c in range(cells):
 
         @pl.when(untouched(halos, place, c))
         def _(c=c):
-            for copy in kept(c):
-                copy.start()
+            kept(c).start()
 
     for h in range(halos):
         terms = [(0, 3 * cells - 2 + h)]
@@ -277,7 +276,7 @@
 
         def send(p, value, h=h, c=c):
             total[h, p] = before[p, 0, c] + value
-            added(h)[p].start()
+            added(h, p).start()
 
         sums = complex_terms(
             high,
@@ -291,12 +290,11 @@
 
         @pl.when(untouched(halos, place, c))
         def _(c=c):
-            for copy in kept(c):
-                copy.wait()
+            kept(c).wait()
 
     for h in range(halos):
-        for copy in added(h):
-            copy.wait()
+        for p in range(2):
+            added(h, p).wait()
 
 
 def slabs_kernel(green, slabs, stage, sems_in, sems_out):
@@ -446,7 +444,7 @@
             out_specs=ANY,
             scratch_shapes=[
                 pltpu.VMEM((halos, 2, orbitals, orbitals), f32),
-                pltpu.SemaphoreType.DMA((2 * (cells + halos),)),
+                pltpu.SemaphoreType.DMA((cells + 2 * halos,)),
             ],
         )
     return out

time: 154 us -> 154 us (level)
  no operation moved by 1% of the time
where the time goes in v9:
time: 154 us
  blocking collectives  89.7 us (58%)
  waiting for transfers between devices  20.3 us (13%)
  starting transfers between devices  16.9 us (11%)
  Pallas kernels  13.8 us (9%)
  local copies, waits for them, and re-layouts  12.6 us (8%)
    all_to_all x3, blocking collectives, exchange(): lax.all_to_all(values, 'energy', split_axis=0, concat_axis=0, axis_index_...  89.7 us
    all_to_all x1, waiting for transfers between devices, exchange(): lax.all_to_all(values, 'energy', split_axis=0, concat_axis=0, axis_index_...  18.1 us
    pallas_call x7, Pallas kernels, call(): pl.pallas_call(kernel, out_shape=outs, in_specs=first + [VMEM] * (len(arg...  11.3 us
    unnamed x30, local copies, waits for them, and re-layouts  10.8 us
    all_to_all x1, starting transfers between devices, exchange(): lax.all_to_all(values, 'energy', split_axis=0, concat_axis=0, axis_index_...  7.76 us
    ppermute x2, starting transfers between devices, swapped(): return lax.ppermute(block, 'cell', [(0, 1), (1, 0)])  6.62 us
  transfers between devices with their start and end apart: 5, of which 2 were waited for; matrix products, arithmetic and copies ran while one was open for 1% of the time, Pallas kernels for 4%

profile of v9, /device:TPU:1, one launch (start us, length us, event | category | flops | bytes accessed | tf_op | source)
XLA Modules:
  0.0 153.7 jit_solution(11577613549757701585)
XLA Ops:
  0.0 2.5 %shard_map.55 = f32[16,4,2,16,256]{4,3,2,1,0:T(8,128)} custom-call(f32[4,1,2,16,16,256]{5,4,3,2,1,0:T(8,128)} %bitcast.9), custom_call_target="tpu_custom_call" | custom-call | tf_op jit(solution)/shard_map/pallas_call | solution.py:403
  2.5 0.0 copy-start.6
  2.5 7.8 %all-to-all-start = ((f32[16,4,2,16,256]{4,3,2,1,0:T(8,128)}), f32[16,4,2,16,256]{4,3,2,1,0:T(8,128)S(1)}, u32[]{:S(2)}, u32[]{:S(2)}) async-start(f32[16,4,2,16,256]{4,3,2,1,0:T(8,128)} %shard_map.55), calls=%async_computation | async-start | bytes 4194304 | tf_op jit(solution)/shard_map/all_to_all | solution.py:344
  10.2 0.0 copy-done.6
  10.2 0.8 slice_bitcast_fusion
  11.1 1.3 collective-permute-start.1
  12.4 1.0 slice_bitcast_fusion.1
  13.3 1.3 collective-permute-start
  14.6 0.1 pad_add_fusion.place
  14.7 2.2 %collective-permute-done.refs_4_ = f32[256,256]{1,0:T(8,128)S(1)} collective-permute-done((f32[256,256]{1,0:T(8,128)S(1)}, f32[256,256]{1,0:T(8,128)S(1)}, u32[]{:S(2)}, u32[]{:S(2)}) %collective-permute-start) | collective-permute-done | bytes 262176 | tf_op jit(solution)/shard_map/ppermute | solution.py:352
  16.9 0.0 copy-start.13
  16.9 0.7 copy-done.13
  17.6 0.0 collective-permute-done.1.refs_5_
  17.6 0.0 copy-start.11
  17.6 0.8 copy-done.11
  18.4 0.0 copy-start.7
  18.4 1.2 copy-done.7
  19.6 0.0 copy-start.8
  19.6 1.0 copy-done.8
  20.7 0.0 copy-start.9
  20.7 1.2 copy-done.9
  21.9 0.0 copy-start.10
  21.9 1.0 copy-done.10
  22.9 0.0 copy-start.12
  22.9 1.0 copy-done.12
  24.0 0.0 copy-start.14
  24.0 0.9 copy-done.14
  24.9 1.5 shard_map.56
  26.4 0.0 copy-start
  26.5 1.1 copy-done
  27.5 0.0 copy-start.2
  27.5 0.8 copy-done.2
  28.4 0.0 copy-start.4
  28.4 0.8 copy-done.4
  29.2 18.1 %all-to-all-done.entries = f32[16,4,2,16,256]{4,3,2,1,0:T(8,128)S(1)} async-done(((f32[16,4,2,16,256]{4,3,2,1,0:T(8,128)}), f32[16,4,2,16,256]{4,3,2,1,0:T(8,128)S(1)}, u32[]{:S(2)}, u32[]{:S(2)}) %all-to-all-start) | async-done | bytes 2097184 | tf_op jit(solution)/shard_map/all_to_all | solution.py:344
  47.3 0.6 shard_map.57
  47.9 0.0 copy-start.3
  47.9 0.0 copy-start.5
  47.9 34.2 %all_to_all.20.here = f32[16,2,2,16,256]{4,3,2,1,0:T(8,128)S(1)} all-to-all(f32[16,2,2,16,256]{4,3,2,1,0:T(8,128)S(1)} %get-tuple-element.22), channel_id=1, replica_groups={{18,20,22,24,26,28,30,0,2,4,6,8,10,12,14,16},{19,21,23,25,27,29,31,1,3,..., dimensions={0} | all-to-all | bytes 2097152 | tf_op jit(solution)/shard_map/all_to_all | solution.py:344
  82.1 0.1 slice_select_fusion.1
  82.2 3.6 %collective-permute-start.2 = (f32[16,2,1,16,256]{4,3,2,1,0:T(8,128)S(1)}, f32[16,2,1,16,256]{4,3,2,1,0:T(8,128)S(1)}, u32[]{:S(2)}, u32[]{:S(2)}) collective-permute-start(f32[16,2,1,16,256]{4,3,2,1,0:T(8,128)S(1)} %slice_select_fusion.1), channel_id=1, source_target_pairs={{0,1},{1,0},{2,3},{3,2},{4,5},{5,4},{6,7},{7,6},{8,9},{9,8},{10,11... | collective-permute-start | bytes 1572872 | tf_op jit(solution)/shard_map/ppermute | solution.py:356
  85.8 0.0 copy-done.3
  85.9 0.0 copy-done.5
  85.9 2.0 %shard_map.58.before = f32[16,2,2,16,256]{4,3,2,1,0:T(8,128)S(1)} custom-call(f32[16,2,2,16,256]{4,3,2,1,0:T(8,128)S(1)} %all_to_all.20.here, bf16[5,256,256]{2,1,0:T(8,128)(2,1)S(1)} %copy-done.3, bf16[5,256,256]{2,1,0:T(8,128)(2,1)S(1)} %copy-done.5), custom_call_target="tpu_custom_call" | custom-call | tf_op jit(solution)/shard_map/pallas_call | solution.py:319
  87.9 0.0 collective-permute-done.2.refs_0_
  87.9 1.3 shard_map.59
  89.2 27.3 %all_to_all.21.screened_hat = f32[16,2,2,16,256]{4,3,2,1,0:T(8,128)S(1)} all-to-all(f32[16,2,2,16,256]{4,3,2,1,0:T(8,128)S(1)} %shard_map.59), channel_id=1, replica_groups={{18,20,22,24,26,28,30,0,2,4,6,8,10,12,14,16},{19,21,23,25,27,29,31,1,3,..., dimensions={0} | all-to-all | bytes 2097152 | tf_op jit(solution)/shard_map/all_to_all | solution.py:344
  116.5 0.5 shard_map.60
  117.0 0.0 copy-start.1
  117.0 28.1 %all_to_all.22.here = f32[16,2,2,16,256]{4,3,2,1,0:T(8,128)S(1)} all-to-all(f32[16,2,2,16,256]{4,3,2,1,0:T(8,128)S(1)} %shard_map.60), channel_id=1, replica_groups={{18,20,22,24,26,28,30,0,2,4,6,8,10,12,14,16},{19,21,23,25,27,29,31,1,3,..., dimensions={0} | all-to-all | bytes 2097152 | tf_op jit(solution)/shard_map/all_to_all | solution.py:344
  145.2 0.1 slice_select_fusion
  145.3 3.0 %collective-permute-start.3 = (f32[16,2,1,16,256]{4,3,2,1,0:T(8,128)S(1)}, f32[16,2,1,16,256]{4,3,2,1,0:T(8,128)S(1)}, u32[]{:S(2)}, u32[]{:S(2)}) collective-permute-start(f32[16,2,1,16,256]{4,3,2,1,0:T(8,128)S(1)} %slice_select_fusion), channel_id=1, source_target_pairs={{0,1},{1,0},{2,3},{3,2},{4,5},{5,4},{6,7},{7,6},{8,9},{9,8},{10,11... | collective-permute-start | bytes 1572872 | tf_op jit(solution)/shard_map/ppermute | solution.py:356
  148.3 0.0 copy-done.1
  148.3 3.1 %shard_map.61.before = f32[2,1,2,256,256]{4,3,2,1,0:T(8,128)S(1)} custom-call(f32[16,2,2,16,256]{4,3,2,1,0:T(8,128)S(1)} %all_to_all.22.here, bf16[2,5,256,256]{3,2,1,0:T(8,128)(2,1)S(1)} %get-tuple-element.25.high.refs_1_, bf16[2,5,256,256]{3,2,1,0:T(8,128)(2,1)S(1)} %copy-done.1), custom_call_target="tpu_custom_call" | custom-call | tf_op jit(solution)/shard_map/pallas_call | solution.py:319
  151.4 0.0 collective-permute-done.3.refs_0_
  151.4 2.3 %shard_map.62 = f32[2,1,2,256,256]{4,3,2,1,0:T(8,128)} custom-call(s32[3]{0:T(128)S(1)} %pad_add_fusion.place, f32[2,1,2,256,256]{4,3,2,1,0:T(8,128)S(1)} %shard_map.61.before, f32[16,2,1,16,256]{4,3,2,1,0:T(8,128)S(1)} %collective-permute-done.3.refs_0_, bf16[2,5,256,256]{3,2,1,0:T(8,128)(2,1)S(1)} %get-tuple-element.25.high.refs_1_, ...), custom_call_target="tpu_custom_call" | custom-call | tf_op jit(solution)/shard_map/pallas_call | solution.py:319
Async XLA Ops:
  2.5 7.8 %copy-start.6 = (f32[2,1,2,256,256]{4,3,2,1,0:T(8,128)S(1)}, f32[2,1,2,256,256]{4,3,2,1,0:T(8,128)}, u32[]{:S(2)}) copy-start(f32[2,1,2,256,256]{4,3,2,1,0:T(8,128)} %refs_3_.1) | copy-start | bytes 3145732
  2.5 44.8 %all-to-all-start = ((f32[16,4,2,16,256]{4,3,2,1,0:T(8,128)}), f32[16,4,2,16,256]{4,3,2,1,0:T(8,128)S(1)}, u32[]{:S(2)}, u32[]{:S(2)}) async-start(f32[16,4,2,16,256]{4,3,2,1,0:T(8,128)} %shard_map.55), calls=%async_computation | async-start | bytes 4194304 | tf_op jit(solution)/shard_map/all_to_all | solution.py:344
  11.1 6.5 %collective-permute-start.1 = (f32[2,256,256]{2,1,0:T(8,128)}, f32[2,256,256]{2,1,0:T(8,128)S(1)}, u32[]{:S(2)}, u32[]{:S(2)}) collective-permute-start(f32[2,256,256]{2,1,0:T(8,128)} %slice_bitcast_fusion), channel_id=1, source_target_pairs={{0,1},{2,3},{4,5},{6,7},{8,9},{10,11},{12,13},{14,15},{16,17},{18,... | collective-permute-start | bytes 1572872 | tf_op jit(solution)/shard_map/ppermute | solution.py:352
  13.3 3.6 %collective-permute-start = (f32[256,256]{1,0:T(8,128)S(1)}, f32[256,256]{1,0:T(8,128)S(1)}, u32[]{:S(2)}, u32[]{:S(2)}) collective-permute-start(f32[256,256]{1,0:T(8,128)S(1)} %slice_bitcast_fusion.1), channel_id=1, source_target_pairs={{0,1},{2,3},{4,5},{6,7},{8,9},{10,11},{12,13},{14,15},{16,17},{18,... | collective-permute-start | bytes 786440 | tf_op jit(solution)/shard_map/ppermute | solution.py:352
  16.9 0.7 copy-start.13
  17.6 0.8 copy-start.11
  18.4 1.2 copy-start.7
  19.6 1.0 copy-start.8
  20.7 1.2 copy-start.9
  21.9 1.0 copy-start.10
  22.9 1.0 copy-start.12
  24.0 0.9 copy-start.14
  26.4 1.1 copy-start
  27.5 0.8 copy-start.2
  28.4 0.8 copy-start.4
  47.9 37.9 %copy-start.3 = (bf16[5,256,256]{2,1,0:T(8,128)(2,1)S(1)}, bf16[5,256,256]{2,1,0:T(8,128)(2,1)}, u32[]{:S(2)}) copy-start(bf16[5,256,256]{2,1,0:T(8,128)(2,1)} %copy-done.2) | copy-start | bytes 1966084
  47.9 37.9 %copy-start.5 = (bf16[5,256,256]{2,1,0:T(8,128)(2,1)S(1)}, bf16[5,256,256]{2,1,0:T(8,128)(2,1)}, u32[]{:S(2)}) copy-start(bf16[5,256,256]{2,1,0:T(8,128)(2,1)} %copy-done.4) | copy-start | bytes 1966084
  82.2 5.6 %collective-permute-start.2 = (f32[16,2,1,16,256]{4,3,2,1,0:T(8,128)S(1)}, f32[16,2,1,16,256]{4,3,2,1,0:T(8,128)S(1)}, u32[]{:S(2)}, u32[]{:S(2)}) collective-permute-start(f32[16,2,1,16,256]{4,3,2,1,0:T(8,128)S(1)} %slice_select_fusion.1), channel_id=1, source_target_pairs={{0,1},{1,0},{2,3},{3,2},{4,5},{5,4},{6,7},{7,6},{8,9},{9,8},{10,11... | collective-permute-start | bytes 1572872 | tf_op jit(solution)/shard_map/ppermute | solution.py:356
  117.0 31.2 %copy-start.1 = (bf16[2,5,256,256]{3,2,1,0:T(8,128)(2,1)S(1)}, bf16[2,5,256,256]{3,2,1,0:T(8,128)(2,1)}, u32[]{:S(2)}) copy-start(bf16[2,5,256,256]{3,2,1,0:T(8,128)(2,1)} %copy-done) | copy-start | bytes 3932164
  145.3 6.1 %collective-permute-start.3 = (f32[16,2,1,16,256]{4,3,2,1,0:T(8,128)S(1)}, f32[16,2,1,16,256]{4,3,2,1,0:T(8,128)S(1)}, u32[]{:S(2)}, u32[]{:S(2)}) collective-permute-start(f32[16,2,1,16,256]{4,3,2,1,0:T(8,128)S(1)} %slice_select_fusion), channel_id=1, source_target_pairs={{0,1},{1,0},{2,3},{3,2},{4,5},{5,4},{6,7},{7,6},{8,9},{9,8},{10,11... | collective-permute-start | bytes 1572872 | tf_op jit(solution)/shard_map/ppermute | solution.py:356
